TPU v7x, 32 devices: a whole 2x2x4 slice. The times are simulated.
32 devices in a mesh: pitch: 2 (over y), span: 4 (over z), axial: 4 (over x, core).
Axes of the slice: x: 2, y: 2, z: 4, core: 2. Of those that a mesh axis runs over, the one named last changes fastest.
Arguments:
- guess: float32 [2, 6, 16, 64, 512], P(None, None, 'pitch', 'span', 'axial'), may hold values from -6 to 6
- right_side: float32 [2, 6, 16, 64, 512], P(None, None, 'pitch', 'span', 'axial'), may hold values from -60 to 60
- diag_block: bfloat16 [6, 6, 16, 64, 512], P(None, None, 'pitch', 'span', 'axial'), may hold values from -4 to 4
- neighbour_blocks: bfloat16 [6, 6, 6, 16, 64, 512], P(None, None, None, 'pitch', 'span', 'axial'), may hold values from -0.6484375 to 0.6484375
- dissipation: float32 [3, 16, 64, 512], P(None, 'pitch', 'span', 'axial'), may hold values from 0.03 to 0.25
- omega_volume: float32 [16, 64, 512], P('pitch', 'span', 'axial'), may hold values from 0.2 to 2
- pseudo_step: float32 [16, 64, 512], P('pitch', 'span', 'axial'), may hold values from 0.03 to 0.3
- phase: float32 [1], replicated, may hold values from -3.140625 to 3.140625
Outputs:
- solution_field: float32 [2, 6, 16, 64, 512], P(None, None, 'pitch', 'span', 'axial')
- norms: float32 [2], replicated
All inputs are finite; a program needn't handle non-finite values.
Results may differ from a plain program's by a relative error of at most 0.0003.
Values sent between devices are 32-bit elements; how exact they have to be, the bound alone decides.
No kernel may reach another device: no remote copies, remote signals or barrier semaphores. Data moves between devices by JAX's collectives and lax.ppermute only.
A program may use at most 128 MiB of HBM per device.

v0:
```python
import jax
import jax.numpy as jnp
from jax import lax
from jax.sharding import PartitionSpec as P

ITERS = 2


def extended_2(cells, sides, width):
    for axis, dim in sides:
        count = lax.axis_size(axis)
        head = lax.slice_in_dim(cells, 0, width, axis=dim)
        tail = lax.slice_in_dim(cells, cells.shape[dim] - width, cells.shape[dim], axis=dim)
        cells = jnp.concatenate(
            [
                lax.ppermute(tail, axis, [(i, (i + 1) % count) for i in range(count)]),
                cells,
                lax.ppermute(head, axis, [((i + 1) % count, i) for i in range(count)]),
            ],
            axis=dim,
        )
    return cells


def block_apply(blocks, vector_in):
    summed = None
    for column in range(blocks.shape[1]):
        product = blocks[:, column].astype(jnp.float32)[None] * vector_in[:, column][:, None]
        summed = product if summed is None else summed + product
    return summed


def rotate(values, cosine, sine_part):
    real_part = values[0]
    imag_part = values[1]
    return jnp.stack(
        [cosine * real_part - sine_part * imag_part, sine_part * real_part + cosine * imag_part]
    )


def operate(
    current, pitch_ext, span_ext, axial_ext, diag_block, neighbour_blocks, dissipation, omega_volume
):
    summed = block_apply(diag_block, current)
    summed = (
        summed
        + block_apply(neighbour_blocks[0], pitch_ext[:, :, 1:-3])
        + block_apply(neighbour_blocks[1], pitch_ext[:, :, 3:-1])
    )
    summed = (
        summed
        + block_apply(neighbour_blocks[2], span_ext[:, :, :, 1:-3])
        + block_apply(neighbour_blocks[3], span_ext[:, :, :, 3:-1])
    )
    summed = (
        summed
        + block_apply(neighbour_blocks[4], axial_ext[:, :, :, :, 1:-3])
        + block_apply(neighbour_blocks[5], axial_ext[:, :, :, :, 3:-1])
    )
    summed = summed + dissipation[0] * (pitch_ext[:, :, :-4] + pitch_ext[:, :, 4:])
    summed = summed + dissipation[1] * (span_ext[:, :, :, :-4] + span_ext[:, :, :, 4:])
    summed = summed + dissipation[2] * (axial_ext[:, :, :, :, :-4] + axial_ext[:, :, :, :, 4:])
    rotation_term = jnp.stack([-omega_volume * current[1], omega_volume * current[0]])
    return summed + rotation_term


def extended(current):
    padded = extended_2(current, (("pitch", 2), ("span", 3), ("axial", 4)), 2)
    pitch_ext = padded[:, :, :, 2:-2, 2:-2]
    span_ext = padded[:, :, 2:-2, :, 2:-2]
    axial_ext = padded[:, :, 2:-2, 2:-2, :]
    first_span = lax.axis_index("span") == 0
    last_span = lax.axis_index("span") == lax.axis_size("span") - 1
    span_ext = jnp.concatenate(
        [
            jnp.where(first_span, 0.0, span_ext[:, :, :, :2]),
            span_ext[:, :, :, 2:-2],
            jnp.where(last_span, 0.0, span_ext[:, :, :, -2:]),
        ],
        axis=3,
    )
    first_axial = lax.axis_index("axial") == 0
    last_axial = lax.axis_index("axial") == lax.axis_size("axial") - 1
    axial_ext = jnp.concatenate(
        [
            jnp.where(first_axial, 0.0, axial_ext[:, :, :, :, :2]),
            axial_ext[:, :, :, :, 2:-2],
            jnp.where(last_axial, 0.0, axial_ext[:, :, :, :, -2:]),
        ],
        axis=4,
    )
    return (pitch_ext, span_ext, axial_ext)


def body(
    guess, right_side, diag_block, neighbour_blocks, dissipation, omega_volume, pseudo_step, phase
):
    cosine = jnp.cos(phase[0])
    sine_part = jnp.sin(phase[0])
    first_pitch = lax.axis_index("pitch") == 0
    last_pitch = lax.axis_index("pitch") == lax.axis_size("pitch") - 1
    current = guess
    global_sums = []
    for iteration in range(ITERS):
        pitch_ext, span_ext, axial_ext = extended(current)
        lower_rim = jnp.where(
            first_pitch, rotate(pitch_ext[:, :, :2], cosine, -sine_part), pitch_ext[:, :, :2]
        )
        upper_rim = jnp.where(
            last_pitch, rotate(pitch_ext[:, :, -2:], cosine, sine_part), pitch_ext[:, :, -2:]
        )
        pitch_ext = jnp.concatenate([lower_rim, pitch_ext[:, :, 2:-2], upper_rim], axis=2)
        residual = right_side - operate(
            current,
            pitch_ext,
            span_ext,
            axial_ext,
            diag_block,
            neighbour_blocks,
            dissipation,
            omega_volume,
        )
        local_square = jnp.sum(residual * residual)
        global_sums.append(lax.psum(local_square, ("pitch", "span", "axial")))
        current = current + pseudo_step[None, None] * residual
    totals = jnp.stack(global_sums)
    cell_count = float(
        guess.size * lax.axis_size("pitch") * lax.axis_size("span") * lax.axis_size("axial")
    )
    norms = jnp.sqrt(totals / cell_count)
    return (current, norms)


def solution(mesh):
    placed = (
        P(None, None, "pitch", "span", "axial"),
        P(None, None, "pitch", "span", "axial"),
        P(None, None, "pitch", "span", "axial"),
        P(None, None, None, "pitch", "span", "axial"),
        P(None, "pitch", "span", "axial"),
        P("pitch", "span", "axial"),
        P("pitch", "span", "axial"),
        P(),
    )
    return jax.shard_map(
        body,
        mesh=mesh,
        in_specs=placed,
        out_specs=(P(None, None, "pitch", "span", "axial"), P()),
        check_vma=False,
    )
```

profile of v0, /device:TPU:0, one launch (start us, length us, event | category | flops | bytes accessed | tf_op | source)
XLA Modules:
  0.0 169.5 jit_solution(514614223801403710)
XLA Ops:
  0.6 1.9 %fusion.63 = (f32[2,6,2,16,128]{4,3,2,1,0:T(8,128)}, f32[2,6,2,16,128]{4,3,2,1,0:T(8,128)}) fusion(f32[2,6,8,16,128]{4,3,2,1,0:T(8,128)} %param.8), kind=kLoop, calls=%fused_computation.247 | loop fusion | bytes 786432 | tf_op jit(solution)/shard_map/slice | solution.py:13
  2.5 3.0 %collective-permute-start = (f32[2,6,2,16,128]{4,3,2,1,0:T(8,128)}, f32[2,6,2,16,128]{4,3,2,1,0:T(8,128)S(1)}, u32[]{:S(2)}, u32[]{:S(2)}) collective-permute-start(f32[2,6,2,16,128]{4,3,2,1,0:T(8,128)} %get-tuple-element.154), channel_id=1, source_target_pairs={{0,16},{16,0},{1,17},{17,1},{2,18},{18,2},{3,19},{19,3},{4,20},{20... | collective-permute-start | bytes 589832 | tf_op jit(solution)/shard_map/ppermute | solution.py:16
  8.7 5.1 %slice_bitcast_fusion.5 = (bf16[6,6,8,16,128]{4,3,2,1,0:T(8,128)(2,1)S(1)}, bf16[6,6,8,16,128]{4,3,2,1,0:T(8,128)(2,1)S(1)}, bf16[6,6,8,16,128]{4,3,2,1,0:T(8,12...) fusion(bf16[6,6,6,8,16,128]{5,4,3,2,1,0:T(8,128)(2,1)} %param.11), kind=kLoop, calls=%fused_computation.7 | loop fusion | bytes 14155776 | tf_op jit(solution)/shard_map/squeeze | solution.py:47
  26.5 2.1 %collective-permute-start.2 = (f32[2,6,12,2,128]{4,2,3,1,0:T(8,128)S(1)}, f32[2,6,12,2,128]{4,2,3,1,0:T(8,128)S(1)}, u32[]{:S(2)}, u32[]{:S(2)}) collective-permute-start(f32[2,6,12,2,128]{4,2,3,1,0:T(8,128)S(1)} %get-tuple-element.94), channel_id=1, source_target_pairs={{0,4},{4,8},{8,12},{12,0},{1,5},{5,9},{9,13},{13,1},{2,6},{6,10},{... | collective-permute-start | bytes 442376 | tf_op jit(solution)/shard_map/ppermute | solution.py:16
  28.6 2.1 %collective-permute-start.3 = (f32[2,6,12,2,128]{4,2,3,1,0:T(8,128)S(1)}, f32[2,6,12,2,128]{4,2,3,1,0:T(8,128)S(1)}, u32[]{:S(2)}, u32[]{:S(2)}) collective-permute-start(f32[2,6,12,2,128]{4,2,3,1,0:T(8,128)S(1)} %get-tuple-element.95), channel_id=1, source_target_pairs={{4,0},{8,4},{12,8},{0,12},{5,1},{9,5},{13,9},{1,13},{6,2},{10,6},{... | collective-permute-start | bytes 442376 | tf_op jit(solution)/shard_map/ppermute | solution.py:18
  32.7 3.7 %collective-permute-done.2 = f32[2,6,12,2,128]{4,2,3,1,0:T(8,128)S(1)} collective-permute-done((f32[2,6,12,2,128]{4,2,3,1,0:T(8,128)S(1)}, f32[2,6,12,2,128]{4,2,3,1,0:T(8,128)S(1)}, u32[]{:S(2)}, u32[]{:S(2)}) %collective-permute-start.2) | collective-permute-done | bytes 147488 | tf_op jit(solution)/shard_map/ppermute | solution.py:16
  36.4 2.1 %collective-permute-done.3 = f32[2,6,12,2,128]{4,2,3,1,0:T(8,128)S(1)} collective-permute-done((f32[2,6,12,2,128]{4,2,3,1,0:T(8,128)S(1)}, f32[2,6,12,2,128]{4,2,3,1,0:T(8,128)S(1)}, u32[]{:S(2)}, u32[]{:S(2)}) %collective-permute-start.3) | collective-permute-done | bytes 147488 | tf_op jit(solution)/shard_map/ppermute | solution.py:18
  39.6 1.9 %fusion.60 = (f32[2,6,12,20,2]{4,2,3,1,0:T(8,128)S(1)}, f32[2,6,12,20,2]{4,2,3,1,0:T(8,128)}) fusion(f32[2,6,12,20,128]{4,2,3,1,0:T(8,128)S(1)} %pad_maximum_fusion), kind=kLoop, calls=%fused_computation.244 | loop fusion | bytes 92160 | tf_op jit(solution)/shard_map/slice | solution.py:13
  41.5 3.5 %copy.102 = f32[2,6,12,20,2]{3,2,4,1,0:T(8,128)} copy(f32[2,6,12,20,2]{4,2,3,1,0:T(8,128)} %get-tuple-element.17) | data formatting | bytes 46080 | tf_op jit(solution)/shard_map/slice | solution.py:12
  45.5 1.9 %copy.100 = f32[2,6,12,20,2]{3,2,4,1,0:T(8,128)} copy(f32[2,6,12,20,2]{4,2,3,1,0:T(8,128)S(1)} %get-tuple-element.16) | data formatting | bytes 46080 | tf_op jit(solution)/shard_map/slice | solution.py:13
  48.2 2.3 %slice_bitcast_fusion.53 = (f32[2,8,16,128]{3,2,1,0:T(8,128)}, f32[2,8,16,128]{3,2,1,0:T(8,128)}, f32[2,8,16,128]{3,2,1,0:T(8,128)}, f32[2,8,16,128]{3,2,1,0:T(8...) fusion(f32[2,6,8,18,128]{4,3,2,1,0:T(8,128)} %copy_dynamic-update-slice_fusion), kind=kLoop, calls=%fused_computation.196 | loop fusion | bytes 1572864 | tf_op jit(solution)/shard_map/mul | solution.py:28
  56.9 12.2 %multiply_reduce_fusion.1 = (f32[]{:T(128)}, f32[2,6,8,16,128]{4,3,2,1,0:T(8,128)S(1)}) fusion(f32[2,6,8,16,128]{4,3,2,1,0:T(8,128)} %param.9, f32[1,6,8,16,128]{4,3,2,1,0:T(8,128)} %get-tuple-element.157, f32[1,6,8,16,128]{4,3,2,1,0:T(8,128)} %get-tuple-element.156, f32[2,6,8,16,2]{4,3,2,1,0:T(8,128)S(1)} %copy.103, f32[2,6,8,16,128]{4,3,2,1,0:T(8,128)S(1)} %copy-done, ...), kind=kLoop, calls=%fused_computation.42 | loop fusion | flops 20054016 | bytes 26664964 | tf_op jit(solution)/shard_map/reduce_sum | solution.py:123
  72.3 4.7 %collective-permute-done.6 = f32[2,6,2,16,128]{4,3,2,1,0:T(8,128)S(1)} collective-permute-done((f32[2,6,2,16,128]{4,3,2,1,0:T(8,128)S(1)}, f32[2,6,2,16,128]{4,3,2,1,0:T(8,128)S(1)}, u32[]{:S(2)}, u32[]{:S(2)}) %collective-permute-start.6) | collective-permute-done | bytes 196640 | tf_op jit(solution)/shard_map/ppermute | solution.py:16
  77.0 4.2 %collective-permute-done.7 = f32[2,6,2,16,128]{4,3,2,1,0:T(8,128)S(1)} collective-permute-done((f32[2,6,2,16,128]{4,3,2,1,0:T(8,128)S(1)}, f32[2,6,2,16,128]{4,3,2,1,0:T(8,128)S(1)}, u32[]{:S(2)}, u32[]{:S(2)}) %collective-permute-start.7) | collective-permute-done | bytes 196640 | tf_op jit(solution)/shard_map/ppermute | solution.py:18
  84.0 2.3 %collective-permute-start.9 = (f32[2,6,12,2,128]{4,2,3,1,0:T(8,128)S(1)}, f32[2,6,12,2,128]{4,2,3,1,0:T(8,128)S(1)}, u32[]{:S(2)}, u32[]{:S(2)}) collective-permute-start(f32[2,6,12,2,128]{4,2,3,1,0:T(8,128)S(1)} %copy.106), channel_id=1, source_target_pairs={{4,0},{8,4},{12,8},{0,12},{5,1},{9,5},{13,9},{1,13},{6,2},{10,6},{... | collective-permute-start | bytes 442376 | tf_op jit(solution)/shard_map/ppermute | solution.py:18
  87.4 4.7 %collective-permute-done.8 = f32[2,6,12,2,128]{4,2,3,1,0:T(8,128)S(1)} collective-permute-done((f32[2,6,12,2,128]{4,2,3,1,0:T(8,128)S(1)}, f32[2,6,12,2,128]{4,2,3,1,0:T(8,128)S(1)}, u32[]{:S(2)}, u32[]{:S(2)}) %collective-permute-start.8) | collective-permute-done | bytes 147488 | tf_op jit(solution)/shard_map/ppermute | solution.py:16
  95.2 2.4 %fusion.61 = (f32[2,6,12,20,2]{4,3,2,1,0:T(8,128)}, f32[2,6,12,20,2]{4,3,2,1,0:T(8,128)}) fusion(f32[2,6,12,20,128]{4,3,2,1,0:T(8,128)S(1)} %pad_maximum_fusion.1), kind=kLoop, calls=%fused_computation.245 | loop fusion | bytes 92160 | tf_op jit(solution)/shard_map/slice | solution.py:13
  97.6 2.7 %copy.110 = f32[2,6,12,20,2]{3,2,4,1,0:T(8,128)S(1)} copy(f32[2,6,12,20,2]{4,3,2,1,0:T(8,128)} %get-tuple-element.18) | data formatting | bytes 46080 | tf_op jit(solution)/shard_map/slice | solution.py:13
  101.2 3.4 %copy.112 = f32[2,6,12,20,2]{3,2,4,1,0:T(8,128)} copy(f32[2,6,12,20,2]{4,3,2,1,0:T(8,128)} %get-tuple-element.19) | data formatting | bytes 46080 | tf_op jit(solution)/shard_map/slice | solution.py:12
  104.6 1.7 %collective-permute-start.11 = (f32[2,6,12,20,2]{3,2,4,1,0:T(8,128)}, f32[2,6,12,20,2]{3,2,4,1,0:T(8,128)}, u32[]{:S(2)}, u32[]{:S(2)}) collective-permute-start(f32[2,6,12,20,2]{3,2,4,1,0:T(8,128)} %copy.112), channel_id=1, source_target_pairs={{1,0},{2,1},{3,2},{0,3},{5,4},{6,5},{7,6},{4,7},{9,8},{10,9},{11,1... | collective-permute-start | bytes 69128 | tf_op jit(solution)/shard_map/ppermute | solution.py:18
  110.2 1.7 slice_select_fusion
  115.0 12.2 %multiply_reduce_fusion = (f32[]{:T(128)}, f32[2,6,8,16,128]{4,3,2,1,0:T(8,128)S(1)}) fusion(f32[2,6,8,16,128]{4,3,2,1,0:T(8,128)} %param.9, f32[1,6,8,16,128]{4,3,2,1,0:T(8,128)} %get-tuple-element.147, f32[1,6,8,16,128]{4,3,2,1,0:T(8,128)} %get-tuple-element.146, f32[2,6,8,16,2]{4,3,2,1,0:T(8,128)S(1)} %copy.113, ...), kind=kLoop, calls=%fused_computation.41 | loop fusion | flops 20250624 | bytes 25976836 | tf_op jit(solution)/shard_map/reduce_sum | solution.py:123
  128.2 39.3 %all-reduce = (f32[1]{0:T(128)}, f32[1]{0:T(128)}) all-reduce(f32[1]{0:T(128)} %bitcast.138, f32[1]{0:T(128)} %bitcast.137), channel_id=1, replica_groups=mesh['pitch'=2,'span'=4,'axial'=4] {'pitch','span','axial'}, use_global_device_ids=true, to_apply=%region_3.4 | all-reduce | flops 2 | bytes 16 | tf_op jit(solution)/shard_map/psum | solution.py:124
  167.6 1.9 %fusion.57 = f32[2]{0:T(128)} fusion(f32[1]{0:T(128)} %get-tuple-element.4, f32[1]{0:T(128)} %get-tuple-element.5), kind=kLoop, calls=%fused_computation.243 | loop fusion | flops 4 | bytes 16 | tf_op jit(solution)/shard_map/sqrt | solution.py:130
  (153 shorter events, 44.5 us)
Async XLA Ops:
  0.6 7.1 %copy-start = (f32[2,6,8,16,128]{4,3,2,1,0:T(8,128)S(1)}, f32[2,6,8,16,128]{4,3,2,1,0:T(8,128)}, u32[]{:S(2)}) copy-start(f32[2,6,8,16,128]{4,3,2,1,0:T(8,128)} %param.8) | copy-start | bytes 2359300
  2.5 23.6 %collective-permute-start = (f32[2,6,2,16,128]{4,3,2,1,0:T(8,128)}, f32[2,6,2,16,128]{4,3,2,1,0:T(8,128)S(1)}, u32[]{:S(2)}, u32[]{:S(2)}) collective-permute-start(f32[2,6,2,16,128]{4,3,2,1,0:T(8,128)} %get-tuple-element.154), channel_id=1, source_target_pairs={{0,16},{16,0},{1,17},{17,1},{2,18},{18,2},{3,19},{19,3},{4,20},{20... | collective-permute-start | bytes 589832 | tf_op jit(solution)/shard_map/ppermute | solution.py:16
  5.5 20.8 %collective-permute-start.1 = (f32[2,6,2,16,128]{4,3,2,1,0:T(8,128)}, f32[2,6,2,16,128]{4,3,2,1,0:T(8,128)S(1)}, u32[]{:S(2)}, u32[]{:S(2)}) collective-permute-start(f32[2,6,2,16,128]{4,3,2,1,0:T(8,128)} %get-tuple-element.155), channel_id=1, source_target_pairs={{16,0},{0,16},{17,1},{1,17},{18,2},{2,18},{19,3},{3,19},{20,4},{4,... | collective-permute-start | bytes 589832 | tf_op jit(solution)/shard_map/ppermute | solution.py:18
  26.5 10.0 %collective-permute-start.2 = (f32[2,6,12,2,128]{4,2,3,1,0:T(8,128)S(1)}, f32[2,6,12,2,128]{4,2,3,1,0:T(8,128)S(1)}, u32[]{:S(2)}, u32[]{:S(2)}) collective-permute-start(f32[2,6,12,2,128]{4,2,3,1,0:T(8,128)S(1)} %get-tuple-element.94), channel_id=1, source_target_pairs={{0,4},{4,8},{8,12},{12,0},{1,5},{5,9},{9,13},{13,1},{2,6},{6,10},{... | collective-permute-start | bytes 442376 | tf_op jit(solution)/shard_map/ppermute | solution.py:16
  28.6 10.0 %collective-permute-start.3 = (f32[2,6,12,2,128]{4,2,3,1,0:T(8,128)S(1)}, f32[2,6,12,2,128]{4,2,3,1,0:T(8,128)S(1)}, u32[]{:S(2)}, u32[]{:S(2)}) collective-permute-start(f32[2,6,12,2,128]{4,2,3,1,0:T(8,128)S(1)} %get-tuple-element.95), channel_id=1, source_target_pairs={{4,0},{8,4},{12,8},{0,12},{5,1},{9,5},{13,9},{1,13},{6,2},{10,6},{... | collective-permute-start | bytes 442376 | tf_op jit(solution)/shard_map/ppermute | solution.py:18
  36.4 2.1 %copy-start.33 = (f32[2,6,12,2,128]{4,2,3,1,0:T(8,128)}, f32[2,6,12,2,128]{4,2,3,1,0:T(8,128)S(1)}, u32[]{:S(2)}) copy-start(f32[2,6,12,2,128]{4,2,3,1,0:T(8,128)S(1)} %collective-permute-done.2) | copy-start | bytes 442372
  41.5 5.9 %copy-start.36 = (f32[2,6,12,2,128]{4,2,3,1,0:T(8,128)S(1)}, f32[2,6,12,2,128]{4,2,3,1,0:T(8,128)}, u32[]{:S(2)}) copy-start(f32[2,6,12,2,128]{4,2,3,1,0:T(8,128)} %copy-done.35) | copy-start | bytes 442372
  45.0 6.4 %collective-permute-start.5 = (f32[2,6,12,20,2]{3,2,4,1,0:T(8,128)}, f32[2,6,12,20,2]{3,2,4,1,0:T(8,128)}, u32[]{:S(2)}, u32[]{:S(2)}) collective-permute-start(f32[2,6,12,20,2]{3,2,4,1,0:T(8,128)} %copy.102), channel_id=1, source_target_pairs={{1,0},{2,1},{3,2},{0,3},{5,4},{6,5},{7,6},{4,7},{9,8},{10,9},{11,1... | collective-permute-start | bytes 69128 | tf_op jit(solution)/shard_map/ppermute | solution.py:18
  45.5 5.0 %copy-start.34 = (f32[2,6,12,2,128]{4,2,3,1,0:T(8,128)S(1)}, f32[2,6,12,2,128]{4,2,3,1,0:T(8,128)}, u32[]{:S(2)}) copy-start(f32[2,6,12,2,128]{4,2,3,1,0:T(8,128)} %copy-done.33) | copy-start | bytes 442372
  47.4 7.3 %collective-permute-start.4 = (f32[2,6,12,20,2]{3,2,4,1,0:T(8,128)}, f32[2,6,12,20,2]{3,2,4,1,0:T(8,128)S(1)}, u32[]{:S(2)}, u32[]{:S(2)}) collective-permute-start(f32[2,6,12,20,2]{3,2,4,1,0:T(8,128)} %copy.100), channel_id=1, source_target_pairs={{0,1},{1,2},{2,3},{3,0},{4,5},{5,6},{6,7},{7,4},{8,9},{9,10},{10,1... | collective-permute-start | bytes 69128 | tf_op jit(solution)/shard_map/ppermute | solution.py:16
  50.5 4.1 %copy-start.14 = (f32[2,6,8,2,128]{4,3,2,1,0:T(2,128)}, f32[2,6,8,2,128]{4,3,2,1,0:T(2,128)S(1)}, u32[]{:S(2)}) copy-start(f32[2,6,8,2,128]{4,3,2,1,0:T(2,128)S(1)} %copy.98) | copy-start | bytes 294916
  56.9 12.2 %copy-start.37 = (f32[8,16,128]{2,1,0:T(8,128)S(1)}, f32[8,16,128]{2,1,0:T(8,128)}, u32[]{:S(2)}) copy-start(f32[8,16,128]{2,1,0:T(8,128)} %param.14) | copy-start | bytes 196612
  69.1 2.2 %copy-start.18 = (f32[8,16,128]{2,1,0:T(8,128)S(1)}, f32[8,16,128]{2,1,0:T(8,128)}, u32[]{:S(2)}) copy-start(f32[8,16,128]{2,1,0:T(8,128)} %param.13) | copy-start | bytes 196612
  69.1 2.2 %copy-start.20 = (f32[8,16,128]{2,1,0:T(8,128)S(1)}, f32[8,16,128]{2,1,0:T(8,128)}, u32[]{:S(2)}) copy-start(f32[8,16,128]{2,1,0:T(8,128)} %copy-done.19) | copy-start | bytes 196612
  69.3 7.7 %collective-permute-start.6 = (f32[2,6,2,16,128]{4,3,2,1,0:T(8,128)S(1)}, f32[2,6,2,16,128]{4,3,2,1,0:T(8,128)S(1)}, u32[]{:S(2)}, u32[]{:S(2)}) collective-permute-start(f32[2,6,2,16,128]{4,3,2,1,0:T(8,128)S(1)} %get-tuple-element.144), channel_id=1, source_target_pairs={{0,16},{16,0},{1,17},{17,1},{2,18},{18,2},{3,19},{19,3},{4,20},{20... | collective-permute-start | bytes 589832 | tf_op jit(solution)/shard_map/ppermute | solution.py:16
  70.9 10.3 %collective-permute-start.7 = (f32[2,6,2,16,128]{4,3,2,1,0:T(8,128)S(1)}, f32[2,6,2,16,128]{4,3,2,1,0:T(8,128)S(1)}, u32[]{:S(2)}, u32[]{:S(2)}) collective-permute-start(f32[2,6,2,16,128]{4,3,2,1,0:T(8,128)S(1)} %get-tuple-element.145), channel_id=1, source_target_pairs={{16,0},{0,16},{17,1},{1,17},{18,2},{2,18},{19,3},{3,19},{20,4},{4,... | collective-permute-start | bytes 589832 | tf_op jit(solution)/shard_map/ppermute | solution.py:18
  82.4 9.7 %collective-permute-start.8 = (f32[2,6,12,2,128]{4,2,3,1,0:T(8,128)S(1)}, f32[2,6,12,2,128]{4,2,3,1,0:T(8,128)S(1)}, u32[]{:S(2)}, u32[]{:S(2)}) collective-permute-start(f32[2,6,12,2,128]{4,2,3,1,0:T(8,128)S(1)} %copy.104), channel_id=1, source_target_pairs={{0,4},{4,8},{8,12},{12,0},{1,5},{5,9},{9,13},{13,1},{2,6},{6,10},{... | collective-permute-start | bytes 442376 | tf_op jit(solution)/shard_map/ppermute | solution.py:16
  84.0 10.6 %collective-permute-start.9 = (f32[2,6,12,2,128]{4,2,3,1,0:T(8,128)S(1)}, f32[2,6,12,2,128]{4,2,3,1,0:T(8,128)S(1)}, u32[]{:S(2)}, u32[]{:S(2)}) collective-permute-start(f32[2,6,12,2,128]{4,2,3,1,0:T(8,128)S(1)} %copy.106), channel_id=1, source_target_pairs={{4,0},{8,4},{12,8},{0,12},{5,1},{9,5},{13,9},{1,13},{6,2},{10,6},{... | collective-permute-start | bytes 442376 | tf_op jit(solution)/shard_map/ppermute | solution.py:18
  86.4 6.7 %copy-start.8 = (f32[2,6,2,16,128]{4,3,2,1,0:T(8,128)}, f32[2,6,2,16,128]{4,3,2,1,0:T(8,128)S(1)}, u32[]{:S(2)}) copy-start(f32[2,6,2,16,128]{4,3,2,1,0:T(8,128)S(1)} %maximum_select_fusion.3) | copy-start | bytes 589828
  92.1 3.0 %copy-start.12 = (f32[2,6,8,2,128]{4,3,2,1,0:T(2,128)}, f32[2,6,8,2,128]{4,3,2,1,0:T(2,128)S(1)}, u32[]{:S(2)}) copy-start(f32[2,6,8,2,128]{4,3,2,1,0:T(2,128)S(1)} %copy.105) | copy-start | bytes 294916
  94.7 5.6 %copy-start.13 = (f32[2,6,8,2,128]{4,3,2,1,0:T(2,128)}, f32[2,6,8,2,128]{4,3,2,1,0:T(2,128)S(1)}, u32[]{:S(2)}) copy-start(f32[2,6,8,2,128]{4,3,2,1,0:T(2,128)S(1)} %copy.107) | copy-start | bytes 294916
  100.2 6.1 %collective-permute-start.10 = (f32[2,6,12,20,2]{3,2,4,1,0:T(8,128)S(1)}, f32[2,6,12,20,2]{3,2,4,1,0:T(8,128)S(1)}, u32[]{:S(2)}, u32[]{:S(2)}) collective-permute-start(f32[2,6,12,20,2]{3,2,4,1,0:T(8,128)S(1)} %copy.110), channel_id=1, source_target_pairs={{0,1},{1,2},{2,3},{3,0},{4,5},{5,6},{6,7},{7,4},{8,9},{9,10},{10,1... | collective-permute-start | bytes 69128 | tf_op jit(solution)/shard_map/ppermute | solution.py:16
  104.6 5.6 %collective-permute-start.11 = (f32[2,6,12,20,2]{3,2,4,1,0:T(8,128)}, f32[2,6,12,20,2]{3,2,4,1,0:T(8,128)}, u32[]{:S(2)}, u32[]{:S(2)}) collective-permute-start(f32[2,6,12,20,2]{3,2,4,1,0:T(8,128)} %copy.112), channel_id=1, source_target_pairs={{1,0},{2,1},{3,2},{0,3},{5,4},{6,5},{7,6},{4,7},{9,8},{10,9},{11,1... | collective-permute-start | bytes 69128 | tf_op jit(solution)/shard_map/ppermute | solution.py:18
  115.0 12.2 %copy-start.38 = (f32[8,16,128]{2,1,0:T(8,128)S(1)}, f32[8,16,128]{2,1,0:T(8,128)}, u32[]{:S(2)}) copy-start(f32[8,16,128]{2,1,0:T(8,128)} %param.14) | copy-start | bytes 196612
  (28 other events, 37.3 us)
where the time goes:
time: 170 us; the launch traced here: 169 us
  other arithmetic  54.7 us (32%)
  blocking collectives  39.3 us (23%)
  local copies, waits for them, and re-layouts  37 us (22%)
  waiting for transfers between devices  21 us (12%)
  starting transfers between devices  15.5 us (9%)
  between operations  1.96 us (1%)
    psum x1, blocking collectives, body(): global_sums.append(lax.psum(local_square, ('pitch', 'span', 'axial')))  39.3 us
    reduce_sum x2, other arithmetic, body(): local_square = jnp.sum(residual * residual)  24.4 us
    ppermute x6, waiting for transfers between devices, extended_2(): lax.ppermute(tail, axis, [(i, (i + 1) % count) for i in range(count)])  13.1 us
    slice x7, local copies, waits for them, and re-layouts, extended_2(): lax.slice_in_dim(cells, cells.shape[dim] - width, cells.shape[dim], axis=...  10.9 us
    mul x11, other arithmetic, block_apply(): blocks[:, column].astype(jnp.float32)[None] * vector_in[:, column][:, None]  10.7 us
    convert_element_type x7, other arithmetic, block_apply(): blocks[:, column].astype(jnp.float32)[None] * vector_in[:, column][:, None]  10.1 us
    ppermute x6, starting transfers between devices, extended_2(): lax.ppermute(tail, axis, [(i, (i + 1) % count) for i in range(count)])  8.35 us
    ppermute x6, waiting for transfers between devices, extended_2(): lax.ppermute(head, axis, [((i + 1) % count, i) for i in range(count)])  7.89 us
  transfers between devices with their start and end apart: 12, of which 6 were waited for; matrix products, arithmetic and copies ran while one was open for 24% of the time, Pallas kernels for 0%

commit v1 on v0

v1 whole, which is shorter than its diff:
```python
import functools

import jax
import jax.numpy as jnp
from jax import lax
from jax.experimental import pallas as pl
from jax.experimental.pallas import tpu as pltpu
from jax.sharding import PartitionSpec as P

ITERS = 2
WIDTH = 2
VMEM = pl.BlockSpec(memory_space=pltpu.VMEM)
SMEM = pl.BlockSpec(memory_space=pltpu.SMEM)
ANY = pl.BlockSpec(memory_space=pl.ANY)
VMEM_LIMIT = 40 * 1024 * 1024
PAD = 8


def resident(values):
    return pltpu.with_memory_space_constraint(values, pltpu.VMEM)


def kept(shape):
    return pltpu.VMEM(shape, jnp.float32)


def params():
    return pltpu.CompilerParams(vmem_limit_bytes=VMEM_LIMIT)


def lane_place(k, planes, lanes):
    per_group = (lanes // (2 * WIDTH)) // planes
    return k // per_group, (k % per_group) * planes


def lane_groups(rows, planes, lanes):
    return lane_place(rows - 1, planes, lanes)[0] + 1


def pitch_faces_kernel(guess_ref, faces_ref, sems):
    planes = guess_ref.shape[1]
    tail = pltpu.make_async_copy(
        guess_ref.at[:, planes - WIDTH : planes], faces_ref.at[0], sems.at[0]
    )
    head = pltpu.make_async_copy(guess_ref.at[:, 0:WIDTH], faces_ref.at[1], sems.at[1])
    tail.start()
    head.start()
    tail.wait()
    head.wait()


def pack_faces(wide_ref, low_ref, high_ref, axial_ref):
    rows, wide, span, lanes = wide_ref.shape
    planes = wide - 2 * WIDTH
    lane = lax.broadcasted_iota(jnp.int32, (span, lanes), 1)
    groups = lane_groups(rows, planes, lanes)
    packed = [None] * groups
    for k in range(rows):
        group, base = lane_place(k, planes, lanes)
        for p in range(planes):
            cells = wide_ref[k, p + WIDTH]
            low_ref[k, p] = cells[:WIDTH]
            high_ref[k, p] = cells[span - WIDTH :]
            place = base + p
            moved = pltpu.roll(cells, (2 * WIDTH * place + WIDTH) % lanes, axis=1)
            if packed[group] is None:
                packed[group] = moved
            else:
                packed[group] = jnp.where(lane >= 2 * WIDTH * place, moved, packed[group])
        if k == rows - 1 or lane_place(k + 1, planes, lanes)[0] != group:
            axial_ref[group] = packed[group]


def first_pack_kernel(guess_ref, wide_ref, low_ref, high_ref, axial_ref, sem):
    rows, wide, span, lanes = wide_ref.shape
    planes = wide - 2 * WIDTH
    copy = pltpu.make_async_copy(guess_ref, wide_ref.at[:, WIDTH : WIDTH + planes], sem)
    copy.start()
    for k in range(rows):
        for p in (0, 1, wide - 2, wide - 1):
            wide_ref[k, p] = jnp.zeros((span, lanes), jnp.float32)
    copy.wait()
    pack_faces(wide_ref, low_ref, high_ref, axial_ref)


def pack_kernel(wide_ref, low_ref, high_ref, axial_ref):
    pack_faces(wide_ref, low_ref, high_ref, axial_ref)


def main_kernel(
    wide_ref,
    low_ref,
    high_ref,
    axial_low_ref,
    axial_high_ref,
    neighbour_ref,
    diag_ref,
    right_ref,
    dissipation_ref,
    omega_ref,
    step_ref,
    next_ref,
    error_ref,
    square_ref,
    span_buf,
    axial_buf,
):
    rows, wide, span, lanes = wide_ref.shape
    planes = wide - 2 * WIDTH
    nv = rows // 2
    lane = lax.broadcasted_iota(jnp.int32, (span, lanes), 1)
    for group in range(axial_buf.shape[0]):
        axial_buf[group] = jnp.where(
            lane % (2 * WIDTH) < WIDTH, axial_low_ref[group], axial_high_ref[group]
        )
    for k in range(rows):
        for p in (0, 1, wide - 2, wide - 1):
            next_ref[k, p] = jnp.zeros((span, lanes), jnp.float32)
    square_ref[...] = jnp.zeros_like(square_ref)

    def plane(p, carry):
        for k in range(rows):
            span_buf[k, PAD - WIDTH : PAD] = low_ref[k, p]
            span_buf[k, PAD : PAD + span] = wide_ref[k, p + WIDTH]
            span_buf[k, PAD + span : PAD + span + WIDTH] = high_ref[k, p]
        total = [None] * rows

        def add(k, value):
            total[k] = value if total[k] is None else total[k] + value

        def column(blocks, j, real, imag):
            for i in range(nv):
                block = blocks(i, j).astype(jnp.float32)
                add(i, block * real)
                add(nv + i, block * imag)

        spread_pitch = dissipation_ref[0, p]
        spread_span = dissipation_ref[1, p]
        spread_axial = dissipation_ref[2, p]
        for j in range(nv):
            pair = (j, nv + j)
            column(lambda i, j: diag_ref[i, j, p], j, *[wide_ref[k, p + 2] for k in pair])
            column(lambda i, j: neighbour_ref[0, i, j, p], j, *[wide_ref[k, p + 1] for k in pair])
            column(lambda i, j: neighbour_ref[1, i, j, p], j, *[wide_ref[k, p + 3] for k in pair])
            column(
                lambda i, j: neighbour_ref[2, i, j, p],
                j,
                *[span_buf[k, PAD - 1 : PAD - 1 + span] for k in pair],
            )
            column(
                lambda i, j: neighbour_ref[3, i, j, p],
                j,
                *[span_buf[k, PAD + 1 : PAD + 1 + span] for k in pair],
            )
            lower = []
            upper = []
            for k in pair:
                cells = wide_ref[k, p + WIDTH]
                group, base = lane_place(k, planes, lanes)
                shift = lanes - WIDTH - 2 * WIDTH * base - 2 * WIDTH * p
                shift = jnp.where(shift < 0, shift + lanes, shift)
                halo = pltpu.roll(axial_buf[group], shift, axis=1)
                low_near = jnp.where(lane >= lanes - 1, halo, cells)
                high_near = jnp.where(lane < 1, halo, cells)
                low_far = jnp.where(lane >= lanes - WIDTH, halo, cells)
                high_far = jnp.where(lane < WIDTH, halo, cells)
                lower.append(pltpu.roll(low_near, 1, axis=1))
                upper.append(pltpu.roll(high_near, lanes - 1, axis=1))
                far = pltpu.roll(low_far, 2, axis=1) + pltpu.roll(high_far, lanes - 2, axis=1)
                add(k, spread_axial * far)
                add(
                    k,
                    spread_span
                    * (
                        span_buf[k, PAD - 2 : PAD - 2 + span]
                        + span_buf[k, PAD + 2 : PAD + 2 + span]
                    ),
                )
                add(k, spread_pitch * (wide_ref[k, p] + wide_ref[k, p + 4]))
            column(lambda i, j: neighbour_ref[4, i, j, p], j, *lower)
            column(lambda i, j: neighbour_ref[5, i, j, p], j, *upper)
        omega = omega_ref[p]
        step = step_ref[p]
        square = None
        for i in range(nv):
            real = wide_ref[i, p + WIDTH]
            imag = wide_ref[nv + i, p + WIDTH]
            for k, cells, turned in ((i, real, -omega * imag), (nv + i, imag, omega * real)):
                error = (total[k] + turned) - right_ref[k, p]
                error_ref[k, p] = error
                next_ref[k, p + WIDTH] = cells - step * error
                square = error * error if square is None else square + error * error
        inner = jnp.logical_and(p >= WIDTH, p < planes - WIDTH)
        square_ref[...] += jnp.where(inner, square, 0.0)
        return carry

    lax.fori_loop(0, planes, plane, 0)


def pitch_terms(halo_ref, turn_ref, neighbour_ref, dissipation_ref, error_ref, store):
    rows, planes, span, lanes = error_ref.shape
    nv = rows // 2
    for side in range(2):
        cosine = turn_ref[2 * side]
        sine_part = turn_ref[2 * side + 1]
        near_at, far_at = (1, 0) if side == 0 else (0, 1)
        edge, inside = (0, 1) if side == 0 else (planes - 1, planes - 2)

        def turned(j, at):
            real = halo_ref[side, j, at]
            imag = halo_ref[side, nv + j, at]
            return (cosine * real - sine_part * imag, sine_part * real + cosine * imag)

        total = [error_ref[k, edge] for k in range(rows)]
        spread_edge = dissipation_ref[0, edge]
        spread_inside = dissipation_ref[0, inside]
        for j in range(nv):
            near = turned(j, near_at)
            far = turned(j, far_at)
            for c in range(2):
                k = c * nv + j
                total[k] = total[k] + spread_edge * far[c]
                store(k, inside, error_ref[k, inside] + spread_inside * near[c])
            for i in range(nv):
                block = neighbour_ref[side, i, j, edge].astype(jnp.float32)
                for c in range(2):
                    total[c * nv + i] = total[c * nv + i] + block * near[c]
        for k in range(rows):
            store(k, edge, total[k])


def turn_kernel(
    halo_ref,
    turn_ref,
    neighbour_ref,
    dissipation_ref,
    step_ref,
    wide_ref,
    error_ref,
    square_in_ref,
    next_in_ref,
    next_ref,
    faces_ref,
    square_ref,
):
    planes = error_ref.shape[1]
    square_ref[...] = square_in_ref[...]

    def store(k, p, error):
        value = wide_ref[k, p + WIDTH] - step_ref[p] * error
        next_ref[k, p + WIDTH] = value
        if p < WIDTH:
            faces_ref[1, k, p] = value
        else:
            faces_ref[0, k, p - (planes - WIDTH)] = value
        square_ref[...] += error * error

    pitch_terms(halo_ref, turn_ref, neighbour_ref, dissipation_ref, error_ref, store)


def last_kernel(
    halo_ref,
    turn_ref,
    neighbour_ref,
    dissipation_ref,
    step_ref,
    wide_ref,
    error_ref,
    next_ref,
    first_square_ref,
    square_in_ref,
    out_ref,
    share_ref,
    edge_buf,
    square_buf,
    sems,
):
    planes = error_ref.shape[1]
    span, lanes = square_buf.shape
    inner = pltpu.make_async_copy(
        next_ref.at[:, 2 * WIDTH : planes], out_ref.at[:, WIDTH : planes - WIDTH], sems.at[0]
    )
    inner.start()
    square_buf[...] = square_in_ref[...]

    def store(k, p, error):
        at = p if p < WIDTH else p - (planes - 2 * WIDTH)
        edge_buf[k, at] = wide_ref[k, p + WIDTH] - step_ref[p] * error
        square_buf[...] += error * error

    pitch_terms(halo_ref, turn_ref, neighbour_ref, dissipation_ref, error_ref, store)
    low = pltpu.make_async_copy(
        edge_buf.at[:, 0:WIDTH], out_ref.at[:, 0:WIDTH], sems.at[1]
    )
    high = pltpu.make_async_copy(
        edge_buf.at[:, WIDTH : 2 * WIDTH], out_ref.at[:, planes - WIDTH : planes], sems.at[2]
    )
    low.start()
    high.start()
    first = jnp.sum(first_square_ref[...], axis=(0, 1), keepdims=True)
    second = jnp.sum(square_buf[...], axis=(0, 1), keepdims=True)
    lane = lax.broadcasted_iota(jnp.int32, share_ref.shape, 2)
    share_ref[...] = jnp.where(
        lane == 0, first.reshape(1, 1, 1), jnp.where(lane == 1, second.reshape(1, 1, 1), 0.0)
    )
    inner.wait()
    low.wait()
    high.wait()


def body(
    guess, right_side, diag_block, neighbour_blocks, dissipation, omega_volume, pseudo_step, phase
):
    parts, nv, planes, span, lanes = guess.shape
    rows = parts * nv
    pitch_count = lax.axis_size("pitch")
    span_count = lax.axis_size("span")
    axial_count = lax.axis_size("axial")
    devices = pitch_count * span_count * axial_count
    wide = (rows, planes + 2 * WIDTH, span, lanes)
    block = (rows, planes, span, lanes)
    faces_shape = (2, rows, WIDTH, span, lanes)
    edge_shape = (rows, planes, WIDTH, lanes)
    axial_shape = (lane_groups(rows, planes, lanes), span, lanes)
    guess = guess.reshape(block)
    right_side = right_side.reshape(block)

    cosine = jnp.cos(phase[0])
    sine_part = jnp.sin(phase[0])
    first_pitch = lax.axis_index("pitch") == 0
    last_pitch = lax.axis_index("pitch") == pitch_count - 1
    one = jnp.float32(1.0)
    zero = jnp.float32(0.0)
    turn = jnp.stack(
        [
            jnp.where(first_pitch, cosine, one),
            jnp.where(first_pitch, -sine_part, zero),
            jnp.where(last_pitch, cosine, one),
            jnp.where(last_pitch, sine_part, zero),
        ]
    )

    def exchange_pitch(faces):
        up = [(i, (i + 1) % pitch_count) for i in range(pitch_count)]
        down = [(j, i) for i, j in up]
        if sorted(up) == sorted(down):
            return lax.ppermute(faces, "pitch", up)
        return jnp.stack(
            [lax.ppermute(faces[0], "pitch", up), lax.ppermute(faces[1], "pitch", down)]
        )

    def exchange_rest(low, high, axial):
        up_span = [(i, i + 1) for i in range(span_count - 1)]
        down_span = [(i + 1, i) for i in range(span_count - 1)]
        up_axial = [(i, i + 1) for i in range(axial_count - 1)]
        down_axial = [(i + 1, i) for i in range(axial_count - 1)]
        return (
            lax.ppermute(high, "span", up_span),
            lax.ppermute(low, "span", down_span),
            lax.ppermute(axial, "axial", up_axial),
            lax.ppermute(axial, "axial", down_axial),
        )

    faces = pl.pallas_call(
        pitch_faces_kernel,
        out_shape=kept(faces_shape),
        in_specs=[ANY],
        out_specs=VMEM,
        scratch_shapes=[pltpu.SemaphoreType.DMA((2,))],
        compiler_params=params(),
        name="pitch_faces",
    )(guess)
    state, low, high, axial = pl.pallas_call(
        first_pack_kernel,
        out_shape=(kept(wide), kept(edge_shape), kept(edge_shape), kept(axial_shape)),
        in_specs=[ANY],
        out_specs=(VMEM,) * 4,
        scratch_shapes=[pltpu.SemaphoreType.DMA],
        compiler_params=params(),
        name="first_pack",
    )(guess)

    neighbour_blocks = resident(neighbour_blocks)
    diag_block = resident(diag_block)
    right_side = resident(right_side)
    dissipation = resident(dissipation)
    omega_volume = resident(omega_volume)
    pseudo_step = resident(pseudo_step)
    squares = []
    for iteration in range(ITERS):
        halo = resident(exchange_pitch(faces))
        around = [resident(part) for part in exchange_rest(low, high, axial)]
        following, error, square = pl.pallas_call(
            main_kernel,
            out_shape=(kept(wide), kept(block), kept((span, lanes))),
            in_specs=[VMEM] * 11,
            out_specs=(VMEM,) * 3,
            scratch_shapes=[
                pltpu.VMEM((rows, span + 2 * PAD, lanes), jnp.float32),
                pltpu.VMEM(axial_shape, jnp.float32),
            ],
            compiler_params=params(),
            name="main",
        )(
            state,
            *around,
            neighbour_blocks,
            diag_block,
            right_side,
            dissipation,
            omega_volume,
            pseudo_step,
        )
        if iteration < ITERS - 1:
            state, faces, square = pl.pallas_call(
                turn_kernel,
                out_shape=(kept(wide), kept(faces_shape), kept((span, lanes))),
                in_specs=[VMEM, SMEM] + [VMEM] * 7,
                out_specs=(VMEM,) * 3,
                input_output_aliases={8: 0},
                compiler_params=params(),
                name="pitch_terms",
            )(
                halo,
                turn,
                neighbour_blocks,
                dissipation,
                pseudo_step,
                state,
                error,
                square,
                following,
            )
            squares.append(square)
            low, high, axial = pl.pallas_call(
                pack_kernel,
                out_shape=(kept(edge_shape), kept(edge_shape), kept(axial_shape)),
                in_specs=[VMEM],
                out_specs=(VMEM,) * 3,
                compiler_params=params(),
                name="pack",
            )(state)
        else:
            out, share = pl.pallas_call(
                last_kernel,
                out_shape=(
                    jax.ShapeDtypeStruct(block, jnp.float32),
                    kept((devices, 1, lanes)),
                ),
                in_specs=[VMEM, SMEM] + [VMEM] * 8,
                out_specs=(ANY, VMEM),
                scratch_shapes=[
                    pltpu.VMEM((rows, 2 * WIDTH, span, lanes), jnp.float32),
                    pltpu.VMEM((span, lanes), jnp.float32),
                    pltpu.SemaphoreType.DMA((3,)),
                ],
                compiler_params=params(),
                name="last_pitch_terms",
            )(
                halo,
                turn,
                neighbour_blocks,
                dissipation,
                pseudo_step,
                state,
                error,
                following,
                squares[0],
                square,
            )
    shares = lax.all_to_all(share, ("pitch", "span", "axial"), 0, 0, tiled=True)
    totals = jnp.sum(shares, axis=(0, 1))[:ITERS]
    cell_count = float(rows * planes * span * lanes * devices)
    norms = jnp.sqrt(totals / cell_count)
    return (out.reshape(parts, nv, planes, span, lanes), norms)


def solution(mesh):
    placed = (
        P(None, None, "pitch", "span", "axial"),
        P(None, None, "pitch", "span", "axial"),
        P(None, None, "pitch", "span", "axial"),
        P(None, None, None, "pitch", "span", "axial"),
        P(None, "pitch", "span", "axial"),
        P("pitch", "span", "axial"),
        P("pitch", "span", "axial"),
        P(),
    )
    return jax.shard_map(
        body,
        mesh=mesh,
        in_specs=placed,
        out_specs=(P(None, None, "pitch", "span", "axial"), P()),
        check_vma=False,
    )
```

time: 170 us -> 67.2 us (0.40)
  other arithmetic: 54.7 us -> 0.65 us
  local copies, waits for them, and re-layouts: 37 us -> 6.85 us
  blocking collectives: 39.3 us -> 14.4 us
  waiting for transfers between devices: 21 us -> 5.84 us
  Pallas kernels: 0 us -> 14.9 us
  starting transfers between devices: 15.5 us -> 22.4 us
    psum x1 -> x0, blocking collectives: 39.3 us -> none  [body(): global_sums.append(lax.psum(local_square, ('pitch', 'span', 'axial')))]
    reduce_sum x2 -> x1, other arithmetic: 24.4 us -> 0.05 us  [body(): totals = jnp.sum(shares, axis=(0, 1))[:ITERS]]
    slice x10 -> x0, local copies, waits for them, and re-layouts: 17.8 us -> none  [the longest x7 10.9 us: extended_2(): lax.slice_in_dim(cells, cells.shape[dim] - width, cells.shape[dim], axis=...]
    ppermute x12 -> x10, waiting for transfers between devices: 21 us -> 5.84 us  [the longest x2 4.77 us: exchange_rest(): lax.ppermute(low, 'span', down_span)]
    pallas_call x0 -> x7, Pallas kernels: none -> 14.9 us  [the longest x2 10.5 us: body(): pl.pallas_call(main_kernel, out_shape=(kept(wide), kept(block), kept((spa...]
    all_to_all x0 -> x1, blocking collectives: none -> 14.4 us  [body(): shares = lax.all_to_all(share, ('pitch', 'span', 'axial'), 0, 0, tiled=True)]
    mul x13 -> x0, other arithmetic: 12.6 us -> none  [the longest x11 10.7 us: block_apply(): blocks[:, column].astype(jnp.float32)[None] * vector_in[:, column][:, None]]
    convert_element_type x7 -> x0, other arithmetic: 10.1 us -> none  [block_apply(): blocks[:, column].astype(jnp.float32)[None] * vector_in[:, column][:, None]]
  transfers between devices with their start and end apart: 12 -> 10, of which waited for: 6 -> 3; matrix products, arithmetic and copies ran while one was open for 24% -> 0% of each run, Pallas kernels for 0% -> 18%
where the time goes in v1:
time: 67.2 us; the launch traced here: 66.7 us
  starting transfers between devices  22.4 us (33%)
  Pallas kernels  14.9 us (22%)
  blocking collectives  14.4 us (21%)
  local copies, waits for them, and re-layouts  6.85 us (10%)
  waiting for transfers between devices  5.84 us (9%)
  between operations  1.6 us (2%)
    all_to_all x1, blocking collectives, body(): shares = lax.all_to_all(share, ('pitch', 'span', 'axial'), 0, 0, tiled=True)  14.4 us
    pallas_call x2, Pallas kernels, body(): pl.pallas_call(main_kernel, out_shape=(kept(wide), kept(block), kept((spa...  10.5 us
    ppermute x2, starting transfers between devices, exchange_rest(): lax.ppermute(high, 'span', up_span)  6.98 us
    unnamed x16, local copies, waits for them, and re-layouts  6.85 us
    ppermute x2, starting transfers between devices, exchange_rest(): lax.ppermute(axial, 'axial', up_axial)  6.66 us
    ppermute x2, waiting for transfers between devices, exchange_rest(): lax.ppermute(low, 'span', down_span)  4.77 us
    ppermute x2, starting transfers between devices, exchange_pitch(): return lax.ppermute(faces, 'pitch', up)  3.6 us
    ppermute x2, starting transfers between devices, exchange_rest(): lax.ppermute(axial, 'axial', down_axial)  2.58 us
  transfers between devices with their start and end apart: 10, of which 3 were waited for; matrix products, arithmetic and copies ran while one was open for 0% of the time, Pallas kernels for 18%

profile of v1, /device:TPU:0, one launch (start us, length us, event | category | flops | bytes accessed | tf_op | source)
XLA Modules:
  0.0 66.7 jit_solution(11827422094773696648)
XLA Ops:
  0.6 1.2 %copy-done.3 = f32[2,6,8,16,128]{4,3,2,1,0:T(8,128)S(1)} copy-done((f32[2,6,8,16,128]{4,3,2,1,0:T(8,128)S(1)}, f32[2,6,8,16,128]{4,3,2,1,0:T(8,128)}, u32[]{:S(2)}) %copy-start.3) | copy-done | bytes 786456
  1.9 0.8 %pitch_faces.1 = f32[2,12,2,16,128]{4,3,2,1,0:T(8,128)} custom-call(f32[12,8,16,128]{3,2,1,0:T(8,128)S(1)} %bitcast.9), custom_call_target="tpu_custom_call" | custom-call | tf_op jit(solution)/shard_map/pitch_faces/pallas_call | solution.py:364
  2.7 3.0 %collective-permute-start = (f32[2,12,2,16,128]{4,3,2,1,0:T(8,128)}, f32[2,12,2,16,128]{4,3,2,1,0:T(8,128)S(1)}, u32[]{:S(2)}, u32[]{:S(2)}) collective-permute-start(f32[2,12,2,16,128]{4,3,2,1,0:T(8,128)} %pitch_faces.1), channel_id=1, source_target_pairs={{0,16},{16,0},{1,17},{17,1},{2,18},{18,2},{3,19},{19,3},{4,20},{20... | collective-permute-start | bytes 1179656 | tf_op jit(solution)/shard_map/ppermute | solution.py:347
  5.7 1.0 %first_pack.1 = (f32[12,12,16,128]{3,2,1,0:T(8,128)S(1)}, f32[12,8,2,128]{3,2,1,0:T(2,128)}, f32[12,8,2,128]{3,2,1,0:T(2,128)}, f32[3,16,128]{2,1,0:T(8,128)}) custom-call(f32[12,8,16,128]{3,2,1,0:T(8,128)S(1)} %bitcast.10), custom_call_target="tpu_custom_call" | custom-call | tf_op jit(solution)/shard_map/first_pack/pallas_call | solution.py:373
  6.7 1.3 %collective-permute-start.4 = (f32[3,16,128]{2,1,0:T(8,128)}, f32[3,16,128]{2,1,0:T(8,128)}, u32[]{:S(2)}, u32[]{:S(2)}) collective-permute-start(f32[3,16,128]{2,1,0:T(8,128)} %get-tuple-element.23), channel_id=1, source_target_pairs={{1,0},{2,1},{3,2},{5,4},{6,5},{7,6},{9,8},{10,9},{11,10},{13,12},{... | collective-permute-start | bytes 73736 | tf_op jit(solution)/shard_map/ppermute | solution.py:361
  8.0 3.6 %collective-permute-start.3 = (f32[3,16,128]{2,1,0:T(8,128)}, f32[3,16,128]{2,1,0:T(8,128)}, u32[]{:S(2)}, u32[]{:S(2)}) collective-permute-start(f32[3,16,128]{2,1,0:T(8,128)} %get-tuple-element.23), channel_id=1, source_target_pairs={{0,1},{1,2},{2,3},{4,5},{5,6},{6,7},{8,9},{9,10},{10,11},{12,13},{... | collective-permute-start | bytes 73736 | tf_op jit(solution)/shard_map/ppermute | solution.py:360
  11.6 4.1 %collective-permute-start.1 = (f32[12,8,2,128]{3,2,1,0:T(2,128)}, f32[12,8,2,128]{3,2,1,0:T(2,128)}, u32[]{:S(2)}, u32[]{:S(2)}) collective-permute-start(f32[12,8,2,128]{3,2,1,0:T(2,128)} %get-tuple-element.21), channel_id=1, source_target_pairs={{0,4},{4,8},{8,12},{1,5},{5,9},{9,13},{2,6},{6,10},{10,14},{3,7},{... | collective-permute-start | bytes 294920 | tf_op jit(solution)/shard_map/ppermute | solution.py:358
  15.7 1.3 %collective-permute-start.2 = (f32[12,8,2,128]{3,2,1,0:T(2,128)}, f32[12,8,2,128]{3,2,1,0:T(2,128)}, u32[]{:S(2)}, u32[]{:S(2)}) collective-permute-start(f32[12,8,2,128]{3,2,1,0:T(2,128)} %get-tuple-element.22), channel_id=1, source_target_pairs={{4,0},{8,4},{12,8},{5,1},{9,5},{13,9},{6,2},{10,6},{14,10},{7,3},{... | collective-permute-start | bytes 294920 | tf_op jit(solution)/shard_map/ppermute | solution.py:359
  18.2 4.7 %collective-permute-done.2.high_ref = f32[12,8,2,128]{3,2,1,0:T(2,128)} collective-permute-done((f32[12,8,2,128]{3,2,1,0:T(2,128)}, f32[12,8,2,128]{3,2,1,0:T(2,128)}, u32[]{:S(2)}, u32[]{:S(2)}) %collective-permute-start.2) | collective-permute-done | bytes 98336 | tf_op jit(solution)/shard_map/ppermute | solution.py:359
  22.9 3.0 %copy-done = bf16[6,6,6,8,16,128]{5,4,3,2,1,0:T(8,128)(2,1)S(1)} copy-done((bf16[6,6,6,8,16,128]{5,4,3,2,1,0:T(8,128)(2,1)S(1)}, bf16[6,6,6,8,16,128]{5,4,3,2,1,0:T(8,128)(2,1)}, u32[]{:S(2)}) %copy-start) | copy-done | bytes 7077912
  25.9 0.9 %copy-done.5 = f32[3,8,16,128]{3,2,1,0:T(8,128)S(1)} copy-done((f32[3,8,16,128]{3,2,1,0:T(8,128)S(1)}, f32[3,8,16,128]{3,2,1,0:T(8,128)}, u32[]{:S(2)}) %copy-start.5) | copy-done | bytes 196632
  26.8 0.8 %copy-done.6 = f32[8,16,128]{2,1,0:T(8,128)S(1)} copy-done((f32[8,16,128]{2,1,0:T(8,128)S(1)}, f32[8,16,128]{2,1,0:T(8,128)}, u32[]{:S(2)}) %copy-start.6) | copy-done | bytes 65560
  27.7 0.8 %copy-done.7 = f32[8,16,128]{2,1,0:T(8,128)S(1)} copy-done((f32[8,16,128]{2,1,0:T(8,128)S(1)}, f32[8,16,128]{2,1,0:T(8,128)}, u32[]{:S(2)}) %copy-start.7) | copy-done | bytes 65560
  28.5 5.8 %main.2 = (f32[12,12,16,128]{3,2,1,0:T(8,128)S(1)}, f32[12,8,16,128]{3,2,1,0:T(8,128)S(1)}, f32[16,128]{1,0:T(8,128)S(1)}) custom-call(f32[12,12,16,128]{3,2,1,0:T(8,128)S(1)} %get-tuple-element.20.wide_ref, f32[12,8,2,128]{3,2,1,0:T(2,128)} %collective-permute-done.1.low_ref, f32[12,8,2,128]{3,2,1,0:T(2,128)} %collective-permute-done.2.high_ref, ...), custom_call_target="tpu_custom_call" | custom-call | tf_op jit(solution)/shard_map/main/pallas_call | solution.py:393
  34.3 0.8 %pitch_terms.1 = (f32[12,12,16,128]{3,2,1,0:T(8,128)S(1)}, f32[2,12,2,16,128]{4,3,2,1,0:T(8,128)S(1)}, f32[16,128]{1,0:T(8,128)S(1)}) custom-call(f32[2,12,2,16,128]{4,3,2,1,0:T(8,128)S(1)} %collective-permute-done.halo_ref, f32[4]{0:T(128)S(1)} %pad_maximum_fusion.turn_ref, ...), custom_call_target="tpu_custom_call", output_to_operand_aliasing={{0}: (8, {})} | custom-call | tf_op jit(solution)/shard_map/pitch_terms/pallas_call | solution.py:415
  35.1 0.6 collective-permute-start.5
  36.0 2.9 %collective-permute-start.6 = (f32[12,8,2,128]{3,2,1,0:T(2,128)S(1)}, f32[12,8,2,128]{3,2,1,0:T(2,128)S(1)}, u32[]{:S(2)}, u32[]{:S(2)}) collective-permute-start(f32[12,8,2,128]{3,2,1,0:T(2,128)S(1)} %get-tuple-element.29), channel_id=1, source_target_pairs={{0,4},{4,8},{8,12},{1,5},{5,9},{9,13},{2,6},{6,10},{10,14},{3,7},{... | collective-permute-start | bytes 294920 | tf_op jit(solution)/shard_map/ppermute | solution.py:358
  38.9 1.3 %collective-permute-start.7 = (f32[12,8,2,128]{3,2,1,0:T(2,128)S(1)}, f32[12,8,2,128]{3,2,1,0:T(2,128)S(1)}, u32[]{:S(2)}, u32[]{:S(2)}) collective-permute-start(f32[12,8,2,128]{3,2,1,0:T(2,128)S(1)} %get-tuple-element.30), channel_id=1, source_target_pairs={{4,0},{8,4},{12,8},{5,1},{9,5},{13,9},{6,2},{10,6},{14,10},{7,3},{... | collective-permute-start | bytes 294920 | tf_op jit(solution)/shard_map/ppermute | solution.py:359
  40.1 1.3 %collective-permute-start.9 = (f32[3,16,128]{2,1,0:T(8,128)S(1)}, f32[3,16,128]{2,1,0:T(8,128)S(1)}, u32[]{:S(2)}, u32[]{:S(2)}) collective-permute-start(f32[3,16,128]{2,1,0:T(8,128)S(1)} %get-tuple-element.31), channel_id=1, source_target_pairs={{1,0},{2,1},{3,2},{5,4},{6,5},{7,6},{9,8},{10,9},{11,10},{13,12},{... | collective-permute-start | bytes 73736 | tf_op jit(solution)/shard_map/ppermute | solution.py:361
  41.5 3.0 %collective-permute-start.8 = (f32[3,16,128]{2,1,0:T(8,128)S(1)}, f32[3,16,128]{2,1,0:T(8,128)S(1)}, u32[]{:S(2)}, u32[]{:S(2)}) collective-permute-start(f32[3,16,128]{2,1,0:T(8,128)S(1)} %get-tuple-element.31), channel_id=1, source_target_pairs={{0,1},{1,2},{2,3},{4,5},{5,6},{6,7},{8,9},{9,10},{10,11},{12,13},{... | collective-permute-start | bytes 73736 | tf_op jit(solution)/shard_map/ppermute | solution.py:360
  44.5 0.8 %collective-permute-done.8.axial_low_ref = f32[3,16,128]{2,1,0:T(8,128)S(1)} collective-permute-done((f32[3,16,128]{2,1,0:T(8,128)S(1)}, f32[3,16,128]{2,1,0:T(8,128)S(1)}, u32[]{:S(2)}, u32[]{:S(2)}) %collective-permute-start.8) | collective-permute-done | bytes 24608 | tf_op jit(solution)/shard_map/ppermute | solution.py:360
  45.4 4.7 %main.3 = (f32[12,12,16,128]{3,2,1,0:T(8,128)S(1)}, f32[12,8,16,128]{3,2,1,0:T(8,128)S(1)}, f32[16,128]{1,0:T(8,128)S(1)}) custom-call(f32[12,12,16,128]{3,2,1,0:T(8,128)S(1)} %get-tuple-element.28.wide_ref, f32[12,8,2,128]{3,2,1,0:T(2,128)S(1)} %collective-permute-done.6.low_ref, f32[12,8,2,128]{3,2,1,0:T(2,128)S(1)} %collective-permute-done.7.high_ref, ...), custom_call_target="tpu_custom_call" | custom-call | tf_op jit(solution)/shard_map/main/pallas_call | solution.py:393
  50.1 1.6 %last_pitch_terms.1 = (f32[12,8,16,128]{3,2,1,0:T(8,128)}, f32[32,1,128]{2,1,0:T(1,128)S(1)}) custom-call(f32[2,12,2,16,128]{4,3,2,1,0:T(8,128)S(1)} %collective-permute-done.5.halo_ref, f32[4]{0:T(128)S(1)} %pad_maximum_fusion.turn_ref, bf16[6,6,6,8,16,128]{5,4,3,2,1,0:T(8,128)(2,1)S(1)} %copy-done.1, f32[3,8,16,128]{3,2,1,0:T(8,128)S(1)} %copy-done.5, ...), custom_call_target="tpu_custom_call" | custom-call | tf_op jit(solution)/shard_map/last_pitch_terms/pallas_call | solution.py:444
  51.7 14.4 %all_to_all.5 = f32[32,1,128]{2,1,0:T(1,128)S(1)} all-to-all(f32[32,1,128]{2,1,0:T(1,128)S(1)} %get-tuple-element.37), channel_id=1, replica_groups=mesh['pitch'=2,'span'=4,'axial'=4] {'pitch','span','axial'}, dimensions={0} | all-to-all | bytes 32768 | tf_op jit(solution)/shard_map/all_to_all | solution.py:471
  (23 shorter events, 1.2 us)
Async XLA Ops:
  0.6 22.3 %copy-start.2 = (bf16[6,6,8,16,128]{4,3,2,1,0:T(8,128)(2,1)S(1)}, bf16[6,6,8,16,128]{4,3,2,1,0:T(8,128)(2,1)}, u32[]{:S(2)}) copy-start(bf16[6,6,8,16,128]{4,3,2,1,0:T(8,128)(2,1)} %diag_ref.3) | copy-start | bytes 3538948
  0.6 1.2 %copy-start.3 = (f32[2,6,8,16,128]{4,3,2,1,0:T(8,128)S(1)}, f32[2,6,8,16,128]{4,3,2,1,0:T(8,128)}, u32[]{:S(2)}) copy-start(f32[2,6,8,16,128]{4,3,2,1,0:T(8,128)} %param.8) | copy-start | bytes 2359300
  1.9 21.0 %copy-start.4 = (f32[2,6,8,16,128]{4,3,2,1,0:T(8,128)S(1)}, f32[2,6,8,16,128]{4,3,2,1,0:T(8,128)}, u32[]{:S(2)}) copy-start(f32[2,6,8,16,128]{4,3,2,1,0:T(8,128)} %param.9) | copy-start | bytes 2359300
  2.7 31.6 %collective-permute-start = (f32[2,12,2,16,128]{4,3,2,1,0:T(8,128)}, f32[2,12,2,16,128]{4,3,2,1,0:T(8,128)S(1)}, u32[]{:S(2)}, u32[]{:S(2)}) collective-permute-start(f32[2,12,2,16,128]{4,3,2,1,0:T(8,128)} %pitch_faces.1), channel_id=1, source_target_pairs={{0,16},{16,0},{1,17},{17,1},{2,18},{18,2},{3,19},{19,3},{4,20},{20... | collective-permute-start | bytes 1179656 | tf_op jit(solution)/shard_map/ppermute | solution.py:347
  6.7 11.2 %collective-permute-start.4 = (f32[3,16,128]{2,1,0:T(8,128)}, f32[3,16,128]{2,1,0:T(8,128)}, u32[]{:S(2)}, u32[]{:S(2)}) collective-permute-start(f32[3,16,128]{2,1,0:T(8,128)} %get-tuple-element.23), channel_id=1, source_target_pairs={{1,0},{2,1},{3,2},{5,4},{6,5},{7,6},{9,8},{10,9},{11,10},{13,12},{... | collective-permute-start | bytes 73736 | tf_op jit(solution)/shard_map/ppermute | solution.py:361
  8.0 9.9 %collective-permute-start.3 = (f32[3,16,128]{2,1,0:T(8,128)}, f32[3,16,128]{2,1,0:T(8,128)}, u32[]{:S(2)}, u32[]{:S(2)}) collective-permute-start(f32[3,16,128]{2,1,0:T(8,128)} %get-tuple-element.23), channel_id=1, source_target_pairs={{0,1},{1,2},{2,3},{4,5},{5,6},{6,7},{8,9},{9,10},{10,11},{12,13},{... | collective-permute-start | bytes 73736 | tf_op jit(solution)/shard_map/ppermute | solution.py:360
  11.6 6.5 %collective-permute-start.1 = (f32[12,8,2,128]{3,2,1,0:T(2,128)}, f32[12,8,2,128]{3,2,1,0:T(2,128)}, u32[]{:S(2)}, u32[]{:S(2)}) collective-permute-start(f32[12,8,2,128]{3,2,1,0:T(2,128)} %get-tuple-element.21), channel_id=1, source_target_pairs={{0,4},{4,8},{8,12},{1,5},{5,9},{9,13},{2,6},{6,10},{10,14},{3,7},{... | collective-permute-start | bytes 294920 | tf_op jit(solution)/shard_map/ppermute | solution.py:358
  15.7 7.2 %collective-permute-start.2 = (f32[12,8,2,128]{3,2,1,0:T(2,128)}, f32[12,8,2,128]{3,2,1,0:T(2,128)}, u32[]{:S(2)}, u32[]{:S(2)}) collective-permute-start(f32[12,8,2,128]{3,2,1,0:T(2,128)} %get-tuple-element.22), channel_id=1, source_target_pairs={{4,0},{8,4},{12,8},{5,1},{9,5},{13,9},{6,2},{10,6},{14,10},{7,3},{... | collective-permute-start | bytes 294920 | tf_op jit(solution)/shard_map/ppermute | solution.py:359
  22.9 3.0 %copy-start = (bf16[6,6,6,8,16,128]{5,4,3,2,1,0:T(8,128)(2,1)S(1)}, bf16[6,6,6,8,16,128]{5,4,3,2,1,0:T(8,128)(2,1)}, u32[]{:S(2)}) copy-start(bf16[6,6,6,8,16,128]{5,4,3,2,1,0:T(8,128)(2,1)} %neighbour_ref.7) | copy-start | bytes 21233668
  25.9 0.9 %copy-start.5 = (f32[3,8,16,128]{3,2,1,0:T(8,128)S(1)}, f32[3,8,16,128]{3,2,1,0:T(8,128)}, u32[]{:S(2)}) copy-start(f32[3,8,16,128]{3,2,1,0:T(8,128)} %dissipation_ref.7) | copy-start | bytes 589828
  26.8 0.8 %copy-start.6 = (f32[8,16,128]{2,1,0:T(8,128)S(1)}, f32[8,16,128]{2,1,0:T(8,128)}, u32[]{:S(2)}) copy-start(f32[8,16,128]{2,1,0:T(8,128)} %step_ref.7) | copy-start | bytes 196612
  27.7 0.8 %copy-start.7 = (f32[8,16,128]{2,1,0:T(8,128)S(1)}, f32[8,16,128]{2,1,0:T(8,128)}, u32[]{:S(2)}) copy-start(f32[8,16,128]{2,1,0:T(8,128)} %omega_ref.3) | copy-start | bytes 196612
  28.5 5.8 %copy-start.1 = (bf16[6,6,6,8,16,128]{5,4,3,2,1,0:T(8,128)(2,1)S(1)}, bf16[6,6,6,8,16,128]{5,4,3,2,1,0:T(8,128)(2,1)}, u32[]{:S(2)}) copy-start(bf16[6,6,6,8,16,128]{5,4,3,2,1,0:T(8,128)(2,1)} %neighbour_ref.7) | copy-start | bytes 21233668
  35.1 15.0 %collective-permute-start.5 = (f32[2,12,2,16,128]{4,3,2,1,0:T(8,128)S(1)}, f32[2,12,2,16,128]{4,3,2,1,0:T(8,128)S(1)}, u32[]{:S(2)}, u32[]{:S(2)}) collective-permute-start(f32[2,12,2,16,128]{4,3,2,1,0:T(8,128)S(1)} %get-tuple-element.27), channel_id=1, source_target_pairs={{0,16},{16,0},{1,17},{17,1},{2,18},{18,2},{3,19},{19,3},{4,20},{20... | collective-permute-start | bytes 1179656 | tf_op jit(solution)/shard_map/ppermute | solution.py:347
  36.0 9.4 %collective-permute-start.6 = (f32[12,8,2,128]{3,2,1,0:T(2,128)S(1)}, f32[12,8,2,128]{3,2,1,0:T(2,128)S(1)}, u32[]{:S(2)}, u32[]{:S(2)}) collective-permute-start(f32[12,8,2,128]{3,2,1,0:T(2,128)S(1)} %get-tuple-element.29), channel_id=1, source_target_pairs={{0,4},{4,8},{8,12},{1,5},{5,9},{9,13},{2,6},{6,10},{10,14},{3,7},{... | collective-permute-start | bytes 294920 | tf_op jit(solution)/shard_map/ppermute | solution.py:358
  38.9 6.5 %collective-permute-start.7 = (f32[12,8,2,128]{3,2,1,0:T(2,128)S(1)}, f32[12,8,2,128]{3,2,1,0:T(2,128)S(1)}, u32[]{:S(2)}, u32[]{:S(2)}) collective-permute-start(f32[12,8,2,128]{3,2,1,0:T(2,128)S(1)} %get-tuple-element.30), channel_id=1, source_target_pairs={{4,0},{8,4},{12,8},{5,1},{9,5},{13,9},{6,2},{10,6},{14,10},{7,3},{... | collective-permute-start | bytes 294920 | tf_op jit(solution)/shard_map/ppermute | solution.py:359
  40.1 4.3 %collective-permute-start.9 = (f32[3,16,128]{2,1,0:T(8,128)S(1)}, f32[3,16,128]{2,1,0:T(8,128)S(1)}, u32[]{:S(2)}, u32[]{:S(2)}) collective-permute-start(f32[3,16,128]{2,1,0:T(8,128)S(1)} %get-tuple-element.31), channel_id=1, source_target_pairs={{1,0},{2,1},{3,2},{5,4},{6,5},{7,6},{9,8},{10,9},{11,10},{13,12},{... | collective-permute-start | bytes 73736 | tf_op jit(solution)/shard_map/ppermute | solution.py:361
  41.5 3.9 %collective-permute-start.8 = (f32[3,16,128]{2,1,0:T(8,128)S(1)}, f32[3,16,128]{2,1,0:T(8,128)S(1)}, u32[]{:S(2)}, u32[]{:S(2)}) collective-permute-start(f32[3,16,128]{2,1,0:T(8,128)S(1)} %get-tuple-element.31), channel_id=1, source_target_pairs={{0,1},{1,2},{2,3},{4,5},{5,6},{6,7},{8,9},{9,10},{10,11},{12,13},{... | collective-permute-start | bytes 73736 | tf_op jit(solution)/shard_map/ppermute | solution.py:360

commit v2 on v1

--- a/solution.py
+++ b/solution.py
@@ -12,8 +12,9 @@
 VMEM = pl.BlockSpec(memory_space=pltpu.VMEM)
 SMEM = pl.BlockSpec(memory_space=pltpu.SMEM)
 ANY = pl.BlockSpec(memory_space=pl.ANY)
-VMEM_LIMIT = 40 * 1024 * 1024
+VMEM_LIMIT = 4 * 1024 * 1024
 PAD = 8
+GROUPS = 4
 
 
 def resident(values):
@@ -49,8 +50,9 @@
     head.wait()
 
 
-def pack_faces(wide_ref, low_ref, high_ref, axial_ref):
+def pack_faces(wide_ref, even_ref, odd_ref, axial_ref):
     rows, wide, span, lanes = wide_ref.shape
+    span_even = lax.axis_index("span") % 2 == 0
     planes = wide - 2 * WIDTH
     lane = lax.broadcasted_iota(jnp.int32, (span, lanes), 1)
     groups = lane_groups(rows, planes, lanes)
@@ -59,8 +61,10 @@
         group, base = lane_place(k, planes, lanes)
         for p in range(planes):
             cells = wide_ref[k, p + WIDTH]
-            low_ref[k, p] = cells[:WIDTH]
-            high_ref[k, p] = cells[span - WIDTH :]
+            low = cells[:WIDTH]
+            high = cells[span - WIDTH :]
+            even_ref[k, p] = jnp.where(span_even, high, low)
+            odd_ref[k, p] = jnp.where(span_even, low, high)
             place = base + p
             moved = pltpu.roll(cells, (2 * WIDTH * place + WIDTH) % lanes, axis=1)
             if packed[group] is None:
@@ -71,7 +75,7 @@
             axial_ref[group] = packed[group]
 
 
-def first_pack_kernel(guess_ref, wide_ref, low_ref, high_ref, axial_ref, sem):
+def first_pack_kernel(guess_ref, wide_ref, even_ref, odd_ref, axial_ref, sem):
     rows, wide, span, lanes = wide_ref.shape
     planes = wide - 2 * WIDTH
     copy = pltpu.make_async_copy(guess_ref, wide_ref.at[:, WIDTH : WIDTH + planes], sem)
@@ -80,85 +84,230 @@
         for p in (0, 1, wide - 2, wide - 1):
             wide_ref[k, p] = jnp.zeros((span, lanes), jnp.float32)
     copy.wait()
-    pack_faces(wide_ref, low_ref, high_ref, axial_ref)
-
-
-def pack_kernel(wide_ref, low_ref, high_ref, axial_ref):
-    pack_faces(wide_ref, low_ref, high_ref, axial_ref)
-
-
-def main_kernel(
+    pack_faces(wide_ref, even_ref, odd_ref, axial_ref)
+
+
+def pack_kernel(wide_ref, even_ref, odd_ref, axial_ref):
+    pack_faces(wide_ref, even_ref, odd_ref, axial_ref)
+
+
+class Loads:
+    def __init__(self, pairs, sems, planes):
+        self.pairs = pairs
+        self.sems = sems
+        self.size = planes // sems.shape[1]
+
+    def copies(self, group):
+        return [
+            pltpu.make_async_copy(
+                source.at[(slice(None),) * dim + (pl.ds(group * self.size, self.size),)],
+                target.at[(slice(None),) * dim + (pl.ds(group * self.size, self.size),)],
+                self.sems.at[at, group],
+            )
+            for at, (source, target, dim) in enumerate(self.pairs)
+        ]
+
+    def start(self):
+        for group in range(self.sems.shape[1]):
+            for copy in self.copies(group):
+                copy.start()
+
+    def ready(self, p):
+        @pl.when(p % self.size == 0)
+        def _():
+            for copy in self.copies(p // self.size):
+                copy.wait()
+
+
+def near_loading_kernel(
     wide_ref,
-    low_ref,
-    high_ref,
-    axial_low_ref,
-    axial_high_ref,
+    neighbour_hbm,
+    diag_hbm,
+    right_hbm,
+    dissipation_hbm,
+    omega_hbm,
+    error_ref,
     neighbour_ref,
     diag_ref,
     right_ref,
     dissipation_ref,
     omega_ref,
+    sems,
+):
+    loads = Loads(
+        [
+            (right_hbm, right_ref, 1),
+            (dissipation_hbm, dissipation_ref, 1),
+            (omega_hbm, omega_ref, 0),
+            (diag_hbm, diag_ref, 2),
+            (neighbour_hbm.at[0:2], neighbour_ref, 3),
+        ],
+        sems,
+        error_ref.shape[1],
+    )
+    near_sweep(
+        wide_ref,
+        neighbour_ref,
+        diag_ref,
+        right_ref,
+        dissipation_ref,
+        omega_ref,
+        error_ref,
+        loads,
+    )
+
+
+def near_kernel(*refs):
+    near_sweep(*refs, None)
+
+
+def near_sweep(
+    wide_ref, neighbour_ref, diag_ref, right_ref, dissipation_ref, omega_ref, error_ref, loads
+):
+    rows, planes, span, lanes = error_ref.shape
+    nv = rows // 2
+    if loads is not None:
+        loads.start()
+
+    def plane(p, carry):
+        if loads is not None:
+            loads.ready(p)
+        omega = omega_ref[p]
+        spread = dissipation_ref[0, p]
+        total = []
+        for k in range(rows):
+            other = wide_ref[(k + nv) % rows, p + WIDTH]
+            turned = -omega * other if k < nv else omega * other
+            far = wide_ref[k, p] + wide_ref[k, p + 2 * WIDTH]
+            total.append((turned - right_ref[k, p]) + spread * far)
+        for j in range(nv):
+            for at, blocks in (
+                (2, lambda i: diag_ref[i, j, p]),
+                (1, lambda i: neighbour_ref[0, i, j, p]),
+                (3, lambda i: neighbour_ref[1, i, j, p]),
+            ):
+                real = wide_ref[j, p + at]
+                imag = wide_ref[nv + j, p + at]
+                for i in range(nv):
+                    block = blocks(i).astype(jnp.float32)
+                    total[i] = total[i] + block * real
+                    total[nv + i] = total[nv + i] + block * imag
+        for k in range(rows):
+            error_ref[k, p] = total[k]
+        return carry
+
+    lax.fori_loop(0, planes, plane, 0)
+
+
+def far_loading_kernel(
+    wide_ref,
+    span_even_ref,
+    span_odd_ref,
+    axial_even_ref,
+    axial_odd_ref,
+    neighbour_hbm,
+    dissipation_ref,
+    step_hbm,
+    error_in_ref,
+    error_ref,
+    next_ref,
+    square_ref,
+    neighbour_ref,
     step_ref,
+    span_buf,
+    axial_buf,
+    sems,
+):
+    loads = Loads(
+        [(step_hbm, step_ref, 0), (neighbour_hbm.at[2:6], neighbour_ref, 3)],
+        sems,
+        step_ref.shape[0],
+    )
+    far_sweep(
+        wide_ref,
+        span_even_ref,
+        span_odd_ref,
+        axial_even_ref,
+        axial_odd_ref,
+        neighbour_ref,
+        dissipation_ref,
+        step_ref,
+        error_in_ref,
+        error_ref,
+        next_ref,
+        square_ref,
+        span_buf,
+        axial_buf,
+        loads,
+    )
+
+
+def far_kernel(*refs):
+    far_sweep(*refs, None)
+
+
+def far_sweep(
+    wide_ref,
+    span_even_ref,
+    span_odd_ref,
+    axial_even_ref,
+    axial_odd_ref,
+    neighbour_ref,
+    dissipation_ref,
+    step_ref,
+    error_in_ref,
+    error_ref,
     next_ref,
-    error_ref,
     square_ref,
     span_buf,
     axial_buf,
+    loads,
 ):
     rows, wide, span, lanes = wide_ref.shape
     planes = wide - 2 * WIDTH
     nv = rows // 2
+    if loads is not None:
+        loads.start()
+    span_even = lax.axis_index("span") % 2 == 0
+    axial_even = lax.axis_index("axial") % 2 == 0
     lane = lax.broadcasted_iota(jnp.int32, (span, lanes), 1)
+    from_even = (lane % (2 * WIDTH) >= WIDTH) == axial_even
     for group in range(axial_buf.shape[0]):
-        axial_buf[group] = jnp.where(
-            lane % (2 * WIDTH) < WIDTH, axial_low_ref[group], axial_high_ref[group]
-        )
+        axial_buf[group] = jnp.where(from_even, axial_even_ref[group], axial_odd_ref[group])
     for k in range(rows):
         for p in (0, 1, wide - 2, wide - 1):
             next_ref[k, p] = jnp.zeros((span, lanes), jnp.float32)
     square_ref[...] = jnp.zeros_like(square_ref)
 
     def plane(p, carry):
+        if loads is not None:
+            loads.ready(p)
         for k in range(rows):
-            span_buf[k, PAD - WIDTH : PAD] = low_ref[k, p]
+            at_even = span_even_ref[k, p]
+            at_odd = span_odd_ref[k, p]
+            span_buf[k, PAD - WIDTH : PAD] = jnp.where(span_even, at_odd, at_even)
             span_buf[k, PAD : PAD + span] = wide_ref[k, p + WIDTH]
-            span_buf[k, PAD + span : PAD + span + WIDTH] = high_ref[k, p]
-        total = [None] * rows
-
-        def add(k, value):
-            total[k] = value if total[k] is None else total[k] + value
-
-        def column(blocks, j, real, imag):
-            for i in range(nv):
-                block = blocks(i, j).astype(jnp.float32)
-                add(i, block * real)
-                add(nv + i, block * imag)
-
-        spread_pitch = dissipation_ref[0, p]
+            span_buf[k, PAD + span : PAD + span + WIDTH] = jnp.where(span_even, at_even, at_odd)
+        total = [error_in_ref[k, p] for k in range(rows)]
         spread_span = dissipation_ref[1, p]
         spread_axial = dissipation_ref[2, p]
+
+        def column(direction, j, real, imag):
+            for i in range(nv):
+                block = neighbour_ref[direction, i, j, p].astype(jnp.float32)
+                total[i] = total[i] + block * real
+                total[nv + i] = total[nv + i] + block * imag
+
         for j in range(nv):
             pair = (j, nv + j)
-            column(lambda i, j: diag_ref[i, j, p], j, *[wide_ref[k, p + 2] for k in pair])
-            column(lambda i, j: neighbour_ref[0, i, j, p], j, *[wide_ref[k, p + 1] for k in pair])
-            column(lambda i, j: neighbour_ref[1, i, j, p], j, *[wide_ref[k, p + 3] for k in pair])
-            column(
-                lambda i, j: neighbour_ref[2, i, j, p],
-                j,
-                *[span_buf[k, PAD - 1 : PAD - 1 + span] for k in pair],
-            )
-            column(
-                lambda i, j: neighbour_ref[3, i, j, p],
-                j,
-                *[span_buf[k, PAD + 1 : PAD + 1 + span] for k in pair],
-            )
+            column(0, j, *[span_buf[k, PAD - 1 : PAD - 1 + span] for k in pair])
+            column(1, j, *[span_buf[k, PAD + 1 : PAD + 1 + span] for k in pair])
             lower = []
             upper = []
             for k in pair:
                 cells = wide_ref[k, p + WIDTH]
                 group, base = lane_place(k, planes, lanes)
                 shift = lanes - WIDTH - 2 * WIDTH * base - 2 * WIDTH * p
-                shift = jnp.where(shift < 0, shift + lanes, shift)
                 halo = pltpu.roll(axial_buf[group], shift, axis=1)
                 low_near = jnp.where(lane >= lanes - 1, halo, cells)
                 high_near = jnp.where(lane < 1, halo, cells)
@@ -167,29 +316,20 @@
                 lower.append(pltpu.roll(low_near, 1, axis=1))
                 upper.append(pltpu.roll(high_near, lanes - 1, axis=1))
                 far = pltpu.roll(low_far, 2, axis=1) + pltpu.roll(high_far, lanes - 2, axis=1)
-                add(k, spread_axial * far)
-                add(
-                    k,
-                    spread_span
-                    * (
-                        span_buf[k, PAD - 2 : PAD - 2 + span]
-                        + span_buf[k, PAD + 2 : PAD + 2 + span]
-                    ),
+                total[k] = total[k] + spread_axial * far
+                far = (
+                    span_buf[k, PAD - 2 : PAD - 2 + span] + span_buf[k, PAD + 2 : PAD + 2 + span]
                 )
-                add(k, spread_pitch * (wide_ref[k, p] + wide_ref[k, p + 4]))
-            column(lambda i, j: neighbour_ref[4, i, j, p], j, *lower)
-            column(lambda i, j: neighbour_ref[5, i, j, p], j, *upper)
-        omega = omega_ref[p]
+                total[k] = total[k] + spread_span * far
+            column(2, j, *lower)
+            column(3, j, *upper)
         step = step_ref[p]
         square = None
-        for i in range(nv):
-            real = wide_ref[i, p + WIDTH]
-            imag = wide_ref[nv + i, p + WIDTH]
-            for k, cells, turned in ((i, real, -omega * imag), (nv + i, imag, omega * real)):
-                error = (total[k] + turned) - right_ref[k, p]
-                error_ref[k, p] = error
-                next_ref[k, p + WIDTH] = cells - step * error
-                square = error * error if square is None else square + error * error
+        for k in range(rows):
+            error = total[k]
+            error_ref[k, p] = error
+            next_ref[k, p + WIDTH] = wide_ref[k, p + WIDTH] - step * error
+            square = error * error if square is None else square + error * error
         inner = jnp.logical_and(p >= WIDTH, p < planes - WIDTH)
         square_ref[...] += jnp.where(inner, square, 0.0)
         return carry
@@ -197,12 +337,17 @@
     lax.fori_loop(0, planes, plane, 0)
 
 
-def pitch_terms(halo_ref, turn_ref, neighbour_ref, dissipation_ref, error_ref, store):
+def pitch_terms(halo_ref, phase_ref, neighbour_ref, dissipation_ref, error_ref, store):
     rows, planes, span, lanes = error_ref.shape
     nv = rows // 2
+    pitch_at = lax.axis_index("pitch")
+    angle = jnp.full((span, lanes), phase_ref[0], jnp.float32)
+    cosine_end = jnp.cos(angle)
+    sine_end = jnp.sin(angle)
     for side in range(2):
-        cosine = turn_ref[2 * side]
-        sine_part = turn_ref[2 * side + 1]
+        at_end = pitch_at == (0 if side == 0 else lax.axis_size("pitch") - 1)
+        cosine = jnp.where(at_end, cosine_end, 1.0)
+        sine_part = jnp.where(at_end, -sine_end if side == 0 else sine_end, 0.0)
         near_at, far_at = (1, 0) if side == 0 else (0, 1)
         edge, inside = (0, 1) if side == 0 else (planes - 1, planes - 2)
 
@@ -231,7 +376,7 @@
 
 def turn_kernel(
     halo_ref,
-    turn_ref,
+    phase_ref,
     neighbour_ref,
     dissipation_ref,
     step_ref,
@@ -255,12 +400,12 @@
             faces_ref[0, k, p - (planes - WIDTH)] = value
         square_ref[...] += error * error
 
-    pitch_terms(halo_ref, turn_ref, neighbour_ref, dissipation_ref, error_ref, store)
+    pitch_terms(halo_ref, phase_ref, neighbour_ref, dissipation_ref, error_ref, store)
 
 
 def last_kernel(
     halo_ref,
-    turn_ref,
+    phase_ref,
     neighbour_ref,
     dissipation_ref,
     step_ref,
@@ -288,7 +433,7 @@
         edge_buf[k, at] = wide_ref[k, p + WIDTH] - step_ref[p] * error
         square_buf[...] += error * error
 
-    pitch_terms(halo_ref, turn_ref, neighbour_ref, dissipation_ref, error_ref, store)
+    pitch_terms(halo_ref, phase_ref, neighbour_ref, dissipation_ref, error_ref, store)
     low = pltpu.make_async_copy(
         edge_buf.at[:, 0:WIDTH], out_ref.at[:, 0:WIDTH], sems.at[1]
     )
@@ -325,20 +470,7 @@
     guess = guess.reshape(block)
     right_side = right_side.reshape(block)
 
-    cosine = jnp.cos(phase[0])
-    sine_part = jnp.sin(phase[0])
-    first_pitch = lax.axis_index("pitch") == 0
-    last_pitch = lax.axis_index("pitch") == pitch_count - 1
-    one = jnp.float32(1.0)
-    zero = jnp.float32(0.0)
-    turn = jnp.stack(
-        [
-            jnp.where(first_pitch, cosine, one),
-            jnp.where(first_pitch, -sine_part, zero),
-            jnp.where(last_pitch, cosine, one),
-            jnp.where(last_pitch, sine_part, zero),
-        ]
-    )
+    guess = pltpu.with_memory_space_constraint(guess, pltpu.HBM)
 
     def exchange_pitch(faces):
         up = [(i, (i + 1) % pitch_count) for i in range(pitch_count)]
@@ -349,16 +481,16 @@
             [lax.ppermute(faces[0], "pitch", up), lax.ppermute(faces[1], "pitch", down)]
         )
 
-    def exchange_rest(low, high, axial):
-        up_span = [(i, i + 1) for i in range(span_count - 1)]
-        down_span = [(i + 1, i) for i in range(span_count - 1)]
-        up_axial = [(i, i + 1) for i in range(axial_count - 1)]
-        down_axial = [(i + 1, i) for i in range(axial_count - 1)]
+    def swap(values, axis, start):
+        ends = [(i, i + 1) for i in range(start, lax.axis_size(axis) - 1, 2)]
+        return resident(lax.ppermute(values, axis, ends + [(j, i) for i, j in ends]))
+
+    def exchange_rest(even, odd, axial):
         return (
-            lax.ppermute(high, "span", up_span),
-            lax.ppermute(low, "span", down_span),
-            lax.ppermute(axial, "axial", up_axial),
-            lax.ppermute(axial, "axial", down_axial),
+            swap(even, "span", 0),
+            swap(odd, "span", 1),
+            swap(axial, "axial", 0),
+            swap(axial, "axial", 1),
         )
 
     faces = pl.pallas_call(
@@ -370,7 +502,7 @@
         compiler_params=params(),
         name="pitch_faces",
     )(guess)
-    state, low, high, axial = pl.pallas_call(
+    state, even, odd, axial = pl.pallas_call(
         first_pack_kernel,
         out_shape=(kept(wide), kept(edge_shape), kept(edge_shape), kept(axial_shape)),
         in_specs=[ANY],
@@ -380,37 +512,68 @@
         name="first_pack",
     )(guess)
 
-    neighbour_blocks = resident(neighbour_blocks)
-    diag_block = resident(diag_block)
-    right_side = resident(right_side)
-    dissipation = resident(dissipation)
-    omega_volume = resident(omega_volume)
-    pseudo_step = resident(pseudo_step)
+    hbm = functools.partial(pltpu.with_memory_space_constraint, memory_space=pltpu.HBM)
+    groups = GROUPS if planes % GROUPS == 0 else 1
+    sources = (neighbour_blocks, diag_block, right_side, dissipation, omega_volume)
+    near_shape = (2,) + neighbour_blocks.shape[1:]
+    far_shape = (4,) + neighbour_blocks.shape[1:]
     squares = []
     for iteration in range(ITERS):
         halo = resident(exchange_pitch(faces))
-        around = [resident(part) for part in exchange_rest(low, high, axial)]
-        following, error, square = pl.pallas_call(
-            main_kernel,
-            out_shape=(kept(wide), kept(block), kept((span, lanes))),
-            in_specs=[VMEM] * 11,
-            out_specs=(VMEM,) * 3,
-            scratch_shapes=[
-                pltpu.VMEM((rows, span + 2 * PAD, lanes), jnp.float32),
-                pltpu.VMEM(axial_shape, jnp.float32),
-            ],
-            compiler_params=params(),
-            name="main",
-        )(
-            state,
-            *around,
-            neighbour_blocks,
-            diag_block,
-            right_side,
-            dissipation,
-            omega_volume,
-            pseudo_step,
-        )
+        around = exchange_rest(even, odd, axial)
+        far_results = (kept(block), kept(wide), kept((span, lanes)))
+        far_scratch = [
+            pltpu.VMEM((rows, span + 2 * PAD, lanes), jnp.float32),
+            pltpu.VMEM(axial_shape, jnp.float32),
+        ]
+        if iteration == 0:
+            error, *near_constants = pl.pallas_call(
+                near_loading_kernel,
+                out_shape=(
+                    kept(block),
+                    pltpu.VMEM(near_shape, neighbour_blocks.dtype),
+                    *[pltpu.VMEM(c.shape, c.dtype) for c in sources[1:]],
+                ),
+                in_specs=[VMEM] + [ANY] * 5,
+                out_specs=(VMEM,) * 6,
+                scratch_shapes=[pltpu.SemaphoreType.DMA((5, groups))],
+                compiler_params=params(),
+                name="first_near",
+            )(state, *[hbm(c) for c in sources])
+            near_blocks, _, _, dissipation, _ = near_constants
+            error, following, square, far_blocks, pseudo_step = pl.pallas_call(
+                far_loading_kernel,
+                out_shape=far_results
+                + (
+                    pltpu.VMEM(far_shape, neighbour_blocks.dtype),
+                    pltpu.VMEM(pseudo_step.shape, pseudo_step.dtype),
+                ),
+                in_specs=[VMEM] * 5 + [ANY, VMEM, ANY, VMEM],
+                out_specs=(VMEM,) * 5,
+                input_output_aliases={8: 0},
+                scratch_shapes=far_scratch + [pltpu.SemaphoreType.DMA((2, groups))],
+                compiler_params=params(),
+                name="first_far",
+            )(state, *around, hbm(neighbour_blocks), dissipation, hbm(pseudo_step), error)
+        else:
+            error = pl.pallas_call(
+                near_kernel,
+                out_shape=kept(block),
+                in_specs=[VMEM] * 6,
+                out_specs=VMEM,
+                compiler_params=params(),
+                name="near",
+            )(state, *near_constants)
+            error, following, square = pl.pallas_call(
+                far_kernel,
+                out_shape=far_results,
+                in_specs=[VMEM] * 9,
+                out_specs=(VMEM,) * 3,
+                input_output_aliases={8: 0},
+                scratch_shapes=far_scratch,
+                compiler_params=params(),
+                name="far",
+            )(state, *around, far_blocks, dissipation, pseudo_step, error)
         if iteration < ITERS - 1:
             state, faces, square = pl.pallas_call(
                 turn_kernel,
@@ -422,8 +585,8 @@
                 name="pitch_terms",
             )(
                 halo,
-                turn,
-                neighbour_blocks,
+                phase,
+                near_blocks,
                 dissipation,
                 pseudo_step,
                 state,
@@ -432,7 +595,7 @@
                 following,
             )
             squares.append(square)
-            low, high, axial = pl.pallas_call(
+            even, odd, axial = pl.pallas_call(
                 pack_kernel,
                 out_shape=(kept(edge_shape), kept(edge_shape), kept(axial_shape)),
                 in_specs=[VMEM],
@@ -458,8 +621,8 @@
                 name="last_pitch_terms",
             )(
                 halo,
-                turn,
-                neighbour_blocks,
+                phase,
+                near_blocks,
                 dissipation,
                 pseudo_step,
                 state,

time: 67.2 us -> 48.1 us (0.72)
  local copies, waits for them, and re-layouts: 6.85 us -> 0 us
  waiting for transfers between devices: 5.84 us -> 0.03 us
  starting transfers between devices: 22.4 us -> 16.6 us
  blocking collectives: 14.4 us -> 11.7 us
  Pallas kernels: 14.9 us -> 17.4 us
    unnamed x16 -> x0, local copies, waits for them, and re-layouts: 6.85 us -> none
    ppermute x8, starting transfers between devices: 18.8 us -> 13 us  [swap(): lax.ppermute(values, axis, ends + [(j, i) for i, j in ends])]
    ppermute x8, waiting for transfers between devices: 5.83 us -> 0.02 us  [swap(): lax.ppermute(values, axis, ends + [(j, i) for i, j in ends])]
    pallas_call x2 -> x4, Pallas kernels: 10.5 us -> 13.2 us  [the longest x1 4.76 us: body(): pl.pallas_call(far_loading_kernel, out_shape=far_results + (pltpu.VMEM(fa...]
    all_to_all x1, blocking collectives: 14.4 us -> 11.7 us  [body(): shares = lax.all_to_all(share, ('pitch', 'span', 'axial'), 0, 0, tiled=True)]
  transfers between devices with their start and end apart: 10 -> 10, of which waited for: 3 -> 0; matrix products, arithmetic and copies ran while one was open for 0% -> 0% of each run, Pallas kernels for 18% -> 31%
where the time goes in v2:
time: 48.1 us; the launch traced here: 47.7 us
  Pallas kernels  17.4 us (36%)
  starting transfers between devices  16.6 us (35%)
  blocking collectives  11.7 us (24%)
  between operations  1.45 us (3%)
  other arithmetic  0.57 us (1%)
    ppermute x8, starting transfers between devices, swap(): lax.ppermute(values, axis, ends + [(j, i) for i, j in ends])  13 us
    all_to_all x1, blocking collectives, body(): shares = lax.all_to_all(share, ('pitch', 'span', 'axial'), 0, 0, tiled=True)  11.7 us
    pallas_call x1, Pallas kernels, body(): pl.pallas_call(far_loading_kernel, out_shape=far_results + (pltpu.VMEM(fa...  4.76 us
    ppermute x2, starting transfers between devices, exchange_pitch(): return lax.ppermute(faces, 'pitch', up)  3.6 us
    pallas_call x1, Pallas kernels, body(): pl.pallas_call(far_kernel, out_shape=far_results, in_specs=[VMEM] * 9, ou...  3.44 us
    pallas_call x1, Pallas kernels, body(): pl.pallas_call(near_loading_kernel, out_shape=(kept(block), pltpu.VMEM(ne...  3.29 us
    pallas_call x1, Pallas kernels, body(): pl.pallas_call(near_kernel, out_shape=kept(block), in_specs=[VMEM] * 6, o...  1.75 us
    pallas_call x1, Pallas kernels, body(): pl.pallas_call(first_pack_kernel, out_shape=(kept(wide), kept(edge_shape)...  1.42 us
  transfers between devices with their start and end apart: 10, of which 0 were waited for; matrix products, arithmetic and copies ran while one was open for 0% of the time, Pallas kernels for 31%

profile of v2, /device:TPU:0, one launch (start us, length us, event | category | flops | bytes accessed | tf_op | source)
XLA Modules:
  0.0 47.7 jit_solution(5423587018300052119)
XLA Ops:
  0.6 1.0 %pitch_faces.1 = f32[2,12,2,16,128]{4,3,2,1,0:T(8,128)S(1)} custom-call(f32[12,8,16,128]{3,2,1,0:T(8,128)} %bitcast.3), custom_call_target="tpu_custom_call" | custom-call | tf_op jit(solution)/shard_map/pitch_faces/pallas_call | solution.py:496
  1.7 3.0 %collective-permute-start = (f32[2,12,2,16,128]{4,3,2,1,0:T(8,128)S(1)}, f32[2,12,2,16,128]{4,3,2,1,0:T(8,128)S(1)}, u32[]{:S(2)}, u32[]{:S(2)}) collective-permute-start(f32[2,12,2,16,128]{4,3,2,1,0:T(8,128)S(1)} %pitch_faces.1), channel_id=1, source_target_pairs={{0,16},{16,0},{1,17},{17,1},{2,18},{18,2},{3,19},{19,3},{4,20},{20... | collective-permute-start | bytes 1179656 | tf_op jit(solution)/shard_map/ppermute | solution.py:479
  4.7 1.4 %first_pack.1 = (f32[12,12,16,128]{3,2,1,0:T(8,128)S(1)}, f32[12,8,2,128]{3,2,1,0:T(2,128)S(1)}, f32[12,8,2,128]{3,2,1,0:T(2,128)S(1)}, f32[3,16,128]{2,1,0:T(8,128)S(1)}) custom-call(f32[12,8,16,128]{3,2,1,0:T(8,128)} %bitcast.4), custom_call_target="tpu_custom_call" | custom-call | tf_op jit(solution)/shard_map/first_pack/pallas_call | solution.py:505
  6.1 1.6 %collective-permute-start.1 = (f32[12,8,2,128]{3,2,1,0:T(2,128)S(1)}, f32[12,8,2,128]{3,2,1,0:T(2,128)S(1)}, u32[]{:S(2)}, u32[]{:S(2)}) collective-permute-start(f32[12,8,2,128]{3,2,1,0:T(2,128)S(1)} %get-tuple-element.31), channel_id=1, source_target_pairs={{0,4},{8,12},{4,0},{12,8},{1,5},{9,13},{5,1},{13,9},{2,6},{10,14},... | collective-permute-start | bytes 294920 | tf_op jit(solution)/shard_map/ppermute | solution.py:486
  7.8 0.7 %collective-permute-start.2 = (f32[12,8,2,128]{3,2,1,0:T(2,128)S(1)}, f32[12,8,2,128]{3,2,1,0:T(2,128)S(1)}, u32[]{:S(2)}, u32[]{:S(2)}) collective-permute-start(f32[12,8,2,128]{3,2,1,0:T(2,128)S(1)} %get-tuple-element.32), channel_id=1, source_target_pairs={{4,8},{8,4},{5,9},{9,5},{6,10},{10,6},{7,11},{11,7},{20,24},{24,20... | collective-permute-start | bytes 294920 | tf_op jit(solution)/shard_map/ppermute | solution.py:486
  8.4 0.7 %collective-permute-start.4 = (f32[3,16,128]{2,1,0:T(8,128)S(1)}, f32[3,16,128]{2,1,0:T(8,128)S(1)}, u32[]{:S(2)}, u32[]{:S(2)}) collective-permute-start(f32[3,16,128]{2,1,0:T(8,128)S(1)} %get-tuple-element.33), channel_id=1, source_target_pairs={{1,2},{2,1},{5,6},{6,5},{9,10},{10,9},{13,14},{14,13},{17,18},{18,... | collective-permute-start | bytes 73736 | tf_op jit(solution)/shard_map/ppermute | solution.py:486
  9.1 2.9 %collective-permute-start.3 = (f32[3,16,128]{2,1,0:T(8,128)S(1)}, f32[3,16,128]{2,1,0:T(8,128)S(1)}, u32[]{:S(2)}, u32[]{:S(2)}) collective-permute-start(f32[3,16,128]{2,1,0:T(8,128)S(1)} %get-tuple-element.33), channel_id=1, source_target_pairs={{0,1},{2,3},{1,0},{3,2},{4,5},{6,7},{5,4},{7,6},{8,9},{10,11},{9,8... | collective-permute-start | bytes 73736 | tf_op jit(solution)/shard_map/ppermute | solution.py:486
  12.7 3.3 %first_near.1 = (f32[12,8,16,128]{3,2,1,0:T(8,128)S(1)}, bf16[2,6,6,8,16,128]{5,4,3,2,1,0:T(8,128)(2,1)S(1)}, bf16[6,6,8,16,128]{4,3,2,1,0:T(8,128)(2,1)S(1)}, f...) custom-call(f32[12,12,16,128]{3,2,1,0:T(8,128)S(1)} %get-tuple-element.28.wide_ref, ...), custom_call_target="tpu_custom_call" | custom-call | tf_op jit(solution)/shard_map/first_near/pallas_call | solution.py:530
  16.0 0.0 collective-permute-done.4.axial_odd_ref
  16.0 0.0 collective-permute-done.1.span_even_ref
  16.0 4.8 %first_far.1 = (f32[12,8,16,128]{3,2,1,0:T(8,128)S(1)}, f32[12,12,16,128]{3,2,1,0:T(8,128)S(1)}, f32[16,128]{1,0:T(8,128)S(1)}, bf16[4,6,6,8,16,128]{5,4,3,2,1,0:T(8,128)(2,1)S(1)}, f32[8,16,128]{2,1,0:T(8,128)S(1)}) custom-call(f32[12,12,16,128]{3,2,1,0:T(8,128)S(1)} %get-tuple-element.28.wide_ref, ...), custom_call_target="tpu_custom_call", output_to_operand_aliasing={{0}: (8, {})} | custom-call | tf_op jit(solution)/shard_map/first_far/pallas_call | solution.py:544
  20.8 0.3 pitch_terms.1
  21.1 0.6 %collective-permute-start.5 = (f32[2,12,2,16,128]{4,3,2,1,0:T(8,128)S(1)}, f32[2,12,2,16,128]{4,3,2,1,0:T(8,128)S(1)}, u32[]{:S(2)}, u32[]{:S(2)}) collective-permute-start(f32[2,12,2,16,128]{4,3,2,1,0:T(8,128)S(1)} %get-tuple-element.39), channel_id=1, source_target_pairs={{0,16},{16,0},{1,17},{17,1},{2,18},{18,2},{3,19},{19,3},{4,20},{20... | collective-permute-start | bytes 1179656 | tf_op jit(solution)/shard_map/ppermute | solution.py:479
  21.7 0.3 pack.1
  21.9 4.5 %collective-permute-start.6 = (f32[12,8,2,128]{3,2,1,0:T(2,128)S(1)}, f32[12,8,2,128]{3,2,1,0:T(2,128)S(1)}, u32[]{:S(2)}, u32[]{:S(2)}) collective-permute-start(f32[12,8,2,128]{3,2,1,0:T(2,128)S(1)} %get-tuple-element.41), channel_id=1, source_target_pairs={{0,4},{8,12},{4,0},{12,8},{1,5},{9,13},{5,1},{13,9},{2,6},{10,14},... | collective-permute-start | bytes 294920 | tf_op jit(solution)/shard_map/ppermute | solution.py:486
  26.4 0.7 %collective-permute-start.7 = (f32[12,8,2,128]{3,2,1,0:T(2,128)S(1)}, f32[12,8,2,128]{3,2,1,0:T(2,128)S(1)}, u32[]{:S(2)}, u32[]{:S(2)}) collective-permute-start(f32[12,8,2,128]{3,2,1,0:T(2,128)S(1)} %get-tuple-element.42), channel_id=1, source_target_pairs={{4,8},{8,4},{5,9},{9,5},{6,10},{10,6},{7,11},{11,7},{20,24},{24,20... | collective-permute-start | bytes 294920 | tf_op jit(solution)/shard_map/ppermute | solution.py:486
  27.1 0.7 %collective-permute-start.9 = (f32[3,16,128]{2,1,0:T(8,128)S(1)}, f32[3,16,128]{2,1,0:T(8,128)S(1)}, u32[]{:S(2)}, u32[]{:S(2)}) collective-permute-start(f32[3,16,128]{2,1,0:T(8,128)S(1)} %get-tuple-element.43), channel_id=1, source_target_pairs={{1,2},{2,1},{5,6},{6,5},{9,10},{10,9},{13,14},{14,13},{17,18},{18,... | collective-permute-start | bytes 73736 | tf_op jit(solution)/shard_map/ppermute | solution.py:486
  27.7 1.3 %collective-permute-start.8 = (f32[3,16,128]{2,1,0:T(8,128)S(1)}, f32[3,16,128]{2,1,0:T(8,128)S(1)}, u32[]{:S(2)}, u32[]{:S(2)}) collective-permute-start(f32[3,16,128]{2,1,0:T(8,128)S(1)} %get-tuple-element.43), channel_id=1, source_target_pairs={{0,1},{2,3},{1,0},{3,2},{4,5},{6,7},{5,4},{7,6},{8,9},{10,11},{9,8... | collective-permute-start | bytes 73736 | tf_op jit(solution)/shard_map/ppermute | solution.py:486
  29.1 1.7 %near.1.refs_8_ = f32[12,8,16,128]{3,2,1,0:T(8,128)S(1)} custom-call(f32[12,12,16,128]{3,2,1,0:T(8,128)S(1)} %get-tuple-element.40.wide_ref.refs_0_, bf16[2,6,6,8,16,128]{5,4,3,2,1,0:T(8,128)(2,1)S(1)} %get-tuple-element.29.neighbour_ref.refs_1_, bf16[6,6,8,16,128]{4,3,2,1,0:T(8,128)(2,1)S(1)} %get-tuple-element.45.refs_2_, ...), custom_call_target="tpu_custom_call" | custom-call | tf_op jit(solution)/shard_map/near/pallas_call | solution.py:559
  30.9 3.4 %far.1 = (f32[12,8,16,128]{3,2,1,0:T(8,128)S(1)}, f32[12,12,16,128]{3,2,1,0:T(8,128)S(1)}, f32[16,128]{1,0:T(8,128)S(1)}) custom-call(f32[12,12,16,128]{3,2,1,0:T(8,128)S(1)} %get-tuple-element.40.wide_ref.refs_0_, f32[12,8,2,128]{3,2,1,0:T(2,128)S(1)} %collective-permute-done.6.refs_1_, ...), custom_call_target="tpu_custom_call", output_to_operand_aliasing={{0}: (8, {})} | custom-call | tf_op jit(solution)/shard_map/far/pallas_call | solution.py:567
  34.3 1.1 %last_pitch_terms.1 = (f32[12,8,16,128]{3,2,1,0:T(8,128)}, f32[32,1,128]{2,1,0:T(1,128)S(1)}) custom-call(f32[2,12,2,16,128]{4,3,2,1,0:T(8,128)S(1)} %collective-permute-done.5.halo_ref, f32[1]{0:T(128)S(6)} %copy.16.phase_ref, bf16[2,6,6,8,16,128]{5,4,3,2,1,0:T(8,128)(2,1)S(1)} %get-tuple-element.29.neighbour_ref.refs_1_, ...), custom_call_target="tpu_custom_call" | custom-call | tf_op jit(solution)/shard_map/last_pitch_terms/pallas_call | solution.py:607
  35.4 11.7 %all_to_all.5 = f32[32,1,128]{2,1,0:T(1,128)S(1)} all-to-all(f32[32,1,128]{2,1,0:T(1,128)S(1)} %get-tuple-element.53), channel_id=1, replica_groups=mesh['pitch'=2,'span'=4,'axial'=4] {'pitch','span','axial'}, dimensions={0} | all-to-all | bytes 32768 | tf_op jit(solution)/shard_map/all_to_all | solution.py:634
  47.2 0.1 reduce_sum.9
  47.2 0.5 %multiply_sqrt_fusion = f32[2]{0:T(128)} fusion(f32[128]{0:T(128)S(1)} %reduce_sum.9), kind=kLoop, calls=%fused_computation | loop fusion | flops 2 | bytes 16 | tf_op jit(solution)/shard_map/sqrt | solution.py:637
  (8 shorter events, 0.0 us)
Async XLA Ops:
  1.7 19.1 %collective-permute-start = (f32[2,12,2,16,128]{4,3,2,1,0:T(8,128)S(1)}, f32[2,12,2,16,128]{4,3,2,1,0:T(8,128)S(1)}, u32[]{:S(2)}, u32[]{:S(2)}) collective-permute-start(f32[2,12,2,16,128]{4,3,2,1,0:T(8,128)S(1)} %pitch_faces.1), channel_id=1, source_target_pairs={{0,16},{16,0},{1,17},{17,1},{2,18},{18,2},{3,19},{19,3},{4,20},{20... | collective-permute-start | bytes 1179656 | tf_op jit(solution)/shard_map/ppermute | solution.py:479
  6.1 9.9 %collective-permute-start.1 = (f32[12,8,2,128]{3,2,1,0:T(2,128)S(1)}, f32[12,8,2,128]{3,2,1,0:T(2,128)S(1)}, u32[]{:S(2)}, u32[]{:S(2)}) collective-permute-start(f32[12,8,2,128]{3,2,1,0:T(2,128)S(1)} %get-tuple-element.31), channel_id=1, source_target_pairs={{0,4},{8,12},{4,0},{12,8},{1,5},{9,13},{5,1},{13,9},{2,6},{10,14},... | collective-permute-start | bytes 294920 | tf_op jit(solution)/shard_map/ppermute | solution.py:486
  7.8 8.2 %collective-permute-start.2 = (f32[12,8,2,128]{3,2,1,0:T(2,128)S(1)}, f32[12,8,2,128]{3,2,1,0:T(2,128)S(1)}, u32[]{:S(2)}, u32[]{:S(2)}) collective-permute-start(f32[12,8,2,128]{3,2,1,0:T(2,128)S(1)} %get-tuple-element.32), channel_id=1, source_target_pairs={{4,8},{8,4},{5,9},{9,5},{6,10},{10,6},{7,11},{11,7},{20,24},{24,20... | collective-permute-start | bytes 294920 | tf_op jit(solution)/shard_map/ppermute | solution.py:486
  8.4 7.5 %collective-permute-start.4 = (f32[3,16,128]{2,1,0:T(8,128)S(1)}, f32[3,16,128]{2,1,0:T(8,128)S(1)}, u32[]{:S(2)}, u32[]{:S(2)}) collective-permute-start(f32[3,16,128]{2,1,0:T(8,128)S(1)} %get-tuple-element.33), channel_id=1, source_target_pairs={{1,2},{2,1},{5,6},{6,5},{9,10},{10,9},{13,14},{14,13},{17,18},{18,... | collective-permute-start | bytes 73736 | tf_op jit(solution)/shard_map/ppermute | solution.py:486
  9.1 6.9 %collective-permute-start.3 = (f32[3,16,128]{2,1,0:T(8,128)S(1)}, f32[3,16,128]{2,1,0:T(8,128)S(1)}, u32[]{:S(2)}, u32[]{:S(2)}) collective-permute-start(f32[3,16,128]{2,1,0:T(8,128)S(1)} %get-tuple-element.33), channel_id=1, source_target_pairs={{0,1},{2,3},{1,0},{3,2},{4,5},{6,7},{5,4},{7,6},{8,9},{10,11},{9,8... | collective-permute-start | bytes 73736 | tf_op jit(solution)/shard_map/ppermute | solution.py:486
  21.1 13.2 %collective-permute-start.5 = (f32[2,12,2,16,128]{4,3,2,1,0:T(8,128)S(1)}, f32[2,12,2,16,128]{4,3,2,1,0:T(8,128)S(1)}, u32[]{:S(2)}, u32[]{:S(2)}) collective-permute-start(f32[2,12,2,16,128]{4,3,2,1,0:T(8,128)S(1)} %get-tuple-element.39), channel_id=1, source_target_pairs={{0,16},{16,0},{1,17},{17,1},{2,18},{18,2},{3,19},{19,3},{4,20},{20... | collective-permute-start | bytes 1179656 | tf_op jit(solution)/shard_map/ppermute | solution.py:479
  21.9 8.9 %collective-permute-start.6 = (f32[12,8,2,128]{3,2,1,0:T(2,128)S(1)}, f32[12,8,2,128]{3,2,1,0:T(2,128)S(1)}, u32[]{:S(2)}, u32[]{:S(2)}) collective-permute-start(f32[12,8,2,128]{3,2,1,0:T(2,128)S(1)} %get-tuple-element.41), channel_id=1, source_target_pairs={{0,4},{8,12},{4,0},{12,8},{1,5},{9,13},{5,1},{13,9},{2,6},{10,14},... | collective-permute-start | bytes 294920 | tf_op jit(solution)/shard_map/ppermute | solution.py:486
  26.4 4.5 %collective-permute-start.7 = (f32[12,8,2,128]{3,2,1,0:T(2,128)S(1)}, f32[12,8,2,128]{3,2,1,0:T(2,128)S(1)}, u32[]{:S(2)}, u32[]{:S(2)}) collective-permute-start(f32[12,8,2,128]{3,2,1,0:T(2,128)S(1)} %get-tuple-element.42), channel_id=1, source_target_pairs={{4,8},{8,4},{5,9},{9,5},{6,10},{10,6},{7,11},{11,7},{20,24},{24,20... | collective-permute-start | bytes 294920 | tf_op jit(solution)/shard_map/ppermute | solution.py:486
  27.1 3.8 %collective-permute-start.9 = (f32[3,16,128]{2,1,0:T(8,128)S(1)}, f32[3,16,128]{2,1,0:T(8,128)S(1)}, u32[]{:S(2)}, u32[]{:S(2)}) collective-permute-start(f32[3,16,128]{2,1,0:T(8,128)S(1)} %get-tuple-element.43), channel_id=1, source_target_pairs={{1,2},{2,1},{5,6},{6,5},{9,10},{10,9},{13,14},{14,13},{17,18},{18,... | collective-permute-start | bytes 73736 | tf_op jit(solution)/shard_map/ppermute | solution.py:486
  27.7 3.1 %collective-permute-start.8 = (f32[3,16,128]{2,1,0:T(8,128)S(1)}, f32[3,16,128]{2,1,0:T(8,128)S(1)}, u32[]{:S(2)}, u32[]{:S(2)}) collective-permute-start(f32[3,16,128]{2,1,0:T(8,128)S(1)} %get-tuple-element.43), channel_id=1, source_target_pairs={{0,1},{2,3},{1,0},{3,2},{4,5},{6,7},{5,4},{7,6},{8,9},{10,11},{9,8... | collective-permute-start | bytes 73736 | tf_op jit(solution)/shard_map/ppermute | solution.py:486

commit v3 on v2

v3 whole, which is shorter than its diff:
```python
import functools

import jax
import jax.numpy as jnp
from jax import lax
from jax.experimental import pallas as pl
from jax.experimental.pallas import tpu as pltpu
from jax.sharding import PartitionSpec as P

ITERS = 2
WIDTH = 2
PAD = 8
GROUPS = 4
VMEM = pl.BlockSpec(memory_space=pltpu.VMEM)
SMEM = pl.BlockSpec(memory_space=pltpu.SMEM)
ANY = pl.BlockSpec(memory_space=pl.ANY)
VMEM_LIMIT = 4 * 1024 * 1024


def resident(values):
    return pltpu.with_memory_space_constraint(values, pltpu.VMEM)


def outside(values):
    return pltpu.with_memory_space_constraint(values, pltpu.HBM)


def kept(shape, dtype=jnp.float32):
    return pltpu.VMEM(shape, dtype)


def call(kernel, name, out_shape, in_specs, scratch_shapes=(), aliases=None):
    return pl.pallas_call(
        kernel,
        out_shape=out_shape,
        in_specs=in_specs,
        out_specs=(VMEM,) * len(out_shape),
        scratch_shapes=scratch_shapes,
        input_output_aliases=aliases or {},
        compiler_params=pltpu.CompilerParams(vmem_limit_bytes=VMEM_LIMIT),
        name=name,
    )


def lane_place(k, planes, lanes):
    per_group = (lanes // (2 * WIDTH)) // planes
    return k // per_group, (k % per_group) * planes


def lane_groups(rows, planes, lanes):
    return lane_place(rows - 1, planes, lanes)[0] + 1


def pack_faces(wide_ref, even_ref, odd_ref, axial_ref):
    rows, wide, span, lanes = wide_ref.shape
    planes = wide - 2 * WIDTH
    span_even = lax.axis_index("span") % 2 == 0
    lane = lax.broadcasted_iota(jnp.int32, (span, lanes), 1)
    packed = None
    for k in range(rows):
        group, base = lane_place(k, planes, lanes)
        for p in range(planes):
            cells = wide_ref[k, p + WIDTH]
            low = cells[:WIDTH]
            high = cells[span - WIDTH :]
            even_ref[k, p] = jnp.where(span_even, high, low)
            odd_ref[k, p] = jnp.where(span_even, low, high)
            place = base + p
            moved = pltpu.roll(cells, (2 * WIDTH * place + WIDTH) % lanes, axis=1)
            if place == 0:
                packed = moved
            else:
                packed = jnp.where(lane >= 2 * WIDTH * place, moved, packed)
        if k == rows - 1 or lane_place(k + 1, planes, lanes)[0] != group:
            axial_ref[group] = packed


class Loads:
    def __init__(self, pairs, sems, first, size):
        self.pairs = pairs
        self.sems = sems
        self.first = first
        self.size = size

    def copies(self, group):
        planes = pl.ds(self.first + group * self.size, self.size)
        return [
            pltpu.make_async_copy(
                source.at[(slice(None),) * dim + (planes,)],
                target.at[(slice(None),) * dim + (planes,)],
                self.sems.at[at, group],
            )
            for at, (source, target, dim) in enumerate(self.pairs)
        ]

    def start(self):
        for group in range(self.sems.shape[1]):
            for copy in self.copies(group):
                copy.start()

    def ready(self, p):
        @pl.when(jnp.logical_and(p >= self.first, (p - self.first) % self.size == 0))
        def _():
            for copy in self.copies((p - self.first) // self.size):
                copy.wait()

    def wait(self):
        for group in range(self.sems.shape[1]):
            for copy in self.copies(group):
                copy.wait()


def open_kernel(
    guess_hbm,
    right_hbm,
    dissipation_hbm,
    omega_hbm,
    step_hbm,
    diag_hbm,
    wide_ref,
    faces_ref,
    even_ref,
    odd_ref,
    axial_ref,
    right_ref,
    dissipation_ref,
    omega_ref,
    step_ref,
    diag_ref,
    sems,
):
    rows, wide, span, lanes = wide_ref.shape
    planes = wide - 2 * WIDTH
    pairs = (
        (guess_hbm, wide_ref.at[:, WIDTH : WIDTH + planes]),
        (dissipation_hbm, dissipation_ref),
        (omega_hbm, omega_ref),
        (step_hbm, step_ref),
        (right_hbm, right_ref),
        (diag_hbm, diag_ref),
    )
    copies = [pltpu.make_async_copy(*pair, sems.at[at]) for at, pair in enumerate(pairs)]
    for copy in copies:
        copy.start()
    for k in range(rows):
        for p in (0, 1, wide - 2, wide - 1):
            wide_ref[k, p] = jnp.zeros((span, lanes), jnp.float32)
    copies[0].wait()
    for k in range(rows):
        for at in range(WIDTH):
            faces_ref[0, k, at] = wide_ref[k, planes + at]
            faces_ref[1, k, at] = wide_ref[k, WIDTH + at]
    pack_faces(wide_ref, even_ref, odd_ref, axial_ref)
    for copy in copies[1:]:
        copy.wait()


def near_loading_kernel(
    wide_ref,
    neighbour_hbm,
    diag_ref,
    right_ref,
    dissipation_ref,
    omega_ref,
    error_ref,
    lower_ref,
    upper_ref,
    spaced_ref,
    neighbour_ref,
    far_ref,
    near_sems,
    far_sems,
):
    planes = error_ref.shape[1]
    groups = near_sems.shape[1]
    loads = Loads([(neighbour_hbm.at[0:2], neighbour_ref, 3)], near_sems, 0, planes // groups)
    later = Loads([(neighbour_hbm.at[2:6], far_ref, 3)], far_sems, 0, planes // 2)
    loads.start()
    later.start()
    near_sweep(
        wide_ref,
        neighbour_ref,
        diag_ref,
        right_ref,
        dissipation_ref,
        omega_ref,
        error_ref,
        lower_ref,
        upper_ref,
        spaced_ref,
        loads,
    )
    later.wait()


def near_kernel(*refs):
    near_sweep(*refs, None)


def near_sweep(
    wide_ref,
    neighbour_ref,
    diag_ref,
    right_ref,
    dissipation_ref,
    omega_ref,
    error_ref,
    lower_ref,
    upper_ref,
    spaced_ref,
    loads,
):
    rows, planes, span, lanes = error_ref.shape
    nv = rows // 2
    lane = lax.broadcasted_iota(jnp.int32, (span, lanes), 1)
    edge = jnp.logical_or(lane < WIDTH, lane >= lanes - WIDTH)

    def plane(p, carry):
        if loads is not None:
            loads.ready(p)
        omega = omega_ref[p]
        spread = dissipation_ref[0, p]
        total = []
        for k in range(rows):
            other = wide_ref[(k + nv) % rows, p + WIDTH]
            turned = -omega * other if k < nv else omega * other
            far = wide_ref[k, p] + wide_ref[k, p + 2 * WIDTH]
            total.append((turned - right_ref[k, p]) + spread * far)
        for j in range(nv):
            for at, blocks in (
                (2, lambda i: diag_ref[i, j, p]),
                (1, lambda i: neighbour_ref[0, i, j, p]),
                (3, lambda i: neighbour_ref[1, i, j, p]),
            ):
                real = wide_ref[j, p + at]
                imag = wide_ref[nv + j, p + at]
                for i in range(nv):
                    block = blocks(i).astype(jnp.float32)
                    total[i] = total[i] + block * real
                    total[nv + i] = total[nv + i] + block * imag
            for k in (j, nv + j):
                cells = wide_ref[k, p + WIDTH]
                lower_ref[k, p] = pltpu.roll(cells, 1, axis=1)
                upper_ref[k, p] = pltpu.roll(cells, lanes - 1, axis=1)
                spaced = pltpu.roll(cells, 2, axis=1) + pltpu.roll(cells, lanes - 2, axis=1)
                low = pltpu.roll(cells, 2, axis=1)
                high = pltpu.roll(cells, lanes - 2, axis=1)
                spaced_ref[k, p] = jnp.where(
                    edge, jnp.where(lane < WIDTH, high, low), spaced
                )
        for k in range(rows):
            error_ref[k, p] = total[k]
        return carry

    lax.fori_loop(0, planes, plane, 0)


def far_loading_kernel(
    wide_in_ref,
    error_in_ref,
    neighbour_in_ref,
    neighbour_hbm,
    span_even_ref,
    span_odd_ref,
    axial_even_ref,
    axial_odd_ref,
    lower_ref,
    upper_ref,
    spaced_ref,
    dissipation_ref,
    step_ref,
    wide_ref,
    error_ref,
    neighbour_ref,
    square_ref,
    span_buf,
    axial_buf,
    sems,
):
    planes = error_ref.shape[1]
    half = planes // 2
    loads = Loads(
        [(neighbour_hbm.at[2:6], neighbour_ref, 3)], sems, half, (planes - half) // sems.shape[1]
    )
    loads.start()
    far_sweep(
        neighbour_ref,
        span_even_ref,
        span_odd_ref,
        axial_even_ref,
        axial_odd_ref,
        lower_ref,
        upper_ref,
        spaced_ref,
        dissipation_ref,
        step_ref,
        wide_ref,
        error_ref,
        square_ref,
        span_buf,
        axial_buf,
        loads,
    )


def far_kernel(wide_in_ref, error_in_ref, *refs):
    far_sweep(*refs, None)


def far_sweep(
    neighbour_ref,
    span_even_ref,
    span_odd_ref,
    axial_even_ref,
    axial_odd_ref,
    lower_ref,
    upper_ref,
    spaced_ref,
    dissipation_ref,
    step_ref,
    wide_ref,
    error_ref,
    square_ref,
    span_buf,
    axial_buf,
    loads,
):
    rows, planes, span, lanes = error_ref.shape
    nv = rows // 2
    span_even = lax.axis_index("span") % 2 == 0
    axial_even = lax.axis_index("axial") % 2 == 0
    lane = lax.broadcasted_iota(jnp.int32, (span, lanes), 1)
    edge = jnp.logical_or(lane < WIDTH, lane >= lanes - WIDTH)
    from_below = lane % (2 * WIDTH) >= WIDTH
    for group in range(axial_buf.shape[0]):
        at_even = axial_even_ref[group]
        at_odd = axial_odd_ref[group]
        below = pltpu.roll(jnp.where(axial_even, at_odd, at_even), WIDTH, axis=1)
        above = pltpu.roll(jnp.where(axial_even, at_even, at_odd), lanes - WIDTH, axis=1)
        axial_buf[group] = jnp.where(from_below, below, above)
    square_ref[...] = jnp.zeros_like(square_ref)

    def plane(p, carry):
        if loads is not None:
            loads.ready(p)
        for k in range(rows):
            at_even = span_even_ref[k, p]
            at_odd = span_odd_ref[k, p]
            span_buf[k, PAD - WIDTH : PAD] = jnp.where(span_even, at_odd, at_even)
            span_buf[k, PAD : PAD + span] = wide_ref[k, p + WIDTH]
            span_buf[k, PAD + span : PAD + span + WIDTH] = jnp.where(span_even, at_even, at_odd)
        total = [error_ref[k, p] for k in range(rows)]
        spread_span = dissipation_ref[1, p]
        spread_axial = dissipation_ref[2, p]

        def column(direction, j, real, imag):
            for i in range(nv):
                block = neighbour_ref[direction, i, j, p].astype(jnp.float32)
                total[i] = total[i] + block * real
                total[nv + i] = total[nv + i] + block * imag

        for j in range(nv):
            pair = (j, nv + j)
            column(0, j, *[span_buf[k, PAD - 1 : PAD - 1 + span] for k in pair])
            column(1, j, *[span_buf[k, PAD + 1 : PAD + 1 + span] for k in pair])
            lower = []
            upper = []
            for k in pair:
                group, base = lane_place(k, planes, lanes)
                packed = axial_buf[group]
                shift = lanes - WIDTH - 2 * WIDTH * base - 2 * WIDTH * p
                below = pltpu.roll(packed, shift - 1, axis=1)
                above = pltpu.roll(packed, shift + 1, axis=1)
                beyond = pltpu.roll(packed, shift, axis=1)
                lower.append(jnp.where(lane < 1, below, lower_ref[k, p]))
                upper.append(jnp.where(lane >= lanes - 1, above, upper_ref[k, p]))
                far = spaced_ref[k, p] + jnp.where(edge, beyond, 0.0)
                total[k] = total[k] + spread_axial * far
                far = (
                    span_buf[k, PAD - 2 : PAD - 2 + span] + span_buf[k, PAD + 2 : PAD + 2 + span]
                )
                total[k] = total[k] + spread_span * far
            column(2, j, *lower)
            column(3, j, *upper)
        step = step_ref[p]
        square = None
        for k in range(rows):
            error = total[k]
            error_ref[k, p] = error
            wide_ref[k, p + WIDTH] = wide_ref[k, p + WIDTH] - step * error
            square = error * error if square is None else square + error * error
        inner = jnp.logical_and(p >= WIDTH, p < planes - WIDTH)
        square_ref[...] += jnp.where(inner, square, 0.0)
        return carry

    lax.fori_loop(0, planes, plane, 0)


def pitch_terms(halo_ref, phase_ref, neighbour_ref, dissipation_ref, error_ref, store):
    rows, planes, span, lanes = error_ref.shape
    nv = rows // 2
    pitch_at = lax.axis_index("pitch")
    angle = jnp.full((span, lanes), phase_ref[0], jnp.float32)
    cosine_end = jnp.cos(angle)
    sine_end = jnp.sin(angle)
    for side in range(2):
        at_end = pitch_at == (0 if side == 0 else lax.axis_size("pitch") - 1)
        cosine = jnp.where(at_end, cosine_end, 1.0)
        sine_part = jnp.where(at_end, -sine_end if side == 0 else sine_end, 0.0)
        near_at, far_at = (1, 0) if side == 0 else (0, 1)
        edge, inside = (0, 1) if side == 0 else (planes - 1, planes - 2)

        def turned(j, at):
            real = halo_ref[side, j, at]
            imag = halo_ref[side, nv + j, at]
            return (cosine * real - sine_part * imag, sine_part * real + cosine * imag)

        total = [None] * rows

        def add(k, value):
            total[k] = value if total[k] is None else total[k] + value

        spread_edge = dissipation_ref[0, edge]
        spread_inside = dissipation_ref[0, inside]
        for j in range(nv):
            near = turned(j, near_at)
            far = turned(j, far_at)
            for c in range(2):
                k = c * nv + j
                add(k, spread_edge * far[c])
                store(k, inside, spread_inside * near[c])
            for i in range(nv):
                block = neighbour_ref[side, i, j, edge].astype(jnp.float32)
                for c in range(2):
                    add(c * nv + i, block * near[c])
        for k in range(rows):
            store(k, edge, total[k])


def turn_kernel(
    wide_in_ref,
    halo_ref,
    phase_ref,
    neighbour_ref,
    dissipation_ref,
    step_ref,
    error_ref,
    square_in_ref,
    wide_ref,
    faces_ref,
    even_ref,
    odd_ref,
    axial_ref,
    square_ref,
):
    planes = error_ref.shape[1]
    square_ref[...] = square_in_ref[...]

    def store(k, p, change):
        value = wide_ref[k, p + WIDTH] - step_ref[p] * change
        wide_ref[k, p + WIDTH] = value
        if p < WIDTH:
            faces_ref[1, k, p] = value
        else:
            faces_ref[0, k, p - (planes - WIDTH)] = value
        error = error_ref[k, p] + change
        square_ref[...] += error * error

    pitch_terms(halo_ref, phase_ref, neighbour_ref, dissipation_ref, error_ref, store)
    pack_faces(wide_ref, even_ref, odd_ref, axial_ref)


def last_kernel(
    wide_ref,
    halo_ref,
    phase_ref,
    neighbour_ref,
    dissipation_ref,
    step_ref,
    error_ref,
    square_in_ref,
    first_square_ref,
    out_ref,
    share_ref,
    square_buf,
):
    rows, planes, _, _ = error_ref.shape
    square_buf[...] = square_in_ref[...]
    for k in range(rows):
        for p in range(WIDTH, planes - WIDTH):
            out_ref[k, p] = wide_ref[k, p + WIDTH]

    def store(k, p, change):
        out_ref[k, p] = wide_ref[k, p + WIDTH] - step_ref[p] * change
        error = error_ref[k, p] + change
        square_buf[...] += error * error

    pitch_terms(halo_ref, phase_ref, neighbour_ref, dissipation_ref, error_ref, store)
    first = jnp.sum(first_square_ref[...], axis=(0, 1), keepdims=True)
    second = jnp.sum(square_buf[...], axis=(0, 1), keepdims=True)
    lane = lax.broadcasted_iota(jnp.int32, share_ref.shape, 2)
    share_ref[...] = jnp.where(
        lane == 0, first.reshape(1, 1, 1), jnp.where(lane == 1, second.reshape(1, 1, 1), 0.0)
    )


def body(
    guess, right_side, diag_block, neighbour_blocks, dissipation, omega_volume, pseudo_step, phase
):
    parts, nv, planes, span, lanes = guess.shape
    rows = parts * nv
    pitch_count = lax.axis_size("pitch")
    devices = pitch_count * lax.axis_size("span") * lax.axis_size("axial")
    wide = (rows, planes + 2 * WIDTH, span, lanes)
    block = (rows, planes, span, lanes)
    tile = (span, lanes)
    face_shapes = (
        kept((2, rows, WIDTH, span, lanes)),
        kept((rows, planes, WIDTH, lanes)),
        kept((rows, planes, WIDTH, lanes)),
        kept((lane_groups(rows, planes, lanes), span, lanes)),
    )
    groups = GROUPS if planes % GROUPS == 0 else 1
    half_groups = 2 if planes % 4 == 0 else 1
    dma = pltpu.SemaphoreType.DMA

    def exchange_pitch(faces):
        up = [(i, (i + 1) % pitch_count) for i in range(pitch_count)]
        down = [(j, i) for i, j in up]
        if sorted(up) == sorted(down):
            return lax.ppermute(faces, "pitch", up)
        return jnp.stack(
            [lax.ppermute(faces[0], "pitch", up), lax.ppermute(faces[1], "pitch", down)]
        )

    def swap(values, axis, start):
        ends = [(i, i + 1) for i in range(start, lax.axis_size(axis) - 1, 2)]
        return resident(lax.ppermute(values, axis, ends + [(j, i) for i, j in ends]))

    def exchange_rest(even, odd, axial):
        return (
            swap(even, "span", 0),
            swap(odd, "span", 1),
            swap(axial, "axial", 0),
            swap(axial, "axial", 1),
        )

    neighbour_blocks = outside(neighbour_blocks)
    sources = (right_side.reshape(block), dissipation, omega_volume, pseudo_step, diag_block)
    state, faces, even, odd, axial, right, dissipation, omega, step, diag = call(
        open_kernel,
        "open",
        (kept(wide),)
        + face_shapes
        + tuple(kept(c.shape, c.dtype) for c in sources),
        [ANY] * 6,
        [dma((6,))],
    )(outside(guess.reshape(block)), *[outside(c) for c in sources])

    squares = []
    for iteration in range(ITERS):
        halo = resident(exchange_pitch(faces))
        around = exchange_rest(even, odd, axial)
        near_results = (kept(block),) * 4
        far_results = (kept(wide), kept(block))
        far_scratch = [pltpu.VMEM((rows, span + 2 * PAD, lanes), jnp.float32)] + [
            pltpu.VMEM(face_shapes[3].shape, jnp.float32)
        ]
        if iteration == 0:
            near_blocks = kept((2,) + neighbour_blocks.shape[1:], neighbour_blocks.dtype)
            far_blocks = kept((4,) + neighbour_blocks.shape[1:], neighbour_blocks.dtype)
            error, lower, upper, spaced, near_blocks, far_half = call(
                near_loading_kernel,
                "first_near",
                near_results + (near_blocks, far_blocks),
                [VMEM, ANY] + [VMEM] * 4,
                [dma((1, groups)), dma((1, 1))],
            )(state, neighbour_blocks, diag, right, dissipation, omega)
            state, error, far_blocks, square = call(
                far_loading_kernel,
                "first_far",
                far_results + (far_blocks, kept(tile)),
                [VMEM] * 3 + [ANY] + [VMEM] * 9,
                far_scratch + [dma((1, half_groups))],
                {0: 0, 1: 1, 2: 2},
            )(
                state,
                error,
                far_half,
                neighbour_blocks,
                *around,
                lower,
                upper,
                spaced,
                dissipation,
                step,
            )
        else:
            error, lower, upper, spaced = call(
                near_kernel, "near", near_results, [VMEM] * 6
            )(state, near_blocks, diag, right, dissipation, omega)
            state, error, square = call(
                far_kernel,
                "far",
                far_results + (kept(tile),),
                [VMEM] * 12,
                far_scratch,
                {0: 0, 1: 1},
            )(state, error, far_blocks, *around, lower, upper, spaced, dissipation, step)
        terms = (state, halo, phase, near_blocks, dissipation, step, error, square)
        if iteration < ITERS - 1:
            state, faces, even, odd, axial, square = call(
                turn_kernel,
                "pitch_terms",
                (kept(wide),) + face_shapes + (kept(tile),),
                [VMEM] * 2 + [SMEM] + [VMEM] * 5,
                aliases={0: 0},
            )(*terms)
            squares.append(square)
        else:
            out, share = call(
                last_kernel,
                "last_pitch_terms",
                (kept(block), kept((devices, 1, lanes))),
                [VMEM] * 2 + [SMEM] + [VMEM] * 6,
                [pltpu.VMEM(tile, jnp.float32)],
            )(*terms, squares[0])
    shares = lax.all_to_all(share, ("pitch", "span", "axial"), 0, 0, tiled=True)
    totals = jnp.sum(shares, axis=(0, 1))[:ITERS]
    cell_count = float(rows * planes * span * lanes * devices)
    norms = jnp.sqrt(totals / cell_count)
    return (out.reshape(parts, nv, planes, span, lanes), norms)


def solution(mesh):
    placed = (
        P(None, None, "pitch", "span", "axial"),
        P(None, None, "pitch", "span", "axial"),
        P(None, None, "pitch", "span", "axial"),
        P(None, None, None, "pitch", "span", "axial"),
        P(None, "pitch", "span", "axial"),
        P("pitch", "span", "axial"),
        P("pitch", "span", "axial"),
        P(),
    )
    return jax.shard_map(
        body,
        mesh=mesh,
        in_specs=placed,
        out_specs=(P(None, None, "pitch", "span", "axial"), P()),
        check_vma=False,
    )
```

time: 48.1 us -> 45.3 us (0.942)
  blocking collectives: 11.7 us -> 0 us
  waiting for transfers between devices: 0.03 us -> 6.29 us
  starting transfers between devices: 16.6 us -> 21.8 us
  Pallas kernels: 17.4 us -> 14.1 us
  local copies, waits for them, and re-layouts: 0 us -> 0.88 us
    all_to_all x1 -> x0, blocking collectives: 11.7 us -> none  [body(): shares = lax.all_to_all(share, ('pitch', 'span', 'axial'), 0, 0, tiled=True)]
    all_to_all x0 -> x1, starting transfers between devices: none -> 7.15 us  [body(): shares = lax.all_to_all(share, ('pitch', 'span', 'axial'), 0, 0, tiled=True)]
    all_to_all x0 -> x1, waiting for transfers between devices: none -> 6.27 us  [body(): shares = lax.all_to_all(share, ('pitch', 'span', 'axial'), 0, 0, tiled=True)]
    pallas_call x9 -> x7, Pallas kernels: 17.4 us -> 14.1 us  [the longest x1 3.03 us: body(): call(far_loading_kernel, 'first_far', far_results + (far_blocks, kept(til...]
    ppermute x8, starting transfers between devices: 13 us -> 10.4 us  [swap(): lax.ppermute(values, axis, ends + [(j, i) for i, j in ends])]
    unnamed x0 -> x1, local copies, waits for them, and re-layouts: none -> 0.88 us
    ppermute x2, starting transfers between devices: 3.6 us -> 4.25 us  [exchange_pitch(): return lax.ppermute(faces, 'pitch', up)]
  transfers between devices with their start and end apart: 10 -> 11, of which waited for: 0 -> 1; matrix products, arithmetic and copies ran while one was open for 0% -> 2% of each run, Pallas kernels for 31% -> 24%
where the time goes in v3:
time: 45.3 us; the launch traced here: 45.1 us
  starting transfers between devices  21.8 us (48%)
  Pallas kernels  14.1 us (31%)
  waiting for transfers between devices  6.29 us (14%)
  between operations  1.45 us (3%)
  local copies, waits for them, and re-layouts  0.88 us (2%)
  other arithmetic  0.57 us (1%)
    ppermute x8, starting transfers between devices, swap(): lax.ppermute(values, axis, ends + [(j, i) for i, j in ends])  10.4 us
    all_to_all x1, starting transfers between devices, body(): shares = lax.all_to_all(share, ('pitch', 'span', 'axial'), 0, 0, tiled=True)  7.15 us
    all_to_all x1, waiting for transfers between devices, body(): shares = lax.all_to_all(share, ('pitch', 'span', 'axial'), 0, 0, tiled=True)  6.27 us
    ppermute x2, starting transfers between devices, exchange_pitch(): return lax.ppermute(faces, 'pitch', up)  4.25 us
    pallas_call x1, Pallas kernels, body(): call(far_loading_kernel, 'first_far', far_results + (far_blocks, kept(til...  3.03 us
    pallas_call x1, Pallas kernels, body(): call(near_loading_kernel, 'first_near', near_results + (near_blocks, far_...  2.97 us
    pallas_call x1, Pallas kernels, body(): call(far_kernel, 'far', far_results + (kept(tile),), [VMEM] * 12, far_scr...  2.95 us
    pallas_call x1, Pallas kernels, body(): call(open_kernel, 'open', (kept(wide),) + face_shapes + tuple((kept(c.sha...  1.9 us
  transfers between devices with their start and end apart: 11, of which 1 were waited for; matrix products, arithmetic and copies ran while one was open for 2% of the time, Pallas kernels for 24%

profile of v3, /device:TPU:0, one launch (start us, length us, event | category | flops | bytes accessed | tf_op | source)
XLA Modules:
  0.0 45.1 jit_solution(12314066316623575406)
XLA Ops:
  0.6 1.9 %open.1 = (f32[12,12,16,128]{3,2,1,0:T(8,128)S(1)}, f32[2,12,2,16,128]{4,3,2,1,0:T(8,128)S(1)}, f32[12,8,2,128]{3,2,1,0:T(2,128)S(1)}, f32[12,8,2,128]{3,2,1,0:T...) custom-call(f32[12,8,16,128]{3,2,1,0:T(8,128)} %bitcast.4, ...), custom_call_target="tpu_custom_call" | custom-call | tf_op jit(solution)/shard_map/open/pallas_call | solution.py:550
  2.5 3.0 %collective-permute-start.4 = (f32[2,12,2,16,128]{4,3,2,1,0:T(8,128)S(1)}, f32[2,12,2,16,128]{4,3,2,1,0:T(8,128)S(1)}, u32[]{:S(2)}, u32[]{:S(2)}) collective-permute-start(f32[2,12,2,16,128]{4,3,2,1,0:T(8,128)S(1)} %get-tuple-element.52), channel_id=1, source_target_pairs={{0,16},{16,0},{1,17},{17,1},{2,18},{18,2},{3,19},{19,3},{4,20},{20... | collective-permute-start | bytes 1179656 | tf_op jit(solution)/shard_map/ppermute | solution.py:531
  5.6 1.6 %collective-permute-start = (f32[12,8,2,128]{3,2,1,0:T(2,128)S(1)}, f32[12,8,2,128]{3,2,1,0:T(2,128)S(1)}, u32[]{:S(2)}, u32[]{:S(2)}) collective-permute-start(f32[12,8,2,128]{3,2,1,0:T(2,128)S(1)} %get-tuple-element.44), channel_id=1, source_target_pairs={{0,4},{8,12},{4,0},{12,8},{1,5},{9,13},{5,1},{13,9},{2,6},{10,14},... | collective-permute-start | bytes 294920 | tf_op jit(solution)/shard_map/ppermute | solution.py:538
  7.2 0.7 %collective-permute-start.1 = (f32[12,8,2,128]{3,2,1,0:T(2,128)S(1)}, f32[12,8,2,128]{3,2,1,0:T(2,128)S(1)}, u32[]{:S(2)}, u32[]{:S(2)}) collective-permute-start(f32[12,8,2,128]{3,2,1,0:T(2,128)S(1)} %get-tuple-element.45), channel_id=1, source_target_pairs={{4,8},{8,4},{5,9},{9,5},{6,10},{10,6},{7,11},{11,7},{20,24},{24,20... | collective-permute-start | bytes 294920 | tf_op jit(solution)/shard_map/ppermute | solution.py:538
  7.8 0.1 collective-permute-start.2
  7.9 0.7 %collective-permute-start.3 = (f32[3,16,128]{2,1,0:T(8,128)S(1)}, f32[3,16,128]{2,1,0:T(8,128)S(1)}, u32[]{:S(2)}, u32[]{:S(2)}) collective-permute-start(f32[3,16,128]{2,1,0:T(8,128)S(1)} %get-tuple-element.46), channel_id=1, source_target_pairs={{1,2},{2,1},{5,6},{6,5},{9,10},{10,9},{13,14},{14,13},{17,18},{18,... | collective-permute-start | bytes 73736 | tf_op jit(solution)/shard_map/ppermute | solution.py:538
  9.2 3.0 %first_near.1 = (f32[12,8,16,128]{3,2,1,0:T(8,128)S(1)}, f32[12,8,16,128]{3,2,1,0:T(8,128)S(1)}, f32[12,8,16,128]{3,2,1,0:T(8,128)S(1)}, f32[12,8,16,128]{3,2,1,...) custom-call(f32[12,12,16,128]{3,2,1,0:T(8,128)S(1)} %get-tuple-element.37.wide_ref., ...), custom_call_target="tpu_custom_call" | custom-call | tf_op jit(solution)/shard_map/first_near/pallas_call | solution.py:572
  12.2 0.0 collective-permute-done.3.axial_odd_ref
  12.2 0.0 collective-permute-done.span_even_ref
  12.2 3.0 %first_far.1 = (f32[12,12,16,128]{3,2,1,0:T(8,128)S(1)}, f32[12,8,16,128]{3,2,1,0:T(8,128)S(1)}, bf16[4,6,6,8,16,128]{5,4,3,2,1,0:T(8,128)(2,1)S(1)}, f32[16,128]{1,0:T(8,128)S(1)}) custom-call(f32[12,12,16,128]{3,2,1,0:T(8,128)S(1)} %get-tuple-element.37.wide_ref.wide_in_ref, ...), custom_call_target="tpu_custom_call", output_to_operand_aliasing={{0}: (0, {}), {1}: (1, {}), {2}: (2, {})} | custom-call | tf_op jit(solution)/shard_map/first_far/pallas_call | solution.py:579
  15.3 0.5 %pitch_terms.1 = (f32[12,12,16,128]{3,2,1,0:T(8,128)S(1)}, f32[2,12,2,16,128]{4,3,2,1,0:T(8,128)S(1)}, f32[12,8,2,128]{3,2,1,0:T(2,128)S(1)}, f32[12,8,2,128]{3,...) custom-call(f32[12,12,16,128]{3,2,1,0:T(8,128)S(1)} %get-tuple-element.51.wi, ...), custom_call_target="tpu_custom_call", output_to_operand_aliasing={{0}: (0, {})} | custom-call | tf_op jit(solution)/shard_map/pitch_terms/pallas_call | solution.py:612
  15.7 1.2 %collective-permute-start.9 = (f32[2,12,2,16,128]{4,3,2,1,0:T(8,128)S(1)}, f32[2,12,2,16,128]{4,3,2,1,0:T(8,128)S(1)}, u32[]{:S(2)}, u32[]{:S(2)}) collective-permute-start(f32[2,12,2,16,128]{4,3,2,1,0:T(8,128)S(1)} %get-tuple-element.66), channel_id=1, source_target_pairs={{0,16},{16,0},{1,17},{17,1},{2,18},{18,2},{3,19},{19,3},{4,20},{20... | collective-permute-start | bytes 1179656 | tf_op jit(solution)/shard_map/ppermute | solution.py:531
  16.9 3.7 %collective-permute-start.5 = (f32[12,8,2,128]{3,2,1,0:T(2,128)S(1)}, f32[12,8,2,128]{3,2,1,0:T(2,128)S(1)}, u32[]{:S(2)}, u32[]{:S(2)}) collective-permute-start(f32[12,8,2,128]{3,2,1,0:T(2,128)S(1)} %get-tuple-element.59), channel_id=1, source_target_pairs={{0,4},{8,12},{4,0},{12,8},{1,5},{9,13},{5,1},{13,9},{2,6},{10,14},... | collective-permute-start | bytes 294920 | tf_op jit(solution)/shard_map/ppermute | solution.py:538
  20.7 0.7 %collective-permute-start.6 = (f32[12,8,2,128]{3,2,1,0:T(2,128)S(1)}, f32[12,8,2,128]{3,2,1,0:T(2,128)S(1)}, u32[]{:S(2)}, u32[]{:S(2)}) collective-permute-start(f32[12,8,2,128]{3,2,1,0:T(2,128)S(1)} %get-tuple-element.60), channel_id=1, source_target_pairs={{4,8},{8,4},{5,9},{9,5},{6,10},{10,6},{7,11},{11,7},{20,24},{24,20... | collective-permute-start | bytes 294920 | tf_op jit(solution)/shard_map/ppermute | solution.py:538
  21.4 2.4 %collective-permute-start.7 = (f32[3,16,128]{2,1,0:T(8,128)S(1)}, f32[3,16,128]{2,1,0:T(8,128)S(1)}, u32[]{:S(2)}, u32[]{:S(2)}) collective-permute-start(f32[3,16,128]{2,1,0:T(8,128)S(1)} %get-tuple-element.61), channel_id=1, source_target_pairs={{0,1},{2,3},{1,0},{3,2},{4,5},{6,7},{5,4},{7,6},{8,9},{10,11},{9,8... | collective-permute-start | bytes 73736 | tf_op jit(solution)/shard_map/ppermute | solution.py:538
  23.7 0.7 %collective-permute-start.8 = (f32[3,16,128]{2,1,0:T(8,128)S(1)}, f32[3,16,128]{2,1,0:T(8,128)S(1)}, u32[]{:S(2)}, u32[]{:S(2)}) collective-permute-start(f32[3,16,128]{2,1,0:T(8,128)S(1)} %get-tuple-element.61), channel_id=1, source_target_pairs={{1,2},{2,1},{5,6},{6,5},{9,10},{10,9},{13,14},{14,13},{17,18},{18,... | collective-permute-start | bytes 73736 | tf_op jit(solution)/shard_map/ppermute | solution.py:538
  24.4 1.8 %near.1 = (f32[12,8,16,128]{3,2,1,0:T(8,128)S(1)}, f32[12,8,16,128]{3,2,1,0:T(8,128)S(1)}, f32[12,8,16,128]{3,2,1,0:T(8,128)S(1)}, f32[12,8,16,128]{3,2,1,0:T(8,128)S(1)}) custom-call(f32[12,12,16,128]{3,2,1,0:T(8,128)S(1)} %get-tuple-element.56.refs_0_.wide_in_ref, bf16[2,6,6,8,16,128]{5,4,3,2,1,0:T(8,128)(2,1)S(1)} %get-tuple-element.53.neighbour_ref.refs_1_, ...), custom_call_target="tpu_custom_call" | custom-call | tf_op jit(solution)/shard_map/near/pallas_call | solution.py:599
  26.3 2.9 %far.1 = (f32[12,12,16,128]{3,2,1,0:T(8,128)S(1)}, f32[12,8,16,128]{3,2,1,0:T(8,128)S(1)}, f32[16,128]{1,0:T(8,128)S(1)}) custom-call(f32[12,12,16,128]{3,2,1,0:T(8,128)S(1)} %get-tuple-element.56.refs_0_.wide_in_ref, f32[12,8,16,128]{3,2,1,0:T(8,128)S(1)} %get-tuple-element.57.error_in_ref, ...), custom_call_target="tpu_custom_call", output_to_operand_aliasing={{0}: (0, {}), {1}: (1, {})} | custom-call | tf_op jit(solution)/shard_map/far/pallas_call | solution.py:602
  29.2 1.0 %last_pitch_terms.1 = (f32[12,8,16,128]{3,2,1,0:T(8,128)S(1)}, f32[32,1,128]{2,1,0:T(1,128)}) custom-call(f32[12,12,16,128]{3,2,1,0:T(8,128)S(1)} %get-tuple-element.65.wide_ref, f32[2,12,2,16,128]{4,3,2,1,0:T(8,128)S(1)} %collective-permute-done.9.halo_ref, f32[1]{0:T(128)S(6)} %copy.23.phase_ref, ...), custom_call_target="tpu_custom_call" | custom-call | tf_op jit(solution)/shard_map/last_pitch_terms/pallas_call | solution.py:621
  30.2 7.1 %all-to-all-start = ((f32[32,1,128]{2,1,0:T(1,128)}), f32[32,1,128]{2,1,0:T(1,128)S(1)}, u32[]{:S(2)}, u32[]{:S(2)}) async-start(f32[32,1,128]{2,1,0:T(1,128)} %get-tuple-element.71), calls=%async_computation | async-start | bytes 32768 | tf_op jit(solution)/shard_map/all_to_all | solution.py:628
  37.3 0.9 %copy.22 = f32[2,6,8,16,128]{4,3,2,1,0:T(8,128)} copy(f32[2,6,8,16,128]{4,3,2,1,0:T(8,128)S(1)} %bitcast.3) | data formatting | bytes 1572864
  38.2 6.3 %all-to-all-done = f32[32,1,128]{2,1,0:T(1,128)S(1)} async-done(((f32[32,1,128]{2,1,0:T(1,128)}), f32[32,1,128]{2,1,0:T(1,128)S(1)}, u32[]{:S(2)}, u32[]{:S(2)}) %all-to-all-start) | async-done | bytes 16416 | tf_op jit(solution)/shard_map/all_to_all | solution.py:628
  44.5 0.1 reduce_sum.9
  44.5 0.5 %multiply_sqrt_fusion = f32[2]{0:T(128)} fusion(f32[128]{0:T(128)S(1)} %reduce_sum.9), kind=kLoop, calls=%fused_computation | loop fusion | flops 2 | bytes 16 | tf_op jit(solution)/shard_map/sqrt | solution.py:631
  (8 shorter events, 0.0 us)
Async XLA Ops:
  2.5 12.7 %collective-permute-start.4 = (f32[2,12,2,16,128]{4,3,2,1,0:T(8,128)S(1)}, f32[2,12,2,16,128]{4,3,2,1,0:T(8,128)S(1)}, u32[]{:S(2)}, u32[]{:S(2)}) collective-permute-start(f32[2,12,2,16,128]{4,3,2,1,0:T(8,128)S(1)} %get-tuple-element.52), channel_id=1, source_target_pairs={{0,16},{16,0},{1,17},{17,1},{2,18},{18,2},{3,19},{19,3},{4,20},{20... | collective-permute-start | bytes 1179656 | tf_op jit(solution)/shard_map/ppermute | solution.py:531
  5.6 6.6 %collective-permute-start = (f32[12,8,2,128]{3,2,1,0:T(2,128)S(1)}, f32[12,8,2,128]{3,2,1,0:T(2,128)S(1)}, u32[]{:S(2)}, u32[]{:S(2)}) collective-permute-start(f32[12,8,2,128]{3,2,1,0:T(2,128)S(1)} %get-tuple-element.44), channel_id=1, source_target_pairs={{0,4},{8,12},{4,0},{12,8},{1,5},{9,13},{5,1},{13,9},{2,6},{10,14},... | collective-permute-start | bytes 294920 | tf_op jit(solution)/shard_map/ppermute | solution.py:538
  7.2 5.1 %collective-permute-start.1 = (f32[12,8,2,128]{3,2,1,0:T(2,128)S(1)}, f32[12,8,2,128]{3,2,1,0:T(2,128)S(1)}, u32[]{:S(2)}, u32[]{:S(2)}) collective-permute-start(f32[12,8,2,128]{3,2,1,0:T(2,128)S(1)} %get-tuple-element.45), channel_id=1, source_target_pairs={{4,8},{8,4},{5,9},{9,5},{6,10},{10,6},{7,11},{11,7},{20,24},{24,20... | collective-permute-start | bytes 294920 | tf_op jit(solution)/shard_map/ppermute | solution.py:538
  7.8 4.4 %collective-permute-start.2 = (f32[3,16,128]{2,1,0:T(8,128)S(1)}, f32[3,16,128]{2,1,0:T(8,128)S(1)}, u32[]{:S(2)}, u32[]{:S(2)}) collective-permute-start(f32[3,16,128]{2,1,0:T(8,128)S(1)} %get-tuple-element.46), channel_id=1, source_target_pairs={{0,1},{2,3},{1,0},{3,2},{4,5},{6,7},{5,4},{7,6},{8,9},{10,11},{9,8... | collective-permute-start | bytes 73736 | tf_op jit(solution)/shard_map/ppermute | solution.py:538
  7.9 4.3 %collective-permute-start.3 = (f32[3,16,128]{2,1,0:T(8,128)S(1)}, f32[3,16,128]{2,1,0:T(8,128)S(1)}, u32[]{:S(2)}, u32[]{:S(2)}) collective-permute-start(f32[3,16,128]{2,1,0:T(8,128)S(1)} %get-tuple-element.46), channel_id=1, source_target_pairs={{1,2},{2,1},{5,6},{6,5},{9,10},{10,9},{13,14},{14,13},{17,18},{18,... | collective-permute-start | bytes 73736 | tf_op jit(solution)/shard_map/ppermute | solution.py:538
  15.7 13.5 %collective-permute-start.9 = (f32[2,12,2,16,128]{4,3,2,1,0:T(8,128)S(1)}, f32[2,12,2,16,128]{4,3,2,1,0:T(8,128)S(1)}, u32[]{:S(2)}, u32[]{:S(2)}) collective-permute-start(f32[2,12,2,16,128]{4,3,2,1,0:T(8,128)S(1)} %get-tuple-element.66), channel_id=1, source_target_pairs={{0,16},{16,0},{1,17},{17,1},{2,18},{18,2},{3,19},{19,3},{4,20},{20... | collective-permute-start | bytes 1179656 | tf_op jit(solution)/shard_map/ppermute | solution.py:531
  16.9 9.3 %collective-permute-start.5 = (f32[12,8,2,128]{3,2,1,0:T(2,128)S(1)}, f32[12,8,2,128]{3,2,1,0:T(2,128)S(1)}, u32[]{:S(2)}, u32[]{:S(2)}) collective-permute-start(f32[12,8,2,128]{3,2,1,0:T(2,128)S(1)} %get-tuple-element.59), channel_id=1, source_target_pairs={{0,4},{8,12},{4,0},{12,8},{1,5},{9,13},{5,1},{13,9},{2,6},{10,14},... | collective-permute-start | bytes 294920 | tf_op jit(solution)/shard_map/ppermute | solution.py:538
  20.7 5.6 %collective-permute-start.6 = (f32[12,8,2,128]{3,2,1,0:T(2,128)S(1)}, f32[12,8,2,128]{3,2,1,0:T(2,128)S(1)}, u32[]{:S(2)}, u32[]{:S(2)}) collective-permute-start(f32[12,8,2,128]{3,2,1,0:T(2,128)S(1)} %get-tuple-element.60), channel_id=1, source_target_pairs={{4,8},{8,4},{5,9},{9,5},{6,10},{10,6},{7,11},{11,7},{20,24},{24,20... | collective-permute-start | bytes 294920 | tf_op jit(solution)/shard_map/ppermute | solution.py:538
  21.4 4.9 %collective-permute-start.7 = (f32[3,16,128]{2,1,0:T(8,128)S(1)}, f32[3,16,128]{2,1,0:T(8,128)S(1)}, u32[]{:S(2)}, u32[]{:S(2)}) collective-permute-start(f32[3,16,128]{2,1,0:T(8,128)S(1)} %get-tuple-element.61), channel_id=1, source_target_pairs={{0,1},{2,3},{1,0},{3,2},{4,5},{6,7},{5,4},{7,6},{8,9},{10,11},{9,8... | collective-permute-start | bytes 73736 | tf_op jit(solution)/shard_map/ppermute | solution.py:538
  23.7 2.5 %collective-permute-start.8 = (f32[3,16,128]{2,1,0:T(8,128)S(1)}, f32[3,16,128]{2,1,0:T(8,128)S(1)}, u32[]{:S(2)}, u32[]{:S(2)}) collective-permute-start(f32[3,16,128]{2,1,0:T(8,128)S(1)} %get-tuple-element.61), channel_id=1, source_target_pairs={{1,2},{2,1},{5,6},{6,5},{9,10},{10,9},{13,14},{14,13},{17,18},{18,... | collective-permute-start | bytes 73736 | tf_op jit(solution)/shard_map/ppermute | solution.py:538
  30.2 14.3 %all-to-all-start = ((f32[32,1,128]{2,1,0:T(1,128)}), f32[32,1,128]{2,1,0:T(1,128)S(1)}, u32[]{:S(2)}, u32[]{:S(2)}) async-start(f32[32,1,128]{2,1,0:T(1,128)} %get-tuple-element.71), calls=%async_computation | async-start | bytes 32768 | tf_op jit(solution)/shard_map/all_to_all | solution.py:628

commit v4 on v3

--- a/solution.py
+++ b/solution.py
@@ -73,6 +73,12 @@
                 packed = jnp.where(lane >= 2 * WIDTH * place, moved, packed)
         if k == rows - 1 or lane_place(k + 1, planes, lanes)[0] != group:
             axial_ref[group] = packed
+
+
+def alone(axis):
+    at = lax.axis_index(axis)
+    count = lax.axis_size(axis)
+    return jnp.logical_or(at == 0, jnp.logical_and(at == count - 1, count % 2 == 0))
 
 
 class Loads:
@@ -329,12 +335,14 @@
     nv = rows // 2
     span_even = lax.axis_index("span") % 2 == 0
     axial_even = lax.axis_index("axial") % 2 == 0
+    span_alone = alone("span")
+    axial_alone = alone("axial")
     lane = lax.broadcasted_iota(jnp.int32, (span, lanes), 1)
     edge = jnp.logical_or(lane < WIDTH, lane >= lanes - WIDTH)
     from_below = lane % (2 * WIDTH) >= WIDTH
     for group in range(axial_buf.shape[0]):
         at_even = axial_even_ref[group]
-        at_odd = axial_odd_ref[group]
+        at_odd = jnp.where(axial_alone, 0.0, axial_odd_ref[group])
         below = pltpu.roll(jnp.where(axial_even, at_odd, at_even), WIDTH, axis=1)
         above = pltpu.roll(jnp.where(axial_even, at_even, at_odd), lanes - WIDTH, axis=1)
         axial_buf[group] = jnp.where(from_below, below, above)
@@ -345,7 +353,7 @@
             loads.ready(p)
         for k in range(rows):
             at_even = span_even_ref[k, p]
-            at_odd = span_odd_ref[k, p]
+            at_odd = jnp.where(span_alone, 0.0, span_odd_ref[k, p])
             span_buf[k, PAD - WIDTH : PAD] = jnp.where(span_even, at_odd, at_even)
             span_buf[k, PAD : PAD + span] = wide_ref[k, p + WIDTH]
             span_buf[k, PAD + span : PAD + span + WIDTH] = jnp.where(span_even, at_even, at_odd)
@@ -533,16 +541,34 @@
             [lax.ppermute(faces[0], "pitch", up), lax.ppermute(faces[1], "pitch", down)]
         )
 
-    def swap(values, axis, start):
-        ends = [(i, i + 1) for i in range(start, lax.axis_size(axis) - 1, 2)]
-        return resident(lax.ppermute(values, axis, ends + [(j, i) for i, j in ends]))
+    span_count = lax.axis_size("span")
+    axial_count = lax.axis_size("axial")
+
+    def span_swap(values, start):
+        partner = {}
+        for i in range(start, span_count - 1, 2):
+            partner.update({i: i + 1, i + 1: i})
+        pairs = []
+        for i in range(span_count):
+            for j in range(axial_count):
+                if i in partner:
+                    pairs.append((i * axial_count + j, partner[i] * axial_count + j))
+                elif axial_count % 2 == 0:
+                    pairs.append((i * axial_count + j, i * axial_count + (j ^ 1)))
+        return resident(lax.ppermute(values, ("span", "axial"), pairs))
+
+    def axial_swap(values, start):
+        pairs = [(i, i + 1) for i in range(start, axial_count - 1, 2)]
+        if start == 1 and axial_count % 2 == 0:
+            pairs.append((0, axial_count - 1))
+        return resident(lax.ppermute(values, "axial", pairs + [(j, i) for i, j in pairs]))
 
     def exchange_rest(even, odd, axial):
         return (
-            swap(even, "span", 0),
-            swap(odd, "span", 1),
-            swap(axial, "axial", 0),
-            swap(axial, "axial", 1),
+            span_swap(even, 0),
+            span_swap(odd, 1),
+            axial_swap(axial, 0),
+            axial_swap(axial, 1),
         )
 
     neighbour_blocks = outside(neighbour_blocks)

time: 45.3 us -> 40.2 us (0.89)
  starting transfers between devices: 21.8 us -> 14.3 us
  waiting for transfers between devices: 6.29 us -> 8.66 us
    ppermute x8, starting transfers between devices: 10.4 us -> 6.56 us  [the longest x4 4.3 us: span_swap(): return resident(lax.ppermute(values, ('span', 'axial'), pairs))]
    all_to_all x1, starting transfers between devices: 7.15 us -> 3.72 us  [body(): shares = lax.all_to_all(share, ('pitch', 'span', 'axial'), 0, 0, tiled=True)]
    ppermute x8, waiting for transfers between devices: 0.02 us -> 1.35 us  [the longest x4 1.34 us: axial_swap(): lax.ppermute(values, 'axial', pairs + [(j, i) for i, j in pairs])]
    ppermute x2, waiting for transfers between devices: 0.01 us -> 1.04 us  [exchange_pitch(): return lax.ppermute(faces, 'pitch', up)]
  transfers between devices with their start and end apart: 11 -> 11, of which waited for: 1 -> 3; matrix products, arithmetic and copies ran while one was open for 2% -> 2% of each run, Pallas kernels for 24% -> 27%
where the time goes in v4:
time: 40.2 us; the launch traced here: 40 us
  starting transfers between devices  14.3 us (36%)
  Pallas kernels  14.1 us (35%)
  waiting for transfers between devices  8.66 us (22%)
  between operations  1.39 us (3%)
  local copies, waits for them, and re-layouts  0.88 us (2%)
  other arithmetic  0.57 us (1%)
    all_to_all x1, waiting for transfers between devices, body(): shares = lax.all_to_all(share, ('pitch', 'span', 'axial'), 0, 0, tiled=True)  6.27 us
    ppermute x4, starting transfers between devices, span_swap(): return resident(lax.ppermute(values, ('span', 'axial'), pairs))  4.3 us
    ppermute x2, starting transfers between devices, exchange_pitch(): return lax.ppermute(faces, 'pitch', up)  4.03 us
    all_to_all x1, starting transfers between devices, body(): shares = lax.all_to_all(share, ('pitch', 'span', 'axial'), 0, 0, tiled=True)  3.72 us
    pallas_call x1, Pallas kernels, body(): call(far_loading_kernel, 'first_far', far_results + (far_blocks, kept(til...  3.04 us
    pallas_call x1, Pallas kernels, body(): call(far_kernel, 'far', far_results + (kept(tile),), [VMEM] * 12, far_scr...  2.98 us
    pallas_call x1, Pallas kernels, body(): call(near_loading_kernel, 'first_near', near_results + (near_blocks, far_...  2.97 us
    ppermute x4, starting transfers between devices, axial_swap(): lax.ppermute(values, 'axial', pairs + [(j, i) for i, j in pairs])  2.26 us
  transfers between devices with their start and end apart: 11, of which 3 were waited for; matrix products, arithmetic and copies ran while one was open for 2% of the time, Pallas kernels for 27%

profile of v4, /device:TPU:0, one launch (start us, length us, event | category | flops | bytes accessed | tf_op | source)
XLA Modules:
  0.0 40.0 jit_solution(6492575249762717524)
XLA Ops:
  0.6 1.9 %open.1 = (f32[12,12,16,128]{3,2,1,0:T(8,128)S(1)}, f32[2,12,2,16,128]{4,3,2,1,0:T(8,128)S(1)}, f32[12,8,2,128]{3,2,1,0:T(2,128)S(1)}, f32[12,8,2,128]{3,2,1,0:T...) custom-call(f32[12,8,16,128]{3,2,1,0:T(8,128)} %bitcast.4, ...), custom_call_target="tpu_custom_call" | custom-call | tf_op jit(solution)/shard_map/open/pallas_call | solution.py:576
  2.5 3.0 %collective-permute-start.4 = (f32[2,12,2,16,128]{4,3,2,1,0:T(8,128)S(1)}, f32[2,12,2,16,128]{4,3,2,1,0:T(8,128)S(1)}, u32[]{:S(2)}, u32[]{:S(2)}) collective-permute-start(f32[2,12,2,16,128]{4,3,2,1,0:T(8,128)S(1)} %get-tuple-element.52), channel_id=1, source_target_pairs={{0,16},{16,0},{1,17},{17,1},{2,18},{18,2},{3,19},{19,3},{4,20},{20... | collective-permute-start | bytes 1179656 | tf_op jit(solution)/shard_map/ppermute | solution.py:539
  5.6 1.6 %collective-permute-start = (f32[12,8,2,128]{3,2,1,0:T(2,128)S(1)}, f32[12,8,2,128]{3,2,1,0:T(2,128)S(1)}, u32[]{:S(2)}, u32[]{:S(2)}) collective-permute-start(f32[12,8,2,128]{3,2,1,0:T(2,128)S(1)} %get-tuple-element.44), channel_id=1, source_target_pairs={{0,4},{1,5},{2,6},{3,7},{4,0},{5,1},{6,2},{7,3},{8,12},{9,13},{10,... | collective-permute-start | bytes 294920 | tf_op jit(solution)/shard_map/ppermute | solution.py:558
  7.2 0.0 collective-permute-start.1
  7.2 0.5 %collective-permute-start.2 = (f32[3,16,128]{2,1,0:T(8,128)S(1)}, f32[3,16,128]{2,1,0:T(8,128)S(1)}, u32[]{:S(2)}, u32[]{:S(2)}) collective-permute-start(f32[3,16,128]{2,1,0:T(8,128)S(1)} %get-tuple-element.46), channel_id=1, source_target_pairs={{0,1},{2,3},{1,0},{3,2},{4,5},{6,7},{5,4},{7,6},{8,9},{10,11},{9,8... | collective-permute-start | bytes 73736 | tf_op jit(solution)/shard_map/ppermute | solution.py:564
  7.7 1.1 %collective-permute-start.3 = (f32[3,16,128]{2,1,0:T(8,128)S(1)}, f32[3,16,128]{2,1,0:T(8,128)S(1)}, u32[]{:S(2)}, u32[]{:S(2)}) collective-permute-start(f32[3,16,128]{2,1,0:T(8,128)S(1)} %get-tuple-element.46), channel_id=1, source_target_pairs={{1,2},{0,3},{2,1},{3,0},{5,6},{4,7},{6,5},{7,4},{9,10},{8,11},{10,... | collective-permute-start | bytes 73736 | tf_op jit(solution)/shard_map/ppermute | solution.py:564
  9.4 3.0 %first_near.1 = (f32[12,8,16,128]{3,2,1,0:T(8,128)S(1)}, f32[12,8,16,128]{3,2,1,0:T(8,128)S(1)}, f32[12,8,16,128]{3,2,1,0:T(8,128)S(1)}, f32[12,8,16,128]{3,2,1,...) custom-call(f32[12,12,16,128]{3,2,1,0:T(8,128)S(1)} %get-tuple-element.37.wide_ref., ...), custom_call_target="tpu_custom_call" | custom-call | tf_op jit(solution)/shard_map/first_near/pallas_call | solution.py:598
  12.4 0.0 collective-permute-done.3.axial_odd_ref
  12.4 3.0 %first_far.1 = (f32[12,12,16,128]{3,2,1,0:T(8,128)S(1)}, f32[12,8,16,128]{3,2,1,0:T(8,128)S(1)}, bf16[4,6,6,8,16,128]{5,4,3,2,1,0:T(8,128)(2,1)S(1)}, f32[16,128]{1,0:T(8,128)S(1)}) custom-call(f32[12,12,16,128]{3,2,1,0:T(8,128)S(1)} %get-tuple-element.37.wide_ref.wide_in_ref, ...), custom_call_target="tpu_custom_call", output_to_operand_aliasing={{0}: (0, {}), {1}: (1, {}), {2}: (2, {})} | custom-call | tf_op jit(solution)/shard_map/first_far/pallas_call | solution.py:605
  15.5 0.5 %pitch_terms.1 = (f32[12,12,16,128]{3,2,1,0:T(8,128)S(1)}, f32[2,12,2,16,128]{4,3,2,1,0:T(8,128)S(1)}, f32[12,8,2,128]{3,2,1,0:T(2,128)S(1)}, f32[12,8,2,128]{3,...) custom-call(f32[12,12,16,128]{3,2,1,0:T(8,128)S(1)} %get-tuple-element.51.wi, ...), custom_call_target="tpu_custom_call", output_to_operand_aliasing={{0}: (0, {})} | custom-call | tf_op jit(solution)/shard_map/pitch_terms/pallas_call | solution.py:638
  15.9 1.0 %collective-permute-start.9 = (f32[2,12,2,16,128]{4,3,2,1,0:T(8,128)S(1)}, f32[2,12,2,16,128]{4,3,2,1,0:T(8,128)S(1)}, u32[]{:S(2)}, u32[]{:S(2)}) collective-permute-start(f32[2,12,2,16,128]{4,3,2,1,0:T(8,128)S(1)} %get-tuple-element.66), channel_id=1, source_target_pairs={{0,16},{16,0},{1,17},{17,1},{2,18},{18,2},{3,19},{19,3},{4,20},{20... | collective-permute-start | bytes 1179656 | tf_op jit(solution)/shard_map/ppermute | solution.py:539
  16.9 2.7 %collective-permute-start.5 = (f32[12,8,2,128]{3,2,1,0:T(2,128)S(1)}, f32[12,8,2,128]{3,2,1,0:T(2,128)S(1)}, u32[]{:S(2)}, u32[]{:S(2)}) collective-permute-start(f32[12,8,2,128]{3,2,1,0:T(2,128)S(1)} %get-tuple-element.59), channel_id=1, source_target_pairs={{0,4},{1,5},{2,6},{3,7},{4,0},{5,1},{6,2},{7,3},{8,12},{9,13},{10,... | collective-permute-start | bytes 294920 | tf_op jit(solution)/shard_map/ppermute | solution.py:558
  19.7 0.5 %collective-permute-start.7 = (f32[3,16,128]{2,1,0:T(8,128)S(1)}, f32[3,16,128]{2,1,0:T(8,128)S(1)}, u32[]{:S(2)}, u32[]{:S(2)}) collective-permute-start(f32[3,16,128]{2,1,0:T(8,128)S(1)} %get-tuple-element.61), channel_id=1, source_target_pairs={{0,1},{2,3},{1,0},{3,2},{4,5},{6,7},{5,4},{7,6},{8,9},{10,11},{9,8... | collective-permute-start | bytes 73736 | tf_op jit(solution)/shard_map/ppermute | solution.py:564
  20.2 0.1 collective-permute-start.8
  20.3 1.8 %near.1 = (f32[12,8,16,128]{3,2,1,0:T(8,128)S(1)}, f32[12,8,16,128]{3,2,1,0:T(8,128)S(1)}, f32[12,8,16,128]{3,2,1,0:T(8,128)S(1)}, f32[12,8,16,128]{3,2,1,0:T(8,128)S(1)}) custom-call(f32[12,12,16,128]{3,2,1,0:T(8,128)S(1)} %get-tuple-element.56.refs_0_.wide_in_ref, bf16[2,6,6,8,16,128]{5,4,3,2,1,0:T(8,128)(2,1)S(1)} %get-tuple-element.53.neighbour_ref.refs_1_, ...), custom_call_target="tpu_custom_call" | custom-call | tf_op jit(solution)/shard_map/near/pallas_call | solution.py:625
  22.2 1.3 %collective-permute-done.8.refs_4_ = f32[3,16,128]{2,1,0:T(8,128)S(1)} collective-permute-done((f32[3,16,128]{2,1,0:T(8,128)S(1)}, f32[3,16,128]{2,1,0:T(8,128)S(1)}, u32[]{:S(2)}, u32[]{:S(2)}) %collective-permute-start.8) | collective-permute-done | bytes 24608 | tf_op jit(solution)/shard_map/ppermute | solution.py:564
  23.5 3.0 %far.1 = (f32[12,12,16,128]{3,2,1,0:T(8,128)S(1)}, f32[12,8,16,128]{3,2,1,0:T(8,128)S(1)}, f32[16,128]{1,0:T(8,128)S(1)}) custom-call(f32[12,12,16,128]{3,2,1,0:T(8,128)S(1)} %get-tuple-element.56.refs_0_.wide_in_ref, f32[12,8,16,128]{3,2,1,0:T(8,128)S(1)} %get-tuple-element.57.error_in_ref, ...), custom_call_target="tpu_custom_call", output_to_operand_aliasing={{0}: (0, {}), {1}: (1, {})} | custom-call | tf_op jit(solution)/shard_map/far/pallas_call | solution.py:628
  26.5 1.0 %collective-permute-done.9.halo_ref = f32[2,12,2,16,128]{4,3,2,1,0:T(8,128)S(1)} collective-permute-done((f32[2,12,2,16,128]{4,3,2,1,0:T(8,128)S(1)}, f32[2,12,2,16,128]{4,3,2,1,0:T(8,128)S(1)}, u32[]{:S(2)}, u32[]{:S(2)}) %collective-permute-start.9) | collective-permute-done | bytes 393248 | tf_op jit(solution)/shard_map/ppermute | solution.py:539
  27.5 1.0 %last_pitch_terms.1 = (f32[12,8,16,128]{3,2,1,0:T(8,128)S(1)}, f32[32,1,128]{2,1,0:T(1,128)}) custom-call(f32[12,12,16,128]{3,2,1,0:T(8,128)S(1)} %get-tuple-element.65.wide_ref, f32[2,12,2,16,128]{4,3,2,1,0:T(8,128)S(1)} %collective-permute-done.9.halo_ref, f32[1]{0:T(128)S(6)} %copy.23.phase_ref, ...), custom_call_target="tpu_custom_call" | custom-call | tf_op jit(solution)/shard_map/last_pitch_terms/pallas_call | solution.py:647
  28.5 3.7 %all-to-all-start = ((f32[32,1,128]{2,1,0:T(1,128)}), f32[32,1,128]{2,1,0:T(1,128)S(1)}, u32[]{:S(2)}, u32[]{:S(2)}) async-start(f32[32,1,128]{2,1,0:T(1,128)} %get-tuple-element.71), calls=%async_computation | async-start | bytes 32768 | tf_op jit(solution)/shard_map/all_to_all | solution.py:654
  32.2 0.9 %copy.22 = f32[2,6,8,16,128]{4,3,2,1,0:T(8,128)} copy(f32[2,6,8,16,128]{4,3,2,1,0:T(8,128)S(1)} %bitcast.3) | data formatting | bytes 1572864
  33.1 6.3 %all-to-all-done = f32[32,1,128]{2,1,0:T(1,128)S(1)} async-done(((f32[32,1,128]{2,1,0:T(1,128)}), f32[32,1,128]{2,1,0:T(1,128)S(1)}, u32[]{:S(2)}, u32[]{:S(2)}) %all-to-all-start) | async-done | bytes 16416 | tf_op jit(solution)/shard_map/all_to_all | solution.py:654
  39.4 0.1 reduce_sum.9
  39.4 0.5 %multiply_sqrt_fusion = f32[2]{0:T(128)} fusion(f32[128]{0:T(128)S(1)} %reduce_sum.9), kind=kLoop, calls=%fused_computation | loop fusion | flops 2 | bytes 16 | tf_op jit(solution)/shard_map/sqrt | solution.py:657
  (8 shorter events, 0.0 us)
Async XLA Ops:
  2.5 12.9 %collective-permute-start.4 = (f32[2,12,2,16,128]{4,3,2,1,0:T(8,128)S(1)}, f32[2,12,2,16,128]{4,3,2,1,0:T(8,128)S(1)}, u32[]{:S(2)}, u32[]{:S(2)}) collective-permute-start(f32[2,12,2,16,128]{4,3,2,1,0:T(8,128)S(1)} %get-tuple-element.52), channel_id=1, source_target_pairs={{0,16},{16,0},{1,17},{17,1},{2,18},{18,2},{3,19},{19,3},{4,20},{20... | collective-permute-start | bytes 1179656 | tf_op jit(solution)/shard_map/ppermute | solution.py:539
  5.6 6.8 %collective-permute-start = (f32[12,8,2,128]{3,2,1,0:T(2,128)S(1)}, f32[12,8,2,128]{3,2,1,0:T(2,128)S(1)}, u32[]{:S(2)}, u32[]{:S(2)}) collective-permute-start(f32[12,8,2,128]{3,2,1,0:T(2,128)S(1)} %get-tuple-element.44), channel_id=1, source_target_pairs={{0,4},{1,5},{2,6},{3,7},{4,0},{5,1},{6,2},{7,3},{8,12},{9,13},{10,... | collective-permute-start | bytes 294920 | tf_op jit(solution)/shard_map/ppermute | solution.py:558
  7.2 5.3 %collective-permute-start.1 = (f32[12,8,2,128]{3,2,1,0:T(2,128)S(1)}, f32[12,8,2,128]{3,2,1,0:T(2,128)S(1)}, u32[]{:S(2)}, u32[]{:S(2)}) collective-permute-start(f32[12,8,2,128]{3,2,1,0:T(2,128)S(1)} %get-tuple-element.45), channel_id=1, source_target_pairs={{0,1},{1,0},{2,3},{3,2},{4,8},{5,9},{6,10},{7,11},{8,4},{9,5},{10,... | collective-permute-start | bytes 294920 | tf_op jit(solution)/shard_map/ppermute | solution.py:558
  7.2 5.2 %collective-permute-start.2 = (f32[3,16,128]{2,1,0:T(8,128)S(1)}, f32[3,16,128]{2,1,0:T(8,128)S(1)}, u32[]{:S(2)}, u32[]{:S(2)}) collective-permute-start(f32[3,16,128]{2,1,0:T(8,128)S(1)} %get-tuple-element.46), channel_id=1, source_target_pairs={{0,1},{2,3},{1,0},{3,2},{4,5},{6,7},{5,4},{7,6},{8,9},{10,11},{9,8... | collective-permute-start | bytes 73736 | tf_op jit(solution)/shard_map/ppermute | solution.py:564
  7.7 4.7 %collective-permute-start.3 = (f32[3,16,128]{2,1,0:T(8,128)S(1)}, f32[3,16,128]{2,1,0:T(8,128)S(1)}, u32[]{:S(2)}, u32[]{:S(2)}) collective-permute-start(f32[3,16,128]{2,1,0:T(8,128)S(1)} %get-tuple-element.46), channel_id=1, source_target_pairs={{1,2},{0,3},{2,1},{3,0},{5,6},{4,7},{6,5},{7,4},{9,10},{8,11},{10,... | collective-permute-start | bytes 73736 | tf_op jit(solution)/shard_map/ppermute | solution.py:564
  15.9 11.6 %collective-permute-start.9 = (f32[2,12,2,16,128]{4,3,2,1,0:T(8,128)S(1)}, f32[2,12,2,16,128]{4,3,2,1,0:T(8,128)S(1)}, u32[]{:S(2)}, u32[]{:S(2)}) collective-permute-start(f32[2,12,2,16,128]{4,3,2,1,0:T(8,128)S(1)} %get-tuple-element.66), channel_id=1, source_target_pairs={{0,16},{16,0},{1,17},{17,1},{2,18},{18,2},{3,19},{19,3},{4,20},{20... | collective-permute-start | bytes 1179656 | tf_op jit(solution)/shard_map/ppermute | solution.py:539
  16.9 6.6 %collective-permute-start.5 = (f32[12,8,2,128]{3,2,1,0:T(2,128)S(1)}, f32[12,8,2,128]{3,2,1,0:T(2,128)S(1)}, u32[]{:S(2)}, u32[]{:S(2)}) collective-permute-start(f32[12,8,2,128]{3,2,1,0:T(2,128)S(1)} %get-tuple-element.59), channel_id=1, source_target_pairs={{0,4},{1,5},{2,6},{3,7},{4,0},{5,1},{6,2},{7,3},{8,12},{9,13},{10,... | collective-permute-start | bytes 294920 | tf_op jit(solution)/shard_map/ppermute | solution.py:558
  19.7 3.8 %collective-permute-start.6 = (f32[12,8,2,128]{3,2,1,0:T(2,128)S(1)}, f32[12,8,2,128]{3,2,1,0:T(2,128)S(1)}, u32[]{:S(2)}, u32[]{:S(2)}) collective-permute-start(f32[12,8,2,128]{3,2,1,0:T(2,128)S(1)} %get-tuple-element.60), channel_id=1, source_target_pairs={{0,1},{1,0},{2,3},{3,2},{4,8},{5,9},{6,10},{7,11},{8,4},{9,5},{10,... | collective-permute-start | bytes 294920 | tf_op jit(solution)/shard_map/ppermute | solution.py:558
  19.7 2.5 %collective-permute-start.7 = (f32[3,16,128]{2,1,0:T(8,128)S(1)}, f32[3,16,128]{2,1,0:T(8,128)S(1)}, u32[]{:S(2)}, u32[]{:S(2)}) collective-permute-start(f32[3,16,128]{2,1,0:T(8,128)S(1)} %get-tuple-element.61), channel_id=1, source_target_pairs={{0,1},{2,3},{1,0},{3,2},{4,5},{6,7},{5,4},{7,6},{8,9},{10,11},{9,8... | collective-permute-start | bytes 73736 | tf_op jit(solution)/shard_map/ppermute | solution.py:564
  20.2 3.3 %collective-permute-start.8 = (f32[3,16,128]{2,1,0:T(8,128)S(1)}, f32[3,16,128]{2,1,0:T(8,128)S(1)}, u32[]{:S(2)}, u32[]{:S(2)}) collective-permute-start(f32[3,16,128]{2,1,0:T(8,128)S(1)} %get-tuple-element.61), channel_id=1, source_target_pairs={{1,2},{0,3},{2,1},{3,0},{5,6},{4,7},{6,5},{7,4},{9,10},{8,11},{10,... | collective-permute-start | bytes 73736 | tf_op jit(solution)/shard_map/ppermute | solution.py:564
  28.5 10.9 %all-to-all-start = ((f32[32,1,128]{2,1,0:T(1,128)}), f32[32,1,128]{2,1,0:T(1,128)S(1)}, u32[]{:S(2)}, u32[]{:S(2)}) async-start(f32[32,1,128]{2,1,0:T(1,128)} %get-tuple-element.71), calls=%async_computation | async-start | bytes 32768 | tf_op jit(solution)/shard_map/all_to_all | solution.py:654

commit v5 on v4

v5 whole, which is shorter than its diff:
```python
import functools

import jax
import jax.numpy as jnp
from jax import lax
from jax.experimental import pallas as pl
from jax.experimental.pallas import tpu as pltpu
from jax.sharding import PartitionSpec as P

ITERS = 2
WIDTH = 2
PAD = 8
GROUPS = 4
VMEM = pl.BlockSpec(memory_space=pltpu.VMEM)
SMEM = pl.BlockSpec(memory_space=pltpu.SMEM)
ANY = pl.BlockSpec(memory_space=pl.ANY)
VMEM_LIMIT = 4 * 1024 * 1024


def resident(values):
    return pltpu.with_memory_space_constraint(values, pltpu.VMEM)


def outside(values):
    return pltpu.with_memory_space_constraint(values, pltpu.HBM)


def kept(shape, dtype=jnp.float32):
    return pltpu.VMEM(shape, dtype)


def call(kernel, name, out_shape, in_specs, scratch_shapes=(), aliases=None, out_specs=None):
    return pl.pallas_call(
        kernel,
        out_shape=out_shape,
        in_specs=in_specs,
        out_specs=out_specs or (VMEM,) * len(out_shape),
        scratch_shapes=scratch_shapes,
        input_output_aliases=aliases or {},
        compiler_params=pltpu.CompilerParams(vmem_limit_bytes=VMEM_LIMIT),
        name=name,
    )


def lane_place(k, planes, lanes):
    per_group = (lanes // (2 * WIDTH)) // planes
    return k // per_group, (k % per_group) * planes


def lane_groups(rows, planes, lanes):
    return lane_place(rows - 1, planes, lanes)[0] + 1


def pack_faces(wide_ref, even_ref, odd_ref, axial_ref):
    rows, wide, span, lanes = wide_ref.shape
    planes = wide - 2 * WIDTH
    span_even = lax.axis_index("span") % 2 == 0
    lane = lax.broadcasted_iota(jnp.int32, (span, lanes), 1)
    packed = None
    for k in range(rows):
        group, base = lane_place(k, planes, lanes)
        for p in range(planes):
            cells = wide_ref[k, p + WIDTH]
            low = cells[:WIDTH]
            high = cells[span - WIDTH :]
            even_ref[k, p] = jnp.where(span_even, high, low)
            odd_ref[k, p] = jnp.where(span_even, low, high)
            place = base + p
            moved = pltpu.roll(cells, (2 * WIDTH * place + WIDTH) % lanes, axis=1)
            if place == 0:
                packed = moved
            else:
                packed = jnp.where(lane >= 2 * WIDTH * place, moved, packed)
        if k == rows - 1 or lane_place(k + 1, planes, lanes)[0] != group:
            axial_ref[group] = packed


def alone(axis):
    at = lax.axis_index(axis)
    count = lax.axis_size(axis)
    return jnp.logical_or(at == 0, jnp.logical_and(at == count - 1, count % 2 == 0))


class Loads:
    def __init__(self, pairs, sems, first, size):
        self.pairs = pairs
        self.sems = sems
        self.first = first
        self.size = size

    def copies(self, group):
        planes = pl.ds(self.first + group * self.size, self.size)
        return [
            pltpu.make_async_copy(
                source.at[(slice(None),) * dim + (planes,)],
                target.at[(slice(None),) * dim + (planes,)],
                self.sems.at[at, group],
            )
            for at, (source, target, dim) in enumerate(self.pairs)
        ]

    def start(self):
        for group in range(self.sems.shape[1]):
            for copy in self.copies(group):
                copy.start()

    def ready(self, p):
        @pl.when(jnp.logical_and(p >= self.first, (p - self.first) % self.size == 0))
        def _():
            for copy in self.copies((p - self.first) // self.size):
                copy.wait()

    def wait(self):
        for group in range(self.sems.shape[1]):
            for copy in self.copies(group):
                copy.wait()


def faces_kernel(guess_hbm, faces_ref, sems):
    planes = guess_hbm.shape[1]
    tail = pltpu.make_async_copy(
        guess_hbm.at[:, planes - WIDTH : planes], faces_ref.at[0], sems.at[0]
    )
    head = pltpu.make_async_copy(guess_hbm.at[:, 0:WIDTH], faces_ref.at[1], sems.at[1])
    tail.start()
    head.start()
    tail.wait()
    head.wait()


def open_kernel(
    guess_hbm,
    right_hbm,
    dissipation_hbm,
    omega_hbm,
    step_hbm,
    diag_hbm,
    wide_ref,
    even_ref,
    odd_ref,
    axial_ref,
    right_ref,
    dissipation_ref,
    omega_ref,
    step_ref,
    diag_ref,
    sems,
):
    rows, wide, span, lanes = wide_ref.shape
    planes = wide - 2 * WIDTH
    pairs = (
        (guess_hbm, wide_ref.at[:, WIDTH : WIDTH + planes]),
        (dissipation_hbm, dissipation_ref),
        (omega_hbm, omega_ref),
        (step_hbm, step_ref),
        (right_hbm, right_ref),
        (diag_hbm, diag_ref),
    )
    copies = [pltpu.make_async_copy(*pair, sems.at[at]) for at, pair in enumerate(pairs)]
    for copy in copies:
        copy.start()
    for k in range(rows):
        for p in (0, 1, wide - 2, wide - 1):
            wide_ref[k, p] = jnp.zeros((span, lanes), jnp.float32)
    copies[0].wait()
    pack_faces(wide_ref, even_ref, odd_ref, axial_ref)
    for copy in copies[1:]:
        copy.wait()


def near_loading_kernel(
    wide_ref,
    neighbour_hbm,
    diag_ref,
    right_ref,
    dissipation_ref,
    omega_ref,
    error_ref,
    lower_ref,
    upper_ref,
    spaced_ref,
    neighbour_ref,
    axial_ref,
    near_sems,
    axial_sem,
):
    planes = error_ref.shape[1]
    groups = near_sems.shape[1]
    loads = Loads([(neighbour_hbm.at[0:2], neighbour_ref, 3)], near_sems, 0, planes // groups)
    later = pltpu.make_async_copy(neighbour_hbm.at[4:6], axial_ref, axial_sem)
    loads.start()
    later.start()
    shifts = (lower_ref, upper_ref)

    def own(p, carry):
        total = own_terms(wide_ref, right_ref, dissipation_ref, omega_ref, p)
        add_blocks(total, [(diag_ref, (), WIDTH)], wide_ref, p, shifts[:2], None)
        for k, value in enumerate(total):
            error_ref[k, p] = value
        return carry

    def pitch(p, carry):
        loads.ready(p)
        total = [error_ref[k, p] for k in range(error_ref.shape[0])]
        add_blocks(
            total,
            [(neighbour_ref, (0,), WIDTH - 1), (neighbour_ref, (1,), WIDTH + 1)],
            wide_ref,
            p,
            None,
            spaced_ref,
        )
        for k, value in enumerate(total):
            error_ref[k, p] = value
        return carry

    lax.fori_loop(0, planes, own, 0)
    lax.fori_loop(0, planes, pitch, 0)
    later.wait()


def near_kernel(
    wide_ref,
    neighbour_ref,
    diag_ref,
    right_ref,
    dissipation_ref,
    omega_ref,
    error_ref,
    lower_ref,
    upper_ref,
    spaced_ref,
):
    def plane(p, carry):
        total = own_terms(wide_ref, right_ref, dissipation_ref, omega_ref, p)
        add_blocks(
            total,
            [
                (diag_ref, (), WIDTH),
                (neighbour_ref, (0,), WIDTH - 1),
                (neighbour_ref, (1,), WIDTH + 1),
            ],
            wide_ref,
            p,
            (lower_ref, upper_ref),
            spaced_ref,
        )
        for k, value in enumerate(total):
            error_ref[k, p] = value
        return carry

    lax.fori_loop(0, error_ref.shape[1], plane, 0)


def own_terms(wide_ref, right_ref, dissipation_ref, omega_ref, p):
    rows = wide_ref.shape[0]
    nv = rows // 2
    omega = omega_ref[p]
    spread = dissipation_ref[0, p]
    total = []
    for k in range(rows):
        other = wide_ref[(k + nv) % rows, p + WIDTH]
        turned = -omega * other if k < nv else omega * other
        far = wide_ref[k, p] + wide_ref[k, p + 2 * WIDTH]
        total.append((turned - right_ref[k, p]) + spread * far)
    return total


def add_blocks(total, sources, wide_ref, p, near_refs, spaced_ref):
    _, _, span, lanes = wide_ref.shape
    nv = len(total) // 2
    lane = lax.broadcasted_iota(jnp.int32, (span, lanes), 1)
    for j in range(nv):
        for blocks_ref, lead, at in sources:
            real = wide_ref[j, p + at]
            imag = wide_ref[nv + j, p + at]
            for i in range(nv):
                block = blocks_ref[lead + (i, j, p)].astype(jnp.float32)
                total[i] = total[i] + block * real
                total[nv + i] = total[nv + i] + block * imag
        for k in (j, nv + j):
            cells = wide_ref[k, p + WIDTH]
            if near_refs is not None:
                near_refs[0][k, p] = pltpu.roll(cells, 1, axis=1)
                near_refs[1][k, p] = pltpu.roll(cells, lanes - 1, axis=1)
            if spaced_ref is not None:
                low = jnp.where(lane < WIDTH, 0.0, pltpu.roll(cells, 2, axis=1))
                high = pltpu.roll(cells, lanes - 2, axis=1)
                spaced_ref[k, p] = low + jnp.where(lane >= lanes - WIDTH, 0.0, high)


def first_axial_kernel(
    error_in_ref,
    even_ref,
    odd_ref,
    lower_ref,
    upper_ref,
    spaced_ref,
    neighbour_ref,
    dissipation_ref,
    phase_ref,
    neighbour_hbm,
    error_ref,
    span_ref,
    turn_ref,
    axial_buf,
    sem,
):
    later = pltpu.make_async_copy(neighbour_hbm.at[2:4], span_ref, sem)
    later.start()
    angle = jnp.full(turn_ref.shape[1:], phase_ref[0], jnp.float32)
    cosine = jnp.cos(angle)
    sine_part = jnp.sin(angle)
    pitch_at = lax.axis_index("pitch")
    first = pitch_at == 0
    last = pitch_at == lax.axis_size("pitch") - 1
    turn_ref[0] = jnp.where(first, cosine, 1.0)
    turn_ref[1] = jnp.where(first, -sine_part, 0.0)
    turn_ref[2] = jnp.where(last, cosine, 1.0)
    turn_ref[3] = jnp.where(last, sine_part, 0.0)
    axial_sweep(
        even_ref,
        odd_ref,
        lower_ref,
        upper_ref,
        spaced_ref,
        neighbour_ref,
        dissipation_ref,
        error_ref,
        axial_buf,
    )
    later.wait()


def axial_kernel(error_in_ref, *refs):
    axial_sweep(*refs)


def axial_sweep(
    even_ref,
    odd_ref,
    lower_ref,
    upper_ref,
    spaced_ref,
    neighbour_ref,
    dissipation_ref,
    error_ref,
    axial_buf,
):
    rows, planes, span, lanes = error_ref.shape
    nv = rows // 2
    axial_even = lax.axis_index("axial") % 2 == 0
    axial_alone = alone("axial")
    lane = lax.broadcasted_iota(jnp.int32, (span, lanes), 1)
    edge = jnp.logical_or(lane < WIDTH, lane >= lanes - WIDTH)
    from_below = lane % (2 * WIDTH) >= WIDTH
    for group in range(axial_buf.shape[0]):
        at_even = even_ref[group]
        at_odd = jnp.where(axial_alone, 0.0, odd_ref[group])
        below = pltpu.roll(jnp.where(axial_even, at_odd, at_even), WIDTH, axis=1)
        above = pltpu.roll(jnp.where(axial_even, at_even, at_odd), lanes - WIDTH, axis=1)
        axial_buf[group] = jnp.where(from_below, below, above)

    def plane(p, carry):
        total = [error_ref[k, p] for k in range(rows)]
        spread = dissipation_ref[2, p]
        for j in range(nv):
            lower = []
            upper = []
            for k in (j, nv + j):
                group, base = lane_place(k, planes, lanes)
                packed = axial_buf[group]
                shift = lanes - WIDTH - 2 * WIDTH * base - 2 * WIDTH * p
                below = pltpu.roll(packed, shift - 1, axis=1)
                above = pltpu.roll(packed, shift + 1, axis=1)
                beyond = pltpu.roll(packed, shift, axis=1)
                lower.append(jnp.where(lane < 1, below, lower_ref[k, p]))
                upper.append(jnp.where(lane >= lanes - 1, above, upper_ref[k, p]))
                far = spaced_ref[k, p] + jnp.where(edge, beyond, 0.0)
                total[k] = total[k] + spread * far
            for side, moved in enumerate((lower, upper)):
                for i in range(nv):
                    block = neighbour_ref[side, i, j, p].astype(jnp.float32)
                    total[i] = total[i] + block * moved[0]
                    total[nv + i] = total[nv + i] + block * moved[1]
        for k in range(rows):
            error_ref[k, p] = total[k]
        return carry

    lax.fori_loop(0, planes, plane, 0)


def span_sweep(
    even_ref,
    odd_ref,
    neighbour_ref,
    dissipation_ref,
    step_ref,
    wide_ref,
    error_ref,
    square_ref,
    span_buf,
    count,
    plane_of,
    after=None,
):
    rows, planes, span, _ = error_ref.shape
    nv = rows // 2
    span_even = lax.axis_index("span") % 2 == 0
    span_alone = alone("span")
    square_ref[...] = jnp.zeros_like(square_ref)

    def plane(at, carry):
        p = plane_of(at)
        for k in range(rows):
            at_even = even_ref[k, p]
            at_odd = jnp.where(span_alone, 0.0, odd_ref[k, p])
            span_buf[k, PAD - WIDTH : PAD] = jnp.where(span_even, at_odd, at_even)
            span_buf[k, PAD : PAD + span] = wide_ref[k, p + WIDTH]
            span_buf[k, PAD + span : PAD + span + WIDTH] = jnp.where(span_even, at_even, at_odd)

        def moved(k, by):
            return span_buf[k, PAD + by : PAD + by + span]

        spread = dissipation_ref[1, p]
        total = [
            error_ref[k, p] + spread * (moved(k, -WIDTH) + moved(k, WIDTH)) for k in range(rows)
        ]
        for j in range(nv):
            for side, by in enumerate((-1, 1)):
                real = moved(j, by)
                imag = moved(nv + j, by)
                for i in range(nv):
                    block = neighbour_ref[side, i, j, p].astype(jnp.float32)
                    total[i] = total[i] + block * real
                    total[nv + i] = total[nv + i] + block * imag
        step = step_ref[p]
        square = None
        for k in range(rows):
            error = total[k]
            error_ref[k, p] = error
            wide_ref[k, p + WIDTH] = wide_ref[k, p + WIDTH] - step * error
            square = error * error if square is None else square + error * error
        inner = jnp.logical_and(p >= WIDTH, p < planes - WIDTH)
        square_ref[...] += jnp.where(inner, square, 0.0)
        if after is not None:
            after(at)
        return carry

    lax.fori_loop(0, count, plane, 0)


def last_span_kernel(wide_in_ref, error_in_ref, *refs):
    planes = error_in_ref.shape[1]
    *args, wide_ref, error_ref, square_ref, out_ref, span_buf, sem = refs
    inner = planes - 2 * WIDTH
    copy = pltpu.make_async_copy(
        wide_ref.at[:, 2 * WIDTH : planes], out_ref.at[:, WIDTH : planes - WIDTH], sem
    )

    def plane_of(at):
        rim = at - inner
        return jnp.where(
            rim < 0, at + WIDTH, jnp.where(rim < WIDTH, rim, rim + planes - 2 * WIDTH)
        )

    def after(at):
        @pl.when(at == inner - 1)
        def _():
            copy.start()

    span_sweep(*args, wide_ref, error_ref, square_ref, span_buf, planes, plane_of, after)
    copy.wait()


def span_rim_kernel(wide_in_ref, error_in_ref, *refs):
    planes = error_in_ref.shape[1]
    span_sweep(
        *refs,
        2 * WIDTH,
        lambda at: jnp.where(at < WIDTH, at, at + planes - 2 * WIDTH),
    )


def span_core_kernel(
    wide_in_ref,
    error_in_ref,
    even_ref,
    odd_ref,
    neighbour_ref,
    dissipation_ref,
    step_ref,
    wide_ref,
    error_ref,
    square_ref,
    even_face_ref,
    odd_face_ref,
    axial_face_ref,
    span_buf,
):
    planes = error_ref.shape[1]
    span_sweep(
        even_ref,
        odd_ref,
        neighbour_ref,
        dissipation_ref,
        step_ref,
        wide_ref,
        error_ref,
        square_ref,
        span_buf,
        planes - 2 * WIDTH,
        lambda at: at + WIDTH,
    )
    pack_faces(wide_ref, even_face_ref, odd_face_ref, axial_face_ref)


def pitch_terms(halo_ref, turn_ref, neighbour_ref, dissipation_ref, error_ref, store):
    rows, planes, span, lanes = error_ref.shape
    nv = rows // 2
    for side in range(2):
        cosine = turn_ref[2 * side]
        sine_part = turn_ref[2 * side + 1]
        near_at, far_at = (1, 0) if side == 0 else (0, 1)
        edge, inside = (0, 1) if side == 0 else (planes - 1, planes - 2)

        def turned(j, at):
            real = halo_ref[side, j, at]
            imag = halo_ref[side, nv + j, at]
            return (cosine * real - sine_part * imag, sine_part * real + cosine * imag)

        total = [None] * rows

        def add(k, value):
            total[k] = value if total[k] is None else total[k] + value

        spread_edge = dissipation_ref[0, edge]
        spread_inside = dissipation_ref[0, inside]
        for j in range(nv):
            near = turned(j, near_at)
            far = turned(j, far_at)
            for c in range(2):
                k = c * nv + j
                add(k, spread_edge * far[c])
                store(k, inside, spread_inside * near[c])
            for i in range(nv):
                block = neighbour_ref[side, i, j, edge].astype(jnp.float32)
                for c in range(2):
                    add(c * nv + i, block * near[c])
        for k in range(rows):
            store(k, edge, total[k])


def rim_kernel(
    wide_in_ref,
    halo_ref,
    turn_ref,
    neighbour_ref,
    dissipation_ref,
    step_ref,
    error_ref,
    square_in_ref,
    wide_ref,
    faces_ref,
    square_ref,
):
    planes = error_ref.shape[1]
    square_ref[...] = square_in_ref[...]

    def store(k, p, change):
        value = wide_ref[k, p + WIDTH] - step_ref[p] * change
        wide_ref[k, p + WIDTH] = value
        if p < WIDTH:
            faces_ref[1, k, p] = value
        else:
            faces_ref[0, k, p - (planes - WIDTH)] = value
        error = error_ref[k, p] + change
        square_ref[...] += error * error

    pitch_terms(halo_ref, turn_ref, neighbour_ref, dissipation_ref, error_ref, store)


def last_kernel(
    wide_ref,
    halo_ref,
    turn_ref,
    neighbour_ref,
    dissipation_ref,
    step_ref,
    error_ref,
    square_in_ref,
    rim_square_ref,
    core_square_ref,
    rim_ref,
    share_ref,
    square_buf,
):
    planes = error_ref.shape[1]
    lanes = share_ref.shape[2]
    square_buf[...] = square_in_ref[...]

    def store(k, p, change):
        at = p if p < WIDTH else p - (planes - 2 * WIDTH)
        rim_ref[k, at] = wide_ref[k, p + WIDTH] - step_ref[p] * change
        error = error_ref[k, p] + change
        square_buf[...] += error * error

    pitch_terms(halo_ref, turn_ref, neighbour_ref, dissipation_ref, error_ref, store)
    lane = lax.broadcasted_iota(jnp.int32, (1, lanes), 1)
    first = jnp.sum(rim_square_ref[...] + core_square_ref[...], axis=0, keepdims=True)
    second = jnp.sum(square_buf[...], axis=0, keepdims=True)
    half = lanes // 2
    folded = jnp.where(
        lane < half,
        first + pltpu.roll(first, half, axis=1),
        second + pltpu.roll(second, half, axis=1),
    )
    share_ref[...] = jnp.broadcast_to(folded[None], share_ref.shape)


def close_kernel(cell_count, out_in_ref, rim_ref, share_ref, out_ref, norm_ref, norm_buf, sems):
    planes = out_ref.shape[1]
    lanes = share_ref.shape[2]
    copies = [
        pltpu.make_async_copy(rim_ref.at[:, 0:WIDTH], out_ref.at[:, 0:WIDTH], sems.at[0]),
        pltpu.make_async_copy(
            rim_ref.at[:, WIDTH : 2 * WIDTH], out_ref.at[:, planes - WIDTH : planes], sems.at[1]
        ),
    ]
    for copy in copies:
        copy.start()
    lane = lax.broadcasted_iota(jnp.int32, (1, lanes), 1)
    row = jnp.sum(share_ref[...], axis=0)
    first = jnp.sum(jnp.where(lane < lanes // 2, row, 0.0), axis=1, keepdims=True)
    second = jnp.sum(jnp.where(lane < lanes // 2, 0.0, row), axis=1, keepdims=True)
    norms = jnp.sqrt(jnp.where(lane == 0, first, second) / cell_count)
    norm_ref[...] = norms[0, 0:ITERS]
    for copy in copies:
        copy.wait()


def body(
    guess, right_side, diag_block, neighbour_blocks, dissipation, omega_volume, pseudo_step, phase
):
    parts, nv, planes, span, lanes = guess.shape
    rows = parts * nv
    pitch_count = lax.axis_size("pitch")
    devices = pitch_count * lax.axis_size("span") * lax.axis_size("axial")
    wide = (rows, planes + 2 * WIDTH, span, lanes)
    block = (rows, planes, span, lanes)
    tile = (span, lanes)
    face_shapes = (
        kept((2, rows, WIDTH, span, lanes)),
        kept((rows, planes, WIDTH, lanes)),
        kept((rows, planes, WIDTH, lanes)),
        kept((lane_groups(rows, planes, lanes), span, lanes)),
    )
    groups = GROUPS if planes % GROUPS == 0 else 1
    dma = pltpu.SemaphoreType.DMA

    def exchange_pitch(faces):
        up = [(i, (i + 1) % pitch_count) for i in range(pitch_count)]
        down = [(j, i) for i, j in up]
        if sorted(up) == sorted(down):
            return lax.ppermute(faces, "pitch", up)
        return jnp.stack(
            [lax.ppermute(faces[0], "pitch", up), lax.ppermute(faces[1], "pitch", down)]
        )

    span_count = lax.axis_size("span")
    axial_count = lax.axis_size("axial")

    def span_swap(values, start):
        partner = {}
        for i in range(start, span_count - 1, 2):
            partner.update({i: i + 1, i + 1: i})
        pairs = []
        for i in range(span_count):
            for j in range(axial_count):
                if i in partner:
                    pairs.append((i * axial_count + j, partner[i] * axial_count + j))
                elif axial_count % 2 == 0:
                    pairs.append((i * axial_count + j, i * axial_count + (j ^ 1)))
        return resident(lax.ppermute(values, ("span", "axial"), pairs))

    def axial_swap(values, start):
        pairs = [(i, i + 1) for i in range(start, axial_count - 1, 2)]
        if start == 1 and axial_count % 2 == 0:
            pairs.append((0, axial_count - 1))
        return resident(lax.ppermute(values, "axial", pairs + [(j, i) for i, j in pairs]))

    def exchange_rest(even, odd, axial):
        return (
            span_swap(even, 0),
            span_swap(odd, 1),
            axial_swap(axial, 0),
            axial_swap(axial, 1),
        )

    neighbour_blocks = outside(neighbour_blocks)
    sources = (right_side.reshape(block), dissipation, omega_volume, pseudo_step, diag_block)
    guess = outside(guess.reshape(block))
    (faces,) = call(faces_kernel, "pitch_faces", face_shapes[:1], [ANY], [dma((2,))])(guess)
    state, even, odd, axial, right, dissipation, omega, step, diag = call(
        open_kernel,
        "open",
        (kept(wide),)
        + face_shapes[1:]
        + tuple(kept(c.shape, c.dtype) for c in sources),
        [ANY] * 6,
        [dma((6,))],
    )(guess, *[outside(c) for c in sources])

    axial_buf = [pltpu.VMEM(face_shapes[3].shape, jnp.float32)]
    span_buf = [pltpu.VMEM((rows, span + 2 * PAD, lanes), jnp.float32)]
    pair = kept((2,) + neighbour_blocks.shape[1:], neighbour_blocks.dtype)
    sweep = (kept(wide), kept(block), kept(tile))
    for iteration in range(ITERS):
        halo = resident(exchange_pitch(faces))
        span_even, span_odd, axial_even, axial_odd = exchange_rest(even, odd, axial)
        if iteration == 0:
            error, *shifts, near_blocks, axial_blocks = call(
                near_loading_kernel,
                "first_near",
                (kept(block),) * 4 + (pair, pair),
                [VMEM, ANY] + [VMEM] * 4,
                [dma((1, groups)), dma],
            )(state, neighbour_blocks, diag, right, dissipation, omega)
            error, span_blocks, turn = call(
                first_axial_kernel,
                "first_axial",
                (kept(block), pair, kept((4,) + tile)),
                [VMEM] * 8 + [SMEM, ANY],
                axial_buf + [dma],
                {0: 0},
            )(
                error,
                axial_even,
                axial_odd,
                *shifts,
                axial_blocks,
                dissipation,
                phase,
                neighbour_blocks,
            )
        else:
            error, *shifts = call(near_kernel, "near", (kept(block),) * 4, [VMEM] * 6)(
                state, near_blocks, diag, right, dissipation, omega
            )
            (error,) = call(axial_kernel, "axial", (kept(block),), [VMEM] * 8, axial_buf, {0: 0})(
                error, axial_even, axial_odd, *shifts, axial_blocks, dissipation
            )
        rest = (span_even, span_odd, span_blocks, dissipation, step)
        terms = (halo, turn, near_blocks, dissipation, step)
        if iteration < ITERS - 1:
            state, error, square = call(
                span_rim_kernel, "span_rim", sweep, [VMEM] * 7, span_buf, {0: 0, 1: 1}
            )(state, error, *rest)
            state, faces, rim_square = call(
                rim_kernel,
                "pitch_terms",
                (kept(wide), face_shapes[0], kept(tile)),
                [VMEM] * 8,
                aliases={0: 0},
            )(state, *terms, error, square)
            state, _, core_square, even, odd, axial = call(
                span_core_kernel,
                "span_core",
                sweep + face_shapes[1:],
                [VMEM] * 7,
                span_buf,
                {0: 0, 1: 1},
            )(state, error, *rest)
        else:
            state, error, square, out = call(
                last_span_kernel,
                "span",
                sweep + (jax.ShapeDtypeStruct(block, jnp.float32),),
                [VMEM] * 7,
                span_buf + [dma],
                {0: 0, 1: 1},
                (VMEM,) * 3 + (ANY,),
            )(state, error, *rest)
            rim, share = call(
                last_kernel,
                "last_pitch_terms",
                (kept((rows, 2 * WIDTH, span, lanes)), kept((devices, 1, lanes))),
                [VMEM] * 10,
                [pltpu.VMEM(tile, jnp.float32)],
            )(state, *terms, error, square, rim_square, core_square)
    shares = lax.all_to_all(share, ("pitch", "span", "axial"), 0, 0, tiled=True)
    cell_count = float(rows * planes * span * lanes * devices)
    out, norms = call(
        functools.partial(close_kernel, cell_count),
        "close",
        (
            jax.ShapeDtypeStruct(block, jnp.float32),
            jax.ShapeDtypeStruct((ITERS,), jnp.float32),
        ),
        [ANY, VMEM, VMEM],
        [pltpu.VMEM((1, lanes), jnp.float32), dma((3,))],
        {0: 0},
        (ANY, VMEM),
    )(out, rim, resident(shares))
    return (out.reshape(parts, nv, planes, span, lanes), norms)


def solution(mesh):
    placed = (
        P(None, None, "pitch", "span", "axial"),
        P(None, None, "pitch", "span", "axial"),
        P(None, None, "pitch", "span", "axial"),
        P(None, None, None, "pitch", "span", "axial"),
        P(None, "pitch", "span", "axial"),
        P("pitch", "span", "axial"),
        P("pitch", "span", "axial"),
        P(),
    )
    return jax.shard_map(
        body,
        mesh=mesh,
        in_specs=placed,
        out_specs=(P(None, None, "pitch", "span", "axial"), P()),
        check_vma=False,
    )
```

time: 40.2 us -> 39.2 us (0.975)
  blocking collectives: 0 us -> 9.95 us
  waiting for transfers between devices: 8.66 us -> 1.37 us
  starting transfers between devices: 14.3 us -> 10.7 us
  Pallas kernels: 14.1 us -> 15.5 us
  local copies, waits for them, and re-layouts: 0.88 us -> 0 us
  other arithmetic: 0.57 us -> 0 us
    all_to_all x0 -> x1, blocking collectives: none -> 9.95 us  [body(): shares = lax.all_to_all(share, ('pitch', 'span', 'axial'), 0, 0, tiled=True)]
    all_to_all x1 -> x0, waiting for transfers between devices: 6.27 us -> none  [body(): shares = lax.all_to_all(share, ('pitch', 'span', 'axial'), 0, 0, tiled=True)]
    all_to_all x1 -> x0, starting transfers between devices: 3.72 us -> none  [body(): shares = lax.all_to_all(share, ('pitch', 'span', 'axial'), 0, 0, tiled=True)]
    pallas_call x7 -> x12, Pallas kernels: 14.1 us -> 15.5 us  [the longest x1 2.64 us: body(): call(near_loading_kernel, 'first_near', (kept(block),) * 4 + (pair, pair)...]
    ppermute x2, waiting for transfers between devices: 1.04 us -> 0.01 us  [exchange_pitch(): return lax.ppermute(faces, 'pitch', up)]
    unnamed x1 -> x0, local copies, waits for them, and re-layouts: 0.88 us -> none
    ppermute x4, starting transfers between devices: 4.3 us -> 4.86 us  [span_swap(): return resident(lax.ppermute(values, ('span', 'axial'), pairs))]
    sqrt x1 -> x0, other arithmetic: 0.52 us -> none  [body(): norms = jnp.sqrt(totals / cell_count)]
  transfers between devices with their start and end apart: 11 -> 10, of which waited for: 3 -> 1; matrix products, arithmetic and copies ran while one was open for 2% -> 0% of each run, Pallas kernels for 27% -> 33%
where the time goes in v5:
time: 39.2 us; the launch traced here: 39 us
  Pallas kernels  15.5 us (40%)
  starting transfers between devices  10.7 us (27%)
  blocking collectives  9.95 us (25%)
  between operations  1.43 us (4%)
  waiting for transfers between devices  1.37 us (3%)
    all_to_all x1, blocking collectives, body(): shares = lax.all_to_all(share, ('pitch', 'span', 'axial'), 0, 0, tiled=True)  9.95 us
    ppermute x4, starting transfers between devices, span_swap(): return resident(lax.ppermute(values, ('span', 'axial'), pairs))  4.86 us
    ppermute x2, starting transfers between devices, exchange_pitch(): return lax.ppermute(faces, 'pitch', up)  3.6 us
    pallas_call x1, Pallas kernels, body(): call(near_loading_kernel, 'first_near', (kept(block),) * 4 + (pair, pair)...  2.64 us
    ppermute x4, starting transfers between devices, axial_swap(): lax.ppermute(values, 'axial', pairs + [(j, i) for i, j in pairs])  2.26 us
    pallas_call x1, Pallas kernels, body(): call(open_kernel, 'open', (kept(wide),) + face_shapes[1:] + tuple((kept(c...  1.9 us
    pallas_call x1, Pallas kernels, body(): call(near_kernel, 'near', (kept(block),) * 4, [VMEM] * 6)  1.83 us
    pallas_call x1, Pallas kernels, body(): call(first_axial_kernel, 'first_axial', (kept(block), pair, kept((4,) + t...  1.73 us
  transfers between devices with their start and end apart: 10, of which 1 were waited for; matrix products, arithmetic and copies ran while one was open for 0% of the time, Pallas kernels for 33%

profile of v5, /device:TPU:0, one launch (start us, length us, event | category | flops | bytes accessed | tf_op | source)
XLA Modules:
  0.0 39.0 jit_solution(18417703053452381625)
XLA Ops:
  0.6 1.0 %pitch_faces.1 = f32[2,12,2,16,128]{4,3,2,1,0:T(8,128)S(1)} custom-call(f32[12,8,16,128]{3,2,1,0:T(8,128)} %bitcast.3), custom_call_target="tpu_custom_call" | custom-call | tf_op jit(solution)/shard_map/pitch_faces/pallas_call | solution.py:703
  1.7 3.0 %collective-permute-start.4 = (f32[2,12,2,16,128]{4,3,2,1,0:T(8,128)S(1)}, f32[2,12,2,16,128]{4,3,2,1,0:T(8,128)S(1)}, u32[]{:S(2)}, u32[]{:S(2)}) collective-permute-start(f32[2,12,2,16,128]{4,3,2,1,0:T(8,128)S(1)} %pitch_faces.1), channel_id=1, source_target_pairs={{0,16},{16,0},{1,17},{17,1},{2,18},{18,2},{3,19},{19,3},{4,20},{20... | collective-permute-start | bytes 1179656 | tf_op jit(solution)/shard_map/ppermute | solution.py:665
  4.7 1.9 %open.1 = (f32[12,12,16,128]{3,2,1,0:T(8,128)S(1)}, f32[12,8,2,128]{3,2,1,0:T(2,128)S(1)}, f32[12,8,2,128]{3,2,1,0:T(2,128)S(1)}, f32[3,16,128]{2,1,0:T(8,128)S(...) custom-call(f32[12,8,16,128]{3,2,1,0:T(8,128)} %bitcast.4, ...), custom_call_target="tpu_custom_call" | custom-call | tf_op jit(solution)/shard_map/open/pallas_call | solution.py:704
  6.6 1.6 %collective-permute-start.2 = (f32[12,8,2,128]{3,2,1,0:T(2,128)S(1)}, f32[12,8,2,128]{3,2,1,0:T(2,128)S(1)}, u32[]{:S(2)}, u32[]{:S(2)}) collective-permute-start(f32[12,8,2,128]{3,2,1,0:T(2,128)S(1)} %get-tuple-element.55), channel_id=1, source_target_pairs={{0,4},{1,5},{2,6},{3,7},{4,0},{5,1},{6,2},{7,3},{8,12},{9,13},{10,... | collective-permute-start | bytes 294920 | tf_op jit(solution)/shard_map/ppermute | solution.py:684
  8.3 0.0 collective-permute-start.3
  8.3 0.5 %collective-permute-start = (f32[3,16,128]{2,1,0:T(8,128)S(1)}, f32[3,16,128]{2,1,0:T(8,128)S(1)}, u32[]{:S(2)}, u32[]{:S(2)}) collective-permute-start(f32[3,16,128]{2,1,0:T(8,128)S(1)} %get-tuple-element.49), channel_id=1, source_target_pairs={{0,1},{2,3},{1,0},{3,2},{4,5},{6,7},{5,4},{7,6},{8,9},{10,11},{9,8... | collective-permute-start | bytes 73736 | tf_op jit(solution)/shard_map/ppermute | solution.py:690
  8.8 1.1 %collective-permute-start.1 = (f32[3,16,128]{2,1,0:T(8,128)S(1)}, f32[3,16,128]{2,1,0:T(8,128)S(1)}, u32[]{:S(2)}, u32[]{:S(2)}) collective-permute-start(f32[3,16,128]{2,1,0:T(8,128)S(1)} %get-tuple-element.49), channel_id=1, source_target_pairs={{1,2},{0,3},{2,1},{3,0},{5,6},{4,7},{6,5},{7,4},{9,10},{8,11},{10,... | collective-permute-start | bytes 73736 | tf_op jit(solution)/shard_map/ppermute | solution.py:690
  10.5 2.6 %first_near.1 = (f32[12,8,16,128]{3,2,1,0:T(8,128)S(1)}, f32[12,8,16,128]{3,2,1,0:T(8,128)S(1)}, f32[12,8,16,128]{3,2,1,0:T(8,128)S(1)}, f32[12,8,16,128]{3,2,1,...) custom-call(f32[12,12,16,128]{3,2,1,0:T(8,128)S(1)} %get-tuple-element.43.wide_ref., ...), custom_call_target="tpu_custom_call" | custom-call | tf_op jit(solution)/shard_map/first_near/pallas_call | solution.py:722
  13.2 0.0 collective-permute-done.1.odd_ref
  13.2 1.7 %first_axial.1 = (f32[12,8,16,128]{3,2,1,0:T(8,128)S(1)}, bf16[2,6,6,8,16,128]{5,4,3,2,1,0:T(8,128)(2,1)S(1)}, f32[4,16,128]{2,1,0:T(8,128)S(1)}) custom-call(f32[12,8,16,128]{3,2,1,0:T(8,128)S(1)} %get-tuple-element.48.error_in_ref, f32[3,16,128]{2,1,0:T(8,128)S(1)} %collective-permute-done.even_ref, ...), custom_call_target="tpu_custom_call", output_to_operand_aliasing={{0}: (0, {})} | custom-call | tf_op jit(solution)/shard_map/first_axial/pallas_call | solution.py:729
  14.9 0.6 %span_rim.1 = (f32[12,12,16,128]{3,2,1,0:T(8,128)S(1)}, f32[12,8,16,128]{3,2,1,0:T(8,128)S(1)}, f32[16,128]{1,0:T(8,128)S(1)}) custom-call(f32[12,12,16,128]{3,2,1,0:T(8,128)S(1)} %get-tuple-element.43.wide_ref.wide_in_ref, f32[12,8,16,128]{3,2,1,0:T(8,128)S(1)} %get-tuple-element.54.error_in_ref, ...), custom_call_target="tpu_custom_call", output_to_operand_aliasing={{0}: (0, {}), {1}: (1, {})} | custom-call | tf_op jit(solution)/shard_map/span_rim/pallas_call | solution.py:756
  15.6 0.2 pitch_terms.1
  15.8 0.6 %collective-permute-start.9 = (f32[2,12,2,16,128]{4,3,2,1,0:T(8,128)S(1)}, f32[2,12,2,16,128]{4,3,2,1,0:T(8,128)S(1)}, u32[]{:S(2)}, u32[]{:S(2)}) collective-permute-start(f32[2,12,2,16,128]{4,3,2,1,0:T(8,128)S(1)} %get-tuple-element.75), channel_id=1, source_target_pairs={{0,16},{16,0},{1,17},{17,1},{2,18},{18,2},{3,19},{19,3},{4,20},{20... | collective-permute-start | bytes 1179656 | tf_op jit(solution)/shard_map/ppermute | solution.py:665
  16.4 0.9 %span_core.1 = (f32[12,12,16,128]{3,2,1,0:T(8,128)S(1)}, f32[12,8,16,128]{3,2,1,0:T(8,128)S(1)}, f32[16,128]{1,0:T(8,128)S(1)}, f32[12,8,2,128]{3,2,1,0:T(2,128)...) custom-call(f32[12,12,16,128]{3,2,1,0:T(8,128)S(1)} %get-tuple-eleme, ...), custom_call_target="tpu_custom_call", output_to_operand_aliasing={{0}: (0, {}), {1}: (1, {})} | custom-call | tf_op jit(solution)/shard_map/span_core/pallas_call | solution.py:766
  17.3 3.2 %collective-permute-start.7 = (f32[12,8,2,128]{3,2,1,0:T(2,128)S(1)}, f32[12,8,2,128]{3,2,1,0:T(2,128)S(1)}, u32[]{:S(2)}, u32[]{:S(2)}) collective-permute-start(f32[12,8,2,128]{3,2,1,0:T(2,128)S(1)} %get-tuple-element.71), channel_id=1, source_target_pairs={{0,4},{1,5},{2,6},{3,7},{4,0},{5,1},{6,2},{7,3},{8,12},{9,13},{10,... | collective-permute-start | bytes 294920 | tf_op jit(solution)/shard_map/ppermute | solution.py:684
  20.5 0.5 %collective-permute-start.5 = (f32[3,16,128]{2,1,0:T(8,128)S(1)}, f32[3,16,128]{2,1,0:T(8,128)S(1)}, u32[]{:S(2)}, u32[]{:S(2)}) collective-permute-start(f32[3,16,128]{2,1,0:T(8,128)S(1)} %get-tuple-element.67), channel_id=1, source_target_pairs={{0,1},{2,3},{1,0},{3,2},{4,5},{6,7},{5,4},{7,6},{8,9},{10,11},{9,8... | collective-permute-start | bytes 73736 | tf_op jit(solution)/shard_map/ppermute | solution.py:690
  21.0 0.1 collective-permute-start.6
  21.2 1.8 %near.1 = (f32[12,8,16,128]{3,2,1,0:T(8,128)S(1)}, f32[12,8,16,128]{3,2,1,0:T(8,128)S(1)}, f32[12,8,16,128]{3,2,1,0:T(8,128)S(1)}, f32[12,8,16,128]{3,2,1,0:T(8,128)S(1)}) custom-call(f32[12,12,16,128]{3,2,1,0:T(8,128)S(1)} %get-tuple-element.65.wide_ref.wide_in_ref, bf16[2,6,6,8,16,128]{5,4,3,2,1,0:T(8,128)(2,1)S(1)} %get-tuple-element.61.neighbour_ref, ...), custom_call_target="tpu_custom_call" | custom-call | tf_op jit(solution)/shard_map/near/pallas_call | solution.py:747
  23.0 1.3 %collective-permute-done.6.refs_1_ = f32[3,16,128]{2,1,0:T(8,128)S(1)} collective-permute-done((f32[3,16,128]{2,1,0:T(8,128)S(1)}, f32[3,16,128]{2,1,0:T(8,128)S(1)}, u32[]{:S(2)}, u32[]{:S(2)}) %collective-permute-start.6) | collective-permute-done | bytes 24608 | tf_op jit(solution)/shard_map/ppermute | solution.py:690
  24.4 1.7 %axial.1.error_in_ref = f32[12,8,16,128]{3,2,1,0:T(8,128)S(1)} custom-call(f32[12,8,16,128]{3,2,1,0:T(8,128)S(1)} %get-tuple-element.66.error_in_ref, f32[3,16,128]{2,1,0:T(8,128)S(1)} %collective-permute-done.5.refs_0_, f32[3,16,128]{2,1,0:T(8,128)S(1)} %collective-permute-done.6.refs_1_, ...), custom_call_target="tpu_custom_call", output_to_operand_aliasing={{}: (0, {})} | custom-call | tf_op jit(solution)/shard_map/axial/pallas_call | solution.py:750
  26.1 1.4 %span.1 = (f32[12,12,16,128]{3,2,1,0:T(8,128)S(1)}, f32[12,8,16,128]{3,2,1,0:T(8,128)S(1)}, f32[16,128]{1,0:T(8,128)S(1)}, f32[12,8,16,128]{3,2,1,0:T(8,128)}) custom-call(f32[12,12,16,128]{3,2,1,0:T(8,128)S(1)} %get-tuple-element.65.wide_ref.wide_in_ref, f32[12,8,16,128]{3,2,1,0:T(8,128)S(1)} %axial.1.error_in_ref, ...), custom_call_target="tpu_custom_call", output_to_operand_aliasing={{0}: (0, {}), {1}: (1, {})} | custom-call | tf_op jit(solution)/shard_map/span/pallas_call | solution.py:775
  27.5 0.3 last_pitch_terms.1
  27.8 10.0 %all_to_all.5.share_ref = f32[32,1,128]{2,1,0:T(1,128)S(1)} all-to-all(f32[32,1,128]{2,1,0:T(1,128)S(1)} %get-tuple-element.81), channel_id=1, replica_groups=mesh['pitch'=2,'span'=4,'axial'=4] {'pitch','span','axial'}, dimensions={0} | all-to-all | bytes 32768 | tf_op jit(solution)/shard_map/all_to_all | solution.py:791
  37.7 1.3 %close.1 = (f32[12,8,16,128]{3,2,1,0:T(8,128)}, f32[2]{0:T(128)}) custom-call(f32[12,8,16,128]{3,2,1,0:T(8,128)} %get-tuple-element.73.out_in_ref, f32[12,4,16,128]{3,2,1,0:T(8,128)S(1)} %get-tuple-element.80.rim_ref, f32[32,1,128]{2,1,0:T(1,128)S(1)} %all_to_all.5.share_ref), custom_call_target="tpu_custom_call", output_to_operand_aliasing={{0}: (0, {})} | custom-call | tf_op jit(solution)/shard_map/close/pallas_call | solution.py:793
  (9 shorter events, 0.0 us)
Async XLA Ops:
  1.7 13.9 %collective-permute-start.4 = (f32[2,12,2,16,128]{4,3,2,1,0:T(8,128)S(1)}, f32[2,12,2,16,128]{4,3,2,1,0:T(8,128)S(1)}, u32[]{:S(2)}, u32[]{:S(2)}) collective-permute-start(f32[2,12,2,16,128]{4,3,2,1,0:T(8,128)S(1)} %pitch_faces.1), channel_id=1, source_target_pairs={{0,16},{16,0},{1,17},{17,1},{2,18},{18,2},{3,19},{19,3},{4,20},{20... | collective-permute-start | bytes 1179656 | tf_op jit(solution)/shard_map/ppermute | solution.py:665
  6.6 8.3 %collective-permute-start.2 = (f32[12,8,2,128]{3,2,1,0:T(2,128)S(1)}, f32[12,8,2,128]{3,2,1,0:T(2,128)S(1)}, u32[]{:S(2)}, u32[]{:S(2)}) collective-permute-start(f32[12,8,2,128]{3,2,1,0:T(2,128)S(1)} %get-tuple-element.55), channel_id=1, source_target_pairs={{0,4},{1,5},{2,6},{3,7},{4,0},{5,1},{6,2},{7,3},{8,12},{9,13},{10,... | collective-permute-start | bytes 294920 | tf_op jit(solution)/shard_map/ppermute | solution.py:684
  8.3 6.7 %collective-permute-start.3 = (f32[12,8,2,128]{3,2,1,0:T(2,128)S(1)}, f32[12,8,2,128]{3,2,1,0:T(2,128)S(1)}, u32[]{:S(2)}, u32[]{:S(2)}) collective-permute-start(f32[12,8,2,128]{3,2,1,0:T(2,128)S(1)} %get-tuple-element.56), channel_id=1, source_target_pairs={{0,1},{1,0},{2,3},{3,2},{4,8},{5,9},{6,10},{7,11},{8,4},{9,5},{10,... | collective-permute-start | bytes 294920 | tf_op jit(solution)/shard_map/ppermute | solution.py:684
  8.3 4.9 %collective-permute-start = (f32[3,16,128]{2,1,0:T(8,128)S(1)}, f32[3,16,128]{2,1,0:T(8,128)S(1)}, u32[]{:S(2)}, u32[]{:S(2)}) collective-permute-start(f32[3,16,128]{2,1,0:T(8,128)S(1)} %get-tuple-element.49), channel_id=1, source_target_pairs={{0,1},{2,3},{1,0},{3,2},{4,5},{6,7},{5,4},{7,6},{8,9},{10,11},{9,8... | collective-permute-start | bytes 73736 | tf_op jit(solution)/shard_map/ppermute | solution.py:690
  8.8 4.4 %collective-permute-start.1 = (f32[3,16,128]{2,1,0:T(8,128)S(1)}, f32[3,16,128]{2,1,0:T(8,128)S(1)}, u32[]{:S(2)}, u32[]{:S(2)}) collective-permute-start(f32[3,16,128]{2,1,0:T(8,128)S(1)} %get-tuple-element.49), channel_id=1, source_target_pairs={{1,2},{0,3},{2,1},{3,0},{5,6},{4,7},{6,5},{7,4},{9,10},{8,11},{10,... | collective-permute-start | bytes 73736 | tf_op jit(solution)/shard_map/ppermute | solution.py:690
  15.8 11.7 %collective-permute-start.9 = (f32[2,12,2,16,128]{4,3,2,1,0:T(8,128)S(1)}, f32[2,12,2,16,128]{4,3,2,1,0:T(8,128)S(1)}, u32[]{:S(2)}, u32[]{:S(2)}) collective-permute-start(f32[2,12,2,16,128]{4,3,2,1,0:T(8,128)S(1)} %get-tuple-element.75), channel_id=1, source_target_pairs={{0,16},{16,0},{1,17},{17,1},{2,18},{18,2},{3,19},{19,3},{4,20},{20... | collective-permute-start | bytes 1179656 | tf_op jit(solution)/shard_map/ppermute | solution.py:665
  17.3 8.8 %collective-permute-start.7 = (f32[12,8,2,128]{3,2,1,0:T(2,128)S(1)}, f32[12,8,2,128]{3,2,1,0:T(2,128)S(1)}, u32[]{:S(2)}, u32[]{:S(2)}) collective-permute-start(f32[12,8,2,128]{3,2,1,0:T(2,128)S(1)} %get-tuple-element.71), channel_id=1, source_target_pairs={{0,4},{1,5},{2,6},{3,7},{4,0},{5,1},{6,2},{7,3},{8,12},{9,13},{10,... | collective-permute-start | bytes 294920 | tf_op jit(solution)/shard_map/ppermute | solution.py:684
  20.5 5.6 %collective-permute-start.8 = (f32[12,8,2,128]{3,2,1,0:T(2,128)S(1)}, f32[12,8,2,128]{3,2,1,0:T(2,128)S(1)}, u32[]{:S(2)}, u32[]{:S(2)}) collective-permute-start(f32[12,8,2,128]{3,2,1,0:T(2,128)S(1)} %get-tuple-element.72), channel_id=1, source_target_pairs={{0,1},{1,0},{2,3},{3,2},{4,8},{5,9},{6,10},{7,11},{8,4},{9,5},{10,... | collective-permute-start | bytes 294920 | tf_op jit(solution)/shard_map/ppermute | solution.py:684
  20.5 2.5 %collective-permute-start.5 = (f32[3,16,128]{2,1,0:T(8,128)S(1)}, f32[3,16,128]{2,1,0:T(8,128)S(1)}, u32[]{:S(2)}, u32[]{:S(2)}) collective-permute-start(f32[3,16,128]{2,1,0:T(8,128)S(1)} %get-tuple-element.67), channel_id=1, source_target_pairs={{0,1},{2,3},{1,0},{3,2},{4,5},{6,7},{5,4},{7,6},{8,9},{10,11},{9,8... | collective-permute-start | bytes 73736 | tf_op jit(solution)/shard_map/ppermute | solution.py:690
  21.0 3.3 %collective-permute-start.6 = (f32[3,16,128]{2,1,0:T(8,128)S(1)}, f32[3,16,128]{2,1,0:T(8,128)S(1)}, u32[]{:S(2)}, u32[]{:S(2)}) collective-permute-start(f32[3,16,128]{2,1,0:T(8,128)S(1)} %get-tuple-element.67), channel_id=1, source_target_pairs={{1,2},{0,3},{2,1},{3,0},{5,6},{4,7},{6,5},{7,4},{9,10},{8,11},{10,... | collective-permute-start | bytes 73736 | tf_op jit(solution)/shard_map/ppermute | solution.py:690

commit v6 on v5

--- a/solution.py
+++ b/solution.py
@@ -391,8 +391,8 @@
 
 
 def span_sweep(
+    odd_ref,
     even_ref,
-    odd_ref,
     neighbour_ref,
     dissipation_ref,
     step_ref,
@@ -485,8 +485,8 @@
 def span_core_kernel(
     wide_in_ref,
     error_in_ref,
+    odd_ref,
     even_ref,
-    odd_ref,
     neighbour_ref,
     dissipation_ref,
     step_ref,
@@ -500,8 +500,8 @@
 ):
     planes = error_ref.shape[1]
     span_sweep(
+        odd_ref,
         even_ref,
-        odd_ref,
         neighbour_ref,
         dissipation_ref,
         step_ref,
@@ -750,7 +750,7 @@
             (error,) = call(axial_kernel, "axial", (kept(block),), [VMEM] * 8, axial_buf, {0: 0})(
                 error, axial_even, axial_odd, *shifts, axial_blocks, dissipation
             )
-        rest = (span_even, span_odd, span_blocks, dissipation, step)
+        rest = (span_odd, span_even, span_blocks, dissipation, step)
         terms = (halo, turn, near_blocks, dissipation, step)
         if iteration < ITERS - 1:
             state, error, square = call(

time: 39.2 us -> 39.1 us (level)
  blocking collectives: 9.95 us -> 8.84 us
  waiting for transfers between devices: 1.37 us -> 1.97 us
  starting transfers between devices: 10.7 us -> 11.1 us
    ppermute x2, waiting for transfers between devices: 0.01 us -> 1.52 us  [exchange_pitch(): return lax.ppermute(faces, 'pitch', up)]
    all_to_all x1, blocking collectives: 9.95 us -> 8.84 us  [body(): shares = lax.all_to_all(share, ('pitch', 'span', 'axial'), 0, 0, tiled=True)]
    ppermute x4, waiting for transfers between devices: 1.35 us -> 0.44 us  [axial_swap(): lax.ppermute(values, 'axial', pairs + [(j, i) for i, j in pairs])]
  transfers between devices with their start and end apart: 10 -> 10, of which waited for: 1 -> 2; matrix products, arithmetic and copies ran while one was open for 0% -> 0% of each run, Pallas kernels for 33% -> 33%
where the time goes in v6:
time: 39.1 us; the launch traced here: 38.9 us
  Pallas kernels  15.5 us (40%)
  starting transfers between devices  11.1 us (28%)
  blocking collectives  8.84 us (23%)
  waiting for transfers between devices  1.97 us (5%)
  between operations  1.44 us (4%)
    all_to_all x1, blocking collectives, body(): shares = lax.all_to_all(share, ('pitch', 'span', 'axial'), 0, 0, tiled=True)  8.84 us
    ppermute x4, starting transfers between devices, span_swap(): return resident(lax.ppermute(values, ('span', 'axial'), pairs))  4.92 us
    ppermute x2, starting transfers between devices, exchange_pitch(): return lax.ppermute(faces, 'pitch', up)  3.6 us
    pallas_call x1, Pallas kernels, body(): call(near_loading_kernel, 'first_near', (kept(block),) * 4 + (pair, pair)...  2.64 us
    ppermute x4, starting transfers between devices, axial_swap(): lax.ppermute(values, 'axial', pairs + [(j, i) for i, j in pairs])  2.58 us
    pallas_call x1, Pallas kernels, body(): call(open_kernel, 'open', (kept(wide),) + face_shapes[1:] + tuple((kept(c...  1.9 us
    pallas_call x1, Pallas kernels, body(): call(near_kernel, 'near', (kept(block),) * 4, [VMEM] * 6)  1.83 us
    pallas_call x1, Pallas kernels, body(): call(first_axial_kernel, 'first_axial', (kept(block), pair, kept((4,) + t...  1.73 us
  transfers between devices with their start and end apart: 10, of which 2 were waited for; matrix products, arithmetic and copies ran while one was open for 0% of the time, Pallas kernels for 33%

profile of v6, /device:TPU:0, one launch (start us, length us, event | category | flops | bytes accessed | tf_op | source)
XLA Modules:
  0.0 38.9 jit_solution(15923163692393736254)
XLA Ops:
  0.6 1.0 %pitch_faces.1 = f32[2,12,2,16,128]{4,3,2,1,0:T(8,128)S(1)} custom-call(f32[12,8,16,128]{3,2,1,0:T(8,128)} %bitcast.3), custom_call_target="tpu_custom_call" | custom-call | tf_op jit(solution)/shard_map/pitch_faces/pallas_call | solution.py:703
  1.7 3.0 %collective-permute-start.4 = (f32[2,12,2,16,128]{4,3,2,1,0:T(8,128)S(1)}, f32[2,12,2,16,128]{4,3,2,1,0:T(8,128)S(1)}, u32[]{:S(2)}, u32[]{:S(2)}) collective-permute-start(f32[2,12,2,16,128]{4,3,2,1,0:T(8,128)S(1)} %pitch_faces.1), channel_id=1, source_target_pairs={{0,16},{16,0},{1,17},{17,1},{2,18},{18,2},{3,19},{19,3},{4,20},{20... | collective-permute-start | bytes 1179656 | tf_op jit(solution)/shard_map/ppermute | solution.py:665
  4.7 1.9 %open.1 = (f32[12,12,16,128]{3,2,1,0:T(8,128)S(1)}, f32[12,8,2,128]{3,2,1,0:T(2,128)S(1)}, f32[12,8,2,128]{3,2,1,0:T(2,128)S(1)}, f32[3,16,128]{2,1,0:T(8,128)S(...) custom-call(f32[12,8,16,128]{3,2,1,0:T(8,128)} %bitcast.4, ...), custom_call_target="tpu_custom_call" | custom-call | tf_op jit(solution)/shard_map/open/pallas_call | solution.py:704
  6.6 0.1 collective-permute-start.2
  6.7 3.1 %collective-permute-start.3 = (f32[12,8,2,128]{3,2,1,0:T(2,128)S(1)}, f32[12,8,2,128]{3,2,1,0:T(2,128)S(1)}, u32[]{:S(2)}, u32[]{:S(2)}) collective-permute-start(f32[12,8,2,128]{3,2,1,0:T(2,128)S(1)} %get-tuple-element.56), channel_id=1, source_target_pairs={{0,4},{1,5},{2,6},{3,7},{4,0},{5,1},{6,2},{7,3},{8,12},{9,13},{10,... | collective-permute-start | bytes 294920 | tf_op jit(solution)/shard_map/ppermute | solution.py:684
  9.8 0.0 collective-permute-start
  9.8 1.6 %collective-permute-start.1 = (f32[3,16,128]{2,1,0:T(8,128)S(1)}, f32[3,16,128]{2,1,0:T(8,128)S(1)}, u32[]{:S(2)}, u32[]{:S(2)}) collective-permute-start(f32[3,16,128]{2,1,0:T(8,128)S(1)} %get-tuple-element.49), channel_id=1, source_target_pairs={{1,2},{0,3},{2,1},{3,0},{5,6},{4,7},{6,5},{7,4},{9,10},{8,11},{10,... | collective-permute-start | bytes 73736 | tf_op jit(solution)/shard_map/ppermute | solution.py:690
  12.1 2.6 %first_near.1 = (f32[12,8,16,128]{3,2,1,0:T(8,128)S(1)}, f32[12,8,16,128]{3,2,1,0:T(8,128)S(1)}, f32[12,8,16,128]{3,2,1,0:T(8,128)S(1)}, f32[12,8,16,128]{3,2,1,...) custom-call(f32[12,12,16,128]{3,2,1,0:T(8,128)S(1)} %get-tuple-element.43.wide_ref., ...), custom_call_target="tpu_custom_call" | custom-call | tf_op jit(solution)/shard_map/first_near/pallas_call | solution.py:722
  14.8 1.7 %first_axial.1 = (f32[12,8,16,128]{3,2,1,0:T(8,128)S(1)}, bf16[2,6,6,8,16,128]{5,4,3,2,1,0:T(8,128)(2,1)S(1)}, f32[4,16,128]{2,1,0:T(8,128)S(1)}) custom-call(f32[12,8,16,128]{3,2,1,0:T(8,128)S(1)} %get-tuple-element.48.error_in_ref, f32[3,16,128]{2,1,0:T(8,128)S(1)} %collective-permute-done.even_ref, ...), custom_call_target="tpu_custom_call", output_to_operand_aliasing={{0}: (0, {})} | custom-call | tf_op jit(solution)/shard_map/first_axial/pallas_call | solution.py:729
  16.5 0.6 %span_rim.1 = (f32[12,12,16,128]{3,2,1,0:T(8,128)S(1)}, f32[12,8,16,128]{3,2,1,0:T(8,128)S(1)}, f32[16,128]{1,0:T(8,128)S(1)}) custom-call(f32[12,12,16,128]{3,2,1,0:T(8,128)S(1)} %get-tuple-element.43.wide_ref.wide_in_ref, f32[12,8,16,128]{3,2,1,0:T(8,128)S(1)} %get-tuple-element.54.error_in_ref, ...), custom_call_target="tpu_custom_call", output_to_operand_aliasing={{0}: (0, {}), {1}: (1, {})} | custom-call | tf_op jit(solution)/shard_map/span_rim/pallas_call | solution.py:756
  17.2 0.2 pitch_terms.1
  17.4 0.6 %collective-permute-start.9 = (f32[2,12,2,16,128]{4,3,2,1,0:T(8,128)S(1)}, f32[2,12,2,16,128]{4,3,2,1,0:T(8,128)S(1)}, u32[]{:S(2)}, u32[]{:S(2)}) collective-permute-start(f32[2,12,2,16,128]{4,3,2,1,0:T(8,128)S(1)} %get-tuple-element.75), channel_id=1, source_target_pairs={{0,16},{16,0},{1,17},{17,1},{2,18},{18,2},{3,19},{19,3},{4,20},{20... | collective-permute-start | bytes 1179656 | tf_op jit(solution)/shard_map/ppermute | solution.py:665
  18.0 0.9 %span_core.1 = (f32[12,12,16,128]{3,2,1,0:T(8,128)S(1)}, f32[12,8,16,128]{3,2,1,0:T(8,128)S(1)}, f32[16,128]{1,0:T(8,128)S(1)}, f32[12,8,2,128]{3,2,1,0:T(2,128)...) custom-call(f32[12,12,16,128]{3,2,1,0:T(8,128)S(1)} %get-tuple-eleme, ...), custom_call_target="tpu_custom_call", output_to_operand_aliasing={{0}: (0, {}), {1}: (1, {})} | custom-call | tf_op jit(solution)/shard_map/span_core/pallas_call | solution.py:766
  18.9 0.1 collective-permute-start.7
  19.0 1.6 %collective-permute-start.8 = (f32[12,8,2,128]{3,2,1,0:T(2,128)S(1)}, f32[12,8,2,128]{3,2,1,0:T(2,128)S(1)}, u32[]{:S(2)}, u32[]{:S(2)}) collective-permute-start(f32[12,8,2,128]{3,2,1,0:T(2,128)S(1)} %get-tuple-element.72), channel_id=1, source_target_pairs={{0,4},{1,5},{2,6},{3,7},{4,0},{5,1},{6,2},{7,3},{8,12},{9,13},{10,... | collective-permute-start | bytes 294920 | tf_op jit(solution)/shard_map/ppermute | solution.py:684
  20.6 1.0 %collective-permute-start.6 = (f32[3,16,128]{2,1,0:T(8,128)S(1)}, f32[3,16,128]{2,1,0:T(8,128)S(1)}, u32[]{:S(2)}, u32[]{:S(2)}) collective-permute-start(f32[3,16,128]{2,1,0:T(8,128)S(1)} %get-tuple-element.67), channel_id=1, source_target_pairs={{1,2},{0,3},{2,1},{3,0},{5,6},{4,7},{6,5},{7,4},{9,10},{8,11},{10,... | collective-permute-start | bytes 73736 | tf_op jit(solution)/shard_map/ppermute | solution.py:690
  21.6 1.8 %near.1 = (f32[12,8,16,128]{3,2,1,0:T(8,128)S(1)}, f32[12,8,16,128]{3,2,1,0:T(8,128)S(1)}, f32[12,8,16,128]{3,2,1,0:T(8,128)S(1)}, f32[12,8,16,128]{3,2,1,0:T(8,128)S(1)}) custom-call(f32[12,12,16,128]{3,2,1,0:T(8,128)S(1)} %get-tuple-element.65.wide_ref.wide_in_ref, bf16[2,6,6,8,16,128]{5,4,3,2,1,0:T(8,128)(2,1)S(1)} %get-tuple-element.61.neighbour_ref, ...), custom_call_target="tpu_custom_call" | custom-call | tf_op jit(solution)/shard_map/near/pallas_call | solution.py:747
  23.4 0.4 %collective-permute-done.6.refs_1_ = f32[3,16,128]{2,1,0:T(8,128)S(1)} collective-permute-done((f32[3,16,128]{2,1,0:T(8,128)S(1)}, f32[3,16,128]{2,1,0:T(8,128)S(1)}, u32[]{:S(2)}, u32[]{:S(2)}) %collective-permute-start.6) | collective-permute-done | bytes 24608 | tf_op jit(solution)/shard_map/ppermute | solution.py:690
  23.8 1.7 %axial.1.error_in_ref = f32[12,8,16,128]{3,2,1,0:T(8,128)S(1)} custom-call(f32[12,8,16,128]{3,2,1,0:T(8,128)S(1)} %get-tuple-element.66.error_in_ref, f32[3,16,128]{2,1,0:T(8,128)S(1)} %collective-permute-done.5.refs_0_, f32[3,16,128]{2,1,0:T(8,128)S(1)} %collective-permute-done.6.refs_1_, ...), custom_call_target="tpu_custom_call", output_to_operand_aliasing={{}: (0, {})} | custom-call | tf_op jit(solution)/shard_map/axial/pallas_call | solution.py:750
  25.6 1.4 %span.1 = (f32[12,12,16,128]{3,2,1,0:T(8,128)S(1)}, f32[12,8,16,128]{3,2,1,0:T(8,128)S(1)}, f32[16,128]{1,0:T(8,128)S(1)}, f32[12,8,16,128]{3,2,1,0:T(8,128)}) custom-call(f32[12,12,16,128]{3,2,1,0:T(8,128)S(1)} %get-tuple-element.65.wide_ref.wide_in_ref, f32[12,8,16,128]{3,2,1,0:T(8,128)S(1)} %axial.1.error_in_ref, ...), custom_call_target="tpu_custom_call", output_to_operand_aliasing={{0}: (0, {}), {1}: (1, {})} | custom-call | tf_op jit(solution)/shard_map/span/pallas_call | solution.py:775
  27.0 1.5 %collective-permute-done.9.halo_ref = f32[2,12,2,16,128]{4,3,2,1,0:T(8,128)S(1)} collective-permute-done((f32[2,12,2,16,128]{4,3,2,1,0:T(8,128)S(1)}, f32[2,12,2,16,128]{4,3,2,1,0:T(8,128)S(1)}, u32[]{:S(2)}, u32[]{:S(2)}) %collective-permute-start.9) | collective-permute-done | bytes 393248 | tf_op jit(solution)/shard_map/ppermute | solution.py:665
  28.5 0.3 last_pitch_terms.1
  28.8 8.8 %all_to_all.5.share_ref = f32[32,1,128]{2,1,0:T(1,128)S(1)} all-to-all(f32[32,1,128]{2,1,0:T(1,128)S(1)} %get-tuple-element.81), channel_id=1, replica_groups=mesh['pitch'=2,'span'=4,'axial'=4] {'pitch','span','axial'}, dimensions={0} | all-to-all | bytes 32768 | tf_op jit(solution)/shard_map/all_to_all | solution.py:791
  37.6 1.3 %close.1 = (f32[12,8,16,128]{3,2,1,0:T(8,128)}, f32[2]{0:T(128)}) custom-call(f32[12,8,16,128]{3,2,1,0:T(8,128)} %get-tuple-element.73.out_in_ref, f32[12,4,16,128]{3,2,1,0:T(8,128)S(1)} %get-tuple-element.80.rim_ref, f32[32,1,128]{2,1,0:T(1,128)S(1)} %all_to_all.5.share_ref), custom_call_target="tpu_custom_call", output_to_operand_aliasing={{0}: (0, {})} | custom-call | tf_op jit(solution)/shard_map/close/pallas_call | solution.py:793
  (9 shorter events, 0.0 us)
Async XLA Ops:
  1.7 15.5 %collective-permute-start.4 = (f32[2,12,2,16,128]{4,3,2,1,0:T(8,128)S(1)}, f32[2,12,2,16,128]{4,3,2,1,0:T(8,128)S(1)}, u32[]{:S(2)}, u32[]{:S(2)}) collective-permute-start(f32[2,12,2,16,128]{4,3,2,1,0:T(8,128)S(1)} %pitch_faces.1), channel_id=1, source_target_pairs={{0,16},{16,0},{1,17},{17,1},{2,18},{18,2},{3,19},{19,3},{4,20},{20... | collective-permute-start | bytes 1179656 | tf_op jit(solution)/shard_map/ppermute | solution.py:665
  6.6 9.9 %collective-permute-start.2 = (f32[12,8,2,128]{3,2,1,0:T(2,128)S(1)}, f32[12,8,2,128]{3,2,1,0:T(2,128)S(1)}, u32[]{:S(2)}, u32[]{:S(2)}) collective-permute-start(f32[12,8,2,128]{3,2,1,0:T(2,128)S(1)} %get-tuple-element.55), channel_id=1, source_target_pairs={{0,1},{1,0},{2,3},{3,2},{4,8},{5,9},{6,10},{7,11},{8,4},{9,5},{10,... | collective-permute-start | bytes 294920 | tf_op jit(solution)/shard_map/ppermute | solution.py:684
  6.7 9.8 %collective-permute-start.3 = (f32[12,8,2,128]{3,2,1,0:T(2,128)S(1)}, f32[12,8,2,128]{3,2,1,0:T(2,128)S(1)}, u32[]{:S(2)}, u32[]{:S(2)}) collective-permute-start(f32[12,8,2,128]{3,2,1,0:T(2,128)S(1)} %get-tuple-element.56), channel_id=1, source_target_pairs={{0,4},{1,5},{2,6},{3,7},{4,0},{5,1},{6,2},{7,3},{8,12},{9,13},{10,... | collective-permute-start | bytes 294920 | tf_op jit(solution)/shard_map/ppermute | solution.py:684
  9.8 4.9 %collective-permute-start = (f32[3,16,128]{2,1,0:T(8,128)S(1)}, f32[3,16,128]{2,1,0:T(8,128)S(1)}, u32[]{:S(2)}, u32[]{:S(2)}) collective-permute-start(f32[3,16,128]{2,1,0:T(8,128)S(1)} %get-tuple-element.49), channel_id=1, source_target_pairs={{0,1},{2,3},{1,0},{3,2},{4,5},{6,7},{5,4},{7,6},{8,9},{10,11},{9,8... | collective-permute-start | bytes 73736 | tf_op jit(solution)/shard_map/ppermute | solution.py:690
  9.8 4.9 %collective-permute-start.1 = (f32[3,16,128]{2,1,0:T(8,128)S(1)}, f32[3,16,128]{2,1,0:T(8,128)S(1)}, u32[]{:S(2)}, u32[]{:S(2)}) collective-permute-start(f32[3,16,128]{2,1,0:T(8,128)S(1)} %get-tuple-element.49), channel_id=1, source_target_pairs={{1,2},{0,3},{2,1},{3,0},{5,6},{4,7},{6,5},{7,4},{9,10},{8,11},{10,... | collective-permute-start | bytes 73736 | tf_op jit(solution)/shard_map/ppermute | solution.py:690
  17.4 11.1 %collective-permute-start.9 = (f32[2,12,2,16,128]{4,3,2,1,0:T(8,128)S(1)}, f32[2,12,2,16,128]{4,3,2,1,0:T(8,128)S(1)}, u32[]{:S(2)}, u32[]{:S(2)}) collective-permute-start(f32[2,12,2,16,128]{4,3,2,1,0:T(8,128)S(1)} %get-tuple-element.75), channel_id=1, source_target_pairs={{0,16},{16,0},{1,17},{17,1},{2,18},{18,2},{3,19},{19,3},{4,20},{20... | collective-permute-start | bytes 1179656 | tf_op jit(solution)/shard_map/ppermute | solution.py:665
  18.9 6.7 %collective-permute-start.7 = (f32[12,8,2,128]{3,2,1,0:T(2,128)S(1)}, f32[12,8,2,128]{3,2,1,0:T(2,128)S(1)}, u32[]{:S(2)}, u32[]{:S(2)}) collective-permute-start(f32[12,8,2,128]{3,2,1,0:T(2,128)S(1)} %get-tuple-element.71), channel_id=1, source_target_pairs={{0,1},{1,0},{2,3},{3,2},{4,8},{5,9},{6,10},{7,11},{8,4},{9,5},{10,... | collective-permute-start | bytes 294920 | tf_op jit(solution)/shard_map/ppermute | solution.py:684
  19.0 6.6 %collective-permute-start.8 = (f32[12,8,2,128]{3,2,1,0:T(2,128)S(1)}, f32[12,8,2,128]{3,2,1,0:T(2,128)S(1)}, u32[]{:S(2)}, u32[]{:S(2)}) collective-permute-start(f32[12,8,2,128]{3,2,1,0:T(2,128)S(1)} %get-tuple-element.72), channel_id=1, source_target_pairs={{0,4},{1,5},{2,6},{3,7},{4,0},{5,1},{6,2},{7,3},{8,12},{9,13},{10,... | collective-permute-start | bytes 294920 | tf_op jit(solution)/shard_map/ppermute | solution.py:684
  20.6 2.8 %collective-permute-start.5 = (f32[3,16,128]{2,1,0:T(8,128)S(1)}, f32[3,16,128]{2,1,0:T(8,128)S(1)}, u32[]{:S(2)}, u32[]{:S(2)}) collective-permute-start(f32[3,16,128]{2,1,0:T(8,128)S(1)} %get-tuple-element.67), channel_id=1, source_target_pairs={{0,1},{2,3},{1,0},{3,2},{4,5},{6,7},{5,4},{7,6},{8,9},{10,11},{9,8... | collective-permute-start | bytes 73736 | tf_op jit(solution)/shard_map/ppermute | solution.py:690
  20.6 3.3 %collective-permute-start.6 = (f32[3,16,128]{2,1,0:T(8,128)S(1)}, f32[3,16,128]{2,1,0:T(8,128)S(1)}, u32[]{:S(2)}, u32[]{:S(2)}) collective-permute-start(f32[3,16,128]{2,1,0:T(8,128)S(1)} %get-tuple-element.67), channel_id=1, source_target_pairs={{1,2},{0,3},{2,1},{3,0},{5,6},{4,7},{6,5},{7,4},{9,10},{8,11},{10,... | collective-permute-start | bytes 73736 | tf_op jit(solution)/shard_map/ppermute | solution.py:690

commit v7 on v6

--- a/solution.py
+++ b/solution.py
@@ -634,7 +634,10 @@
     first = jnp.sum(jnp.where(lane < lanes // 2, row, 0.0), axis=1, keepdims=True)
     second = jnp.sum(jnp.where(lane < lanes // 2, 0.0, row), axis=1, keepdims=True)
     norms = jnp.sqrt(jnp.where(lane == 0, first, second) / cell_count)
-    norm_ref[...] = norms[0, 0:ITERS]
+    for at in range(ITERS):
+        norm_buf[at] = norms[0, at]
+    copies.append(pltpu.make_async_copy(norm_buf, norm_ref, sems.at[2]))
+    copies[2].start()
     for copy in copies:
         copy.wait()
 
@@ -798,9 +801,9 @@
             jax.ShapeDtypeStruct((ITERS,), jnp.float32),
         ),
         [ANY, VMEM, VMEM],
-        [pltpu.VMEM((1, lanes), jnp.float32), dma((3,))],
+        [pltpu.SMEM((ITERS,), jnp.float32), dma((3,))],
         {0: 0},
-        (ANY, VMEM),
+        (ANY, ANY),
     )(out, rim, resident(shares))
     return (out.reshape(parts, nv, planes, span, lanes), norms)
 

time: 39.1 us -> 38.6 us (0.987)
  Pallas kernels: 15.5 us -> 15 us
    pallas_call x1, Pallas kernels: 1.29 us -> 0.78 us  [body(): call(functools.partial(close_kernel, cell_count), 'close', (jax.ShapeDtyp...]
where the time goes in v7:
time: 38.6 us; the launch traced here: 38.4 us
  Pallas kernels  15 us (39%)
  starting transfers between devices  11.1 us (29%)
  blocking collectives  8.84 us (23%)
  waiting for transfers between devices  1.97 us (5%)
  between operations  1.44 us (4%)
    all_to_all x1, blocking collectives, body(): shares = lax.all_to_all(share, ('pitch', 'span', 'axial'), 0, 0, tiled=True)  8.84 us
    ppermute x4, starting transfers between devices, span_swap(): return resident(lax.ppermute(values, ('span', 'axial'), pairs))  4.92 us
    ppermute x2, starting transfers between devices, exchange_pitch(): return lax.ppermute(faces, 'pitch', up)  3.6 us
    pallas_call x1, Pallas kernels, body(): call(near_loading_kernel, 'first_near', (kept(block),) * 4 + (pair, pair)...  2.64 us
    ppermute x4, starting transfers between devices, axial_swap(): lax.ppermute(values, 'axial', pairs + [(j, i) for i, j in pairs])  2.58 us
    pallas_call x1, Pallas kernels, body(): call(open_kernel, 'open', (kept(wide),) + face_shapes[1:] + tuple((kept(c...  1.9 us
    pallas_call x1, Pallas kernels, body(): call(near_kernel, 'near', (kept(block),) * 4, [VMEM] * 6)  1.83 us
    pallas_call x1, Pallas kernels, body(): call(first_axial_kernel, 'first_axial', (kept(block), pair, kept((4,) + t...  1.73 us
  transfers between devices with their start and end apart: 10, of which 2 were waited for; matrix products, arithmetic and copies ran while one was open for 0% of the time, Pallas kernels for 33%

profile of v7, /device:TPU:0, one launch (start us, length us, event | category | flops | bytes accessed | tf_op | source)
XLA Modules:
  0.0 38.4 jit_solution(1303939470194419143)
XLA Ops:
  0.6 1.0 %pitch_faces.1 = f32[2,12,2,16,128]{4,3,2,1,0:T(8,128)S(1)} custom-call(f32[12,8,16,128]{3,2,1,0:T(8,128)} %bitcast.3), custom_call_target="tpu_custom_call" | custom-call | tf_op jit(solution)/shard_map/pitch_faces/pallas_call | solution.py:706
  1.7 3.0 %collective-permute-start.4 = (f32[2,12,2,16,128]{4,3,2,1,0:T(8,128)S(1)}, f32[2,12,2,16,128]{4,3,2,1,0:T(8,128)S(1)}, u32[]{:S(2)}, u32[]{:S(2)}) collective-permute-start(f32[2,12,2,16,128]{4,3,2,1,0:T(8,128)S(1)} %pitch_faces.1), channel_id=1, source_target_pairs={{0,16},{16,0},{1,17},{17,1},{2,18},{18,2},{3,19},{19,3},{4,20},{20... | collective-permute-start | bytes 1179656 | tf_op jit(solution)/shard_map/ppermute | solution.py:668
  4.7 1.9 %open.1 = (f32[12,12,16,128]{3,2,1,0:T(8,128)S(1)}, f32[12,8,2,128]{3,2,1,0:T(2,128)S(1)}, f32[12,8,2,128]{3,2,1,0:T(2,128)S(1)}, f32[3,16,128]{2,1,0:T(8,128)S(...) custom-call(f32[12,8,16,128]{3,2,1,0:T(8,128)} %bitcast.4, ...), custom_call_target="tpu_custom_call" | custom-call | tf_op jit(solution)/shard_map/open/pallas_call | solution.py:707
  6.6 0.1 collective-permute-start.2
  6.7 3.1 %collective-permute-start.3 = (f32[12,8,2,128]{3,2,1,0:T(2,128)S(1)}, f32[12,8,2,128]{3,2,1,0:T(2,128)S(1)}, u32[]{:S(2)}, u32[]{:S(2)}) collective-permute-start(f32[12,8,2,128]{3,2,1,0:T(2,128)S(1)} %get-tuple-element.56), channel_id=1, source_target_pairs={{0,4},{1,5},{2,6},{3,7},{4,0},{5,1},{6,2},{7,3},{8,12},{9,13},{10,... | collective-permute-start | bytes 294920 | tf_op jit(solution)/shard_map/ppermute | solution.py:687
  9.8 0.0 collective-permute-start
  9.8 1.6 %collective-permute-start.1 = (f32[3,16,128]{2,1,0:T(8,128)S(1)}, f32[3,16,128]{2,1,0:T(8,128)S(1)}, u32[]{:S(2)}, u32[]{:S(2)}) collective-permute-start(f32[3,16,128]{2,1,0:T(8,128)S(1)} %get-tuple-element.49), channel_id=1, source_target_pairs={{1,2},{0,3},{2,1},{3,0},{5,6},{4,7},{6,5},{7,4},{9,10},{8,11},{10,... | collective-permute-start | bytes 73736 | tf_op jit(solution)/shard_map/ppermute | solution.py:693
  12.1 2.6 %first_near.1 = (f32[12,8,16,128]{3,2,1,0:T(8,128)S(1)}, f32[12,8,16,128]{3,2,1,0:T(8,128)S(1)}, f32[12,8,16,128]{3,2,1,0:T(8,128)S(1)}, f32[12,8,16,128]{3,2,1,...) custom-call(f32[12,12,16,128]{3,2,1,0:T(8,128)S(1)} %get-tuple-element.43.wide_ref., ...), custom_call_target="tpu_custom_call" | custom-call | tf_op jit(solution)/shard_map/first_near/pallas_call | solution.py:725
  14.8 1.7 %first_axial.1 = (f32[12,8,16,128]{3,2,1,0:T(8,128)S(1)}, bf16[2,6,6,8,16,128]{5,4,3,2,1,0:T(8,128)(2,1)S(1)}, f32[4,16,128]{2,1,0:T(8,128)S(1)}) custom-call(f32[12,8,16,128]{3,2,1,0:T(8,128)S(1)} %get-tuple-element.48.error_in_ref, f32[3,16,128]{2,1,0:T(8,128)S(1)} %collective-permute-done.even_ref, ...), custom_call_target="tpu_custom_call", output_to_operand_aliasing={{0}: (0, {})} | custom-call | tf_op jit(solution)/shard_map/first_axial/pallas_call | solution.py:732
  16.5 0.6 %span_rim.1 = (f32[12,12,16,128]{3,2,1,0:T(8,128)S(1)}, f32[12,8,16,128]{3,2,1,0:T(8,128)S(1)}, f32[16,128]{1,0:T(8,128)S(1)}) custom-call(f32[12,12,16,128]{3,2,1,0:T(8,128)S(1)} %get-tuple-element.43.wide_ref.wide_in_ref, f32[12,8,16,128]{3,2,1,0:T(8,128)S(1)} %get-tuple-element.54.error_in_ref, ...), custom_call_target="tpu_custom_call", output_to_operand_aliasing={{0}: (0, {}), {1}: (1, {})} | custom-call | tf_op jit(solution)/shard_map/span_rim/pallas_call | solution.py:759
  17.2 0.2 pitch_terms.1
  17.4 0.6 %collective-permute-start.9 = (f32[2,12,2,16,128]{4,3,2,1,0:T(8,128)S(1)}, f32[2,12,2,16,128]{4,3,2,1,0:T(8,128)S(1)}, u32[]{:S(2)}, u32[]{:S(2)}) collective-permute-start(f32[2,12,2,16,128]{4,3,2,1,0:T(8,128)S(1)} %get-tuple-element.75), channel_id=1, source_target_pairs={{0,16},{16,0},{1,17},{17,1},{2,18},{18,2},{3,19},{19,3},{4,20},{20... | collective-permute-start | bytes 1179656 | tf_op jit(solution)/shard_map/ppermute | solution.py:668
  18.0 0.9 %span_core.1 = (f32[12,12,16,128]{3,2,1,0:T(8,128)S(1)}, f32[12,8,16,128]{3,2,1,0:T(8,128)S(1)}, f32[16,128]{1,0:T(8,128)S(1)}, f32[12,8,2,128]{3,2,1,0:T(2,128)...) custom-call(f32[12,12,16,128]{3,2,1,0:T(8,128)S(1)} %get-tuple-eleme, ...), custom_call_target="tpu_custom_call", output_to_operand_aliasing={{0}: (0, {}), {1}: (1, {})} | custom-call | tf_op jit(solution)/shard_map/span_core/pallas_call | solution.py:769
  18.9 0.1 collective-permute-start.7
  19.0 1.6 %collective-permute-start.8 = (f32[12,8,2,128]{3,2,1,0:T(2,128)S(1)}, f32[12,8,2,128]{3,2,1,0:T(2,128)S(1)}, u32[]{:S(2)}, u32[]{:S(2)}) collective-permute-start(f32[12,8,2,128]{3,2,1,0:T(2,128)S(1)} %get-tuple-element.72), channel_id=1, source_target_pairs={{0,4},{1,5},{2,6},{3,7},{4,0},{5,1},{6,2},{7,3},{8,12},{9,13},{10,... | collective-permute-start | bytes 294920 | tf_op jit(solution)/shard_map/ppermute | solution.py:687
  20.6 1.0 %collective-permute-start.6 = (f32[3,16,128]{2,1,0:T(8,128)S(1)}, f32[3,16,128]{2,1,0:T(8,128)S(1)}, u32[]{:S(2)}, u32[]{:S(2)}) collective-permute-start(f32[3,16,128]{2,1,0:T(8,128)S(1)} %get-tuple-element.67), channel_id=1, source_target_pairs={{1,2},{0,3},{2,1},{3,0},{5,6},{4,7},{6,5},{7,4},{9,10},{8,11},{10,... | collective-permute-start | bytes 73736 | tf_op jit(solution)/shard_map/ppermute | solution.py:693
  21.6 1.8 %near.1 = (f32[12,8,16,128]{3,2,1,0:T(8,128)S(1)}, f32[12,8,16,128]{3,2,1,0:T(8,128)S(1)}, f32[12,8,16,128]{3,2,1,0:T(8,128)S(1)}, f32[12,8,16,128]{3,2,1,0:T(8,128)S(1)}) custom-call(f32[12,12,16,128]{3,2,1,0:T(8,128)S(1)} %get-tuple-element.65.wide_ref.wide_in_ref, bf16[2,6,6,8,16,128]{5,4,3,2,1,0:T(8,128)(2,1)S(1)} %get-tuple-element.61.neighbour_ref, ...), custom_call_target="tpu_custom_call" | custom-call | tf_op jit(solution)/shard_map/near/pallas_call | solution.py:750
  23.4 0.4 %collective-permute-done.6.refs_1_ = f32[3,16,128]{2,1,0:T(8,128)S(1)} collective-permute-done((f32[3,16,128]{2,1,0:T(8,128)S(1)}, f32[3,16,128]{2,1,0:T(8,128)S(1)}, u32[]{:S(2)}, u32[]{:S(2)}) %collective-permute-start.6) | collective-permute-done | bytes 24608 | tf_op jit(solution)/shard_map/ppermute | solution.py:693
  23.8 1.7 %axial.1.error_in_ref = f32[12,8,16,128]{3,2,1,0:T(8,128)S(1)} custom-call(f32[12,8,16,128]{3,2,1,0:T(8,128)S(1)} %get-tuple-element.66.error_in_ref, f32[3,16,128]{2,1,0:T(8,128)S(1)} %collective-permute-done.5.refs_0_, f32[3,16,128]{2,1,0:T(8,128)S(1)} %collective-permute-done.6.refs_1_, ...), custom_call_target="tpu_custom_call", output_to_operand_aliasing={{}: (0, {})} | custom-call | tf_op jit(solution)/shard_map/axial/pallas_call | solution.py:753
  25.6 1.4 %span.1 = (f32[12,12,16,128]{3,2,1,0:T(8,128)S(1)}, f32[12,8,16,128]{3,2,1,0:T(8,128)S(1)}, f32[16,128]{1,0:T(8,128)S(1)}, f32[12,8,16,128]{3,2,1,0:T(8,128)}) custom-call(f32[12,12,16,128]{3,2,1,0:T(8,128)S(1)} %get-tuple-element.65.wide_ref.wide_in_ref, f32[12,8,16,128]{3,2,1,0:T(8,128)S(1)} %axial.1.error_in_ref, ...), custom_call_target="tpu_custom_call", output_to_operand_aliasing={{0}: (0, {}), {1}: (1, {})} | custom-call | tf_op jit(solution)/shard_map/span/pallas_call | solution.py:778
  27.0 1.5 %collective-permute-done.9.halo_ref = f32[2,12,2,16,128]{4,3,2,1,0:T(8,128)S(1)} collective-permute-done((f32[2,12,2,16,128]{4,3,2,1,0:T(8,128)S(1)}, f32[2,12,2,16,128]{4,3,2,1,0:T(8,128)S(1)}, u32[]{:S(2)}, u32[]{:S(2)}) %collective-permute-start.9) | collective-permute-done | bytes 393248 | tf_op jit(solution)/shard_map/ppermute | solution.py:668
  28.5 0.3 last_pitch_terms.1
  28.8 8.8 %all_to_all.5.share_ref = f32[32,1,128]{2,1,0:T(1,128)S(1)} all-to-all(f32[32,1,128]{2,1,0:T(1,128)S(1)} %get-tuple-element.81), channel_id=1, replica_groups=mesh['pitch'=2,'span'=4,'axial'=4] {'pitch','span','axial'}, dimensions={0} | all-to-all | bytes 32768 | tf_op jit(solution)/shard_map/all_to_all | solution.py:794
  37.6 0.8 %close.1 = (f32[12,8,16,128]{3,2,1,0:T(8,128)}, f32[2]{0:T(128)}) custom-call(f32[12,8,16,128]{3,2,1,0:T(8,128)} %get-tuple-element.73.out_in_ref, f32[12,4,16,128]{3,2,1,0:T(8,128)S(1)} %get-tuple-element.80.rim_ref, f32[32,1,128]{2,1,0:T(1,128)S(1)} %all_to_all.5.share_ref), custom_call_target="tpu_custom_call", output_to_operand_aliasing={{0}: (0, {})} | custom-call | tf_op jit(solution)/shard_map/close/pallas_call | solution.py:796
  (9 shorter events, 0.0 us)
Async XLA Ops:
  1.7 15.5 %collective-permute-start.4 = (f32[2,12,2,16,128]{4,3,2,1,0:T(8,128)S(1)}, f32[2,12,2,16,128]{4,3,2,1,0:T(8,128)S(1)}, u32[]{:S(2)}, u32[]{:S(2)}) collective-permute-start(f32[2,12,2,16,128]{4,3,2,1,0:T(8,128)S(1)} %pitch_faces.1), channel_id=1, source_target_pairs={{0,16},{16,0},{1,17},{17,1},{2,18},{18,2},{3,19},{19,3},{4,20},{20... | collective-permute-start | bytes 1179656 | tf_op jit(solution)/shard_map/ppermute | solution.py:668
  6.6 9.9 %collective-permute-start.2 = (f32[12,8,2,128]{3,2,1,0:T(2,128)S(1)}, f32[12,8,2,128]{3,2,1,0:T(2,128)S(1)}, u32[]{:S(2)}, u32[]{:S(2)}) collective-permute-start(f32[12,8,2,128]{3,2,1,0:T(2,128)S(1)} %get-tuple-element.55), channel_id=1, source_target_pairs={{0,1},{1,0},{2,3},{3,2},{4,8},{5,9},{6,10},{7,11},{8,4},{9,5},{10,... | collective-permute-start | bytes 294920 | tf_op jit(solution)/shard_map/ppermute | solution.py:687
  6.7 9.8 %collective-permute-start.3 = (f32[12,8,2,128]{3,2,1,0:T(2,128)S(1)}, f32[12,8,2,128]{3,2,1,0:T(2,128)S(1)}, u32[]{:S(2)}, u32[]{:S(2)}) collective-permute-start(f32[12,8,2,128]{3,2,1,0:T(2,128)S(1)} %get-tuple-element.56), channel_id=1, source_target_pairs={{0,4},{1,5},{2,6},{3,7},{4,0},{5,1},{6,2},{7,3},{8,12},{9,13},{10,... | collective-permute-start | bytes 294920 | tf_op jit(solution)/shard_map/ppermute | solution.py:687
  9.8 4.9 %collective-permute-start = (f32[3,16,128]{2,1,0:T(8,128)S(1)}, f32[3,16,128]{2,1,0:T(8,128)S(1)}, u32[]{:S(2)}, u32[]{:S(2)}) collective-permute-start(f32[3,16,128]{2,1,0:T(8,128)S(1)} %get-tuple-element.49), channel_id=1, source_target_pairs={{0,1},{2,3},{1,0},{3,2},{4,5},{6,7},{5,4},{7,6},{8,9},{10,11},{9,8... | collective-permute-start | bytes 73736 | tf_op jit(solution)/shard_map/ppermute | solution.py:693
  9.8 4.9 %collective-permute-start.1 = (f32[3,16,128]{2,1,0:T(8,128)S(1)}, f32[3,16,128]{2,1,0:T(8,128)S(1)}, u32[]{:S(2)}, u32[]{:S(2)}) collective-permute-start(f32[3,16,128]{2,1,0:T(8,128)S(1)} %get-tuple-element.49), channel_id=1, source_target_pairs={{1,2},{0,3},{2,1},{3,0},{5,6},{4,7},{6,5},{7,4},{9,10},{8,11},{10,... | collective-permute-start | bytes 73736 | tf_op jit(solution)/shard_map/ppermute | solution.py:693
  17.4 11.1 %collective-permute-start.9 = (f32[2,12,2,16,128]{4,3,2,1,0:T(8,128)S(1)}, f32[2,12,2,16,128]{4,3,2,1,0:T(8,128)S(1)}, u32[]{:S(2)}, u32[]{:S(2)}) collective-permute-start(f32[2,12,2,16,128]{4,3,2,1,0:T(8,128)S(1)} %get-tuple-element.75), channel_id=1, source_target_pairs={{0,16},{16,0},{1,17},{17,1},{2,18},{18,2},{3,19},{19,3},{4,20},{20... | collective-permute-start | bytes 1179656 | tf_op jit(solution)/shard_map/ppermute | solution.py:668
  18.9 6.7 %collective-permute-start.7 = (f32[12,8,2,128]{3,2,1,0:T(2,128)S(1)}, f32[12,8,2,128]{3,2,1,0:T(2,128)S(1)}, u32[]{:S(2)}, u32[]{:S(2)}) collective-permute-start(f32[12,8,2,128]{3,2,1,0:T(2,128)S(1)} %get-tuple-element.71), channel_id=1, source_target_pairs={{0,1},{1,0},{2,3},{3,2},{4,8},{5,9},{6,10},{7,11},{8,4},{9,5},{10,... | collective-permute-start | bytes 294920 | tf_op jit(solution)/shard_map/ppermute | solution.py:687
  19.0 6.6 %collective-permute-start.8 = (f32[12,8,2,128]{3,2,1,0:T(2,128)S(1)}, f32[12,8,2,128]{3,2,1,0:T(2,128)S(1)}, u32[]{:S(2)}, u32[]{:S(2)}) collective-permute-start(f32[12,8,2,128]{3,2,1,0:T(2,128)S(1)} %get-tuple-element.72), channel_id=1, source_target_pairs={{0,4},{1,5},{2,6},{3,7},{4,0},{5,1},{6,2},{7,3},{8,12},{9,13},{10,... | collective-permute-start | bytes 294920 | tf_op jit(solution)/shard_map/ppermute | solution.py:687
  20.6 2.8 %collective-permute-start.5 = (f32[3,16,128]{2,1,0:T(8,128)S(1)}, f32[3,16,128]{2,1,0:T(8,128)S(1)}, u32[]{:S(2)}, u32[]{:S(2)}) collective-permute-start(f32[3,16,128]{2,1,0:T(8,128)S(1)} %get-tuple-element.67), channel_id=1, source_target_pairs={{0,1},{2,3},{1,0},{3,2},{4,5},{6,7},{5,4},{7,6},{8,9},{10,11},{9,8... | collective-permute-start | bytes 73736 | tf_op jit(solution)/shard_map/ppermute | solution.py:693
  20.6 3.3 %collective-permute-start.6 = (f32[3,16,128]{2,1,0:T(8,128)S(1)}, f32[3,16,128]{2,1,0:T(8,128)S(1)}, u32[]{:S(2)}, u32[]{:S(2)}) collective-permute-start(f32[3,16,128]{2,1,0:T(8,128)S(1)} %get-tuple-element.67), channel_id=1, source_target_pairs={{1,2},{0,3},{2,1},{3,0},{5,6},{4,7},{6,5},{7,4},{9,10},{8,11},{10,... | collective-permute-start | bytes 73736 | tf_op jit(solution)/shard_map/ppermute | solution.py:693

commit v8 on v7

--- a/solution.py
+++ b/solution.py
@@ -116,7 +116,7 @@
                 copy.wait()
 
 
-def faces_kernel(guess_hbm, faces_ref, sems):
+def faces_kernel(guess_hbm, after_ref, faces_ref, sems):
     planes = guess_hbm.shape[1]
     tail = pltpu.make_async_copy(
         guess_hbm.at[:, planes - WIDTH : planes], faces_ref.at[0], sems.at[0]
@@ -126,6 +126,12 @@
     head.start()
     tail.wait()
     head.wait()
+
+
+def staggered_open_kernel(turn, *refs):
+    @pl.when(lax.axis_index("axial") % 2 == turn)
+    def _():
+        open_kernel(*refs[:6], *refs[-10:])
 
 
 def open_kernel(
@@ -703,16 +709,28 @@
     neighbour_blocks = outside(neighbour_blocks)
     sources = (right_side.reshape(block), dissipation, omega_volume, pseudo_step, diag_block)
     guess = outside(guess.reshape(block))
-    (faces,) = call(faces_kernel, "pitch_faces", face_shapes[:1], [ANY], [dma((2,))])(guess)
-    state, even, odd, axial, right, dissipation, omega, step, diag = call(
-        open_kernel,
-        "open",
-        (kept(wide),)
-        + face_shapes[1:]
-        + tuple(kept(c.shape, c.dtype) for c in sources),
+    opening = (
+        (kept(wide),) + face_shapes[1:] + tuple(kept(c.shape, c.dtype) for c in sources)
+    )
+    given = (guess, *[outside(c) for c in sources])
+    opened = call(
+        functools.partial(staggered_open_kernel, 0),
+        "open_even",
+        opening,
         [ANY] * 6,
         [dma((6,))],
-    )(guess, *[outside(c) for c in sources])
+    )(*given)
+    (faces,) = call(faces_kernel, "pitch_faces", face_shapes[:1], [ANY, VMEM], [dma((2,))])(
+        guess, opened[3]
+    )
+    state, even, odd, axial, right, dissipation, omega, step, diag = call(
+        functools.partial(staggered_open_kernel, 1),
+        "open_odd",
+        opening,
+        [ANY] * 6 + [VMEM] * 9,
+        [dma((6,))],
+        {6 + at: at for at in range(9)},
+    )(*given, *opened)
 
     axial_buf = [pltpu.VMEM(face_shapes[3].shape, jnp.float32)]
     span_buf = [pltpu.VMEM((rows, span + 2 * PAD, lanes), jnp.float32)]

time: 38.6 us -> 38.7 us (level)
    pallas_call x2 -> x3, Pallas kernels: 2.94 us -> 3.02 us  [the longest x1 1.92 us: body(): call(functools.partial(staggered_open_kernel, 0), 'open_even', opening, [...]
  transfers between devices with their start and end apart: 10 -> 10, of which waited for: 2 -> 2; matrix products, arithmetic and copies ran while one was open for 0% -> 0% of each run, Pallas kernels for 33% -> 28%
where the time goes in v8:
time: 38.7 us; the launch traced here: 38.5 us
  Pallas kernels  15.1 us (39%)
  starting transfers between devices  11.1 us (29%)
  blocking collectives  8.84 us (23%)
  waiting for transfers between devices  1.98 us (5%)
  between operations  1.44 us (4%)
    all_to_all x1, blocking collectives, body(): shares = lax.all_to_all(share, ('pitch', 'span', 'axial'), 0, 0, tiled=True)  8.84 us
    ppermute x4, starting transfers between devices, span_swap(): return resident(lax.ppermute(values, ('span', 'axial'), pairs))  4.92 us
    ppermute x2, starting transfers between devices, exchange_pitch(): return lax.ppermute(faces, 'pitch', up)  3.6 us
    pallas_call x1, Pallas kernels, body(): call(near_loading_kernel, 'first_near', (kept(block),) * 4 + (pair, pair)...  2.64 us
    ppermute x4, starting transfers between devices, axial_swap(): lax.ppermute(values, 'axial', pairs + [(j, i) for i, j in pairs])  2.59 us
    pallas_call x1, Pallas kernels, body(): call(functools.partial(staggered_open_kernel, 0), 'open_even', opening, [...  1.92 us
    pallas_call x1, Pallas kernels, body(): call(near_kernel, 'near', (kept(block),) * 4, [VMEM] * 6)  1.83 us
    pallas_call x1, Pallas kernels, body(): call(first_axial_kernel, 'first_axial', (kept(block), pair, kept((4,) + t...  1.73 us
  transfers between devices with their start and end apart: 10, of which 2 were waited for; matrix products, arithmetic and copies ran while one was open for 0% of the time, Pallas kernels for 28%

profile of v8, /device:TPU:0, one launch (start us, length us, event | category | flops | bytes accessed | tf_op | source)
XLA Modules:
  0.0 38.5 jit_solution(5836591339586639141)
XLA Ops:
  0.6 1.9 %open_even.1 = (f32[12,12,16,128]{3,2,1,0:T(8,128)S(1)}, f32[12,8,2,128]{3,2,1,0:T(2,128)S(1)}, f32[12,8,2,128]{3,2,1,0:T(2,128)S(1)}, f32[3,16,128]{2,1,0:T(8,1...) custom-call(f32[12,8,16,128]{3,2,1,0:T(8,128)} %bitcast.3, ...), custom_call_target="tpu_custom_call" | custom-call | tf_op jit(solution)/shard_map/open_even/pallas_call | solution.py:716
  2.6 1.0 %pitch_faces.1 = f32[2,12,2,16,128]{4,3,2,1,0:T(8,128)S(1)} custom-call(f32[12,8,16,128]{3,2,1,0:T(8,128)} %bitcast.4, f32[3,16,128]{2,1,0:T(8,128)S(1)} %get-tuple-element.55.refs_9_.after_ref), custom_call_target="tpu_custom_call" | custom-call | tf_op jit(solution)/shard_map/pitch_faces/pallas_call | solution.py:723
  3.6 3.0 %collective-permute-start.4 = (f32[2,12,2,16,128]{4,3,2,1,0:T(8,128)S(1)}, f32[2,12,2,16,128]{4,3,2,1,0:T(8,128)S(1)}, u32[]{:S(2)}, u32[]{:S(2)}) collective-permute-start(f32[2,12,2,16,128]{4,3,2,1,0:T(8,128)S(1)} %pitch_faces.1), channel_id=1, source_target_pairs={{0,16},{16,0},{1,17},{17,1},{2,18},{18,2},{3,19},{19,3},{4,20},{20... | collective-permute-start | bytes 1179656 | tf_op jit(solution)/shard_map/ppermute | solution.py:674
  6.7 0.1 collective-permute-start.2
  6.8 3.1 %collective-permute-start.3 = (f32[12,8,2,128]{3,2,1,0:T(2,128)S(1)}, f32[12,8,2,128]{3,2,1,0:T(2,128)S(1)}, u32[]{:S(2)}, u32[]{:S(2)}) collective-permute-start(f32[12,8,2,128]{3,2,1,0:T(2,128)S(1)} %get-tuple-element.74), channel_id=1, source_target_pairs={{0,4},{1,5},{2,6},{3,7},{4,0},{5,1},{6,2},{7,3},{8,12},{9,13},{10,... | collective-permute-start | bytes 294920 | tf_op jit(solution)/shard_map/ppermute | solution.py:693
  9.9 0.1 collective-permute-start.1
  10.0 1.5 %collective-permute-start = (f32[3,16,128]{2,1,0:T(8,128)S(1)}, f32[3,16,128]{2,1,0:T(8,128)S(1)}, u32[]{:S(2)}, u32[]{:S(2)}) collective-permute-start(f32[3,16,128]{2,1,0:T(8,128)S(1)} %get-tuple-element.67), channel_id=1, source_target_pairs={{0,1},{2,3},{1,0},{3,2},{4,5},{6,7},{5,4},{7,6},{8,9},{10,11},{9,8... | collective-permute-start | bytes 73736 | tf_op jit(solution)/shard_map/ppermute | solution.py:699
  12.2 2.6 %first_near.1 = (f32[12,8,16,128]{3,2,1,0:T(8,128)S(1)}, f32[12,8,16,128]{3,2,1,0:T(8,128)S(1)}, f32[12,8,16,128]{3,2,1,0:T(8,128)S(1)}, f32[12,8,16,128]{3,2,1,...) custom-call(f32[12,12,16,128]{3,2,1,0:T(8,128)S(1)} %get-tuple-element.61.wide_ref., ...), custom_call_target="tpu_custom_call" | custom-call | tf_op jit(solution)/shard_map/first_near/pallas_call | solution.py:743
  14.8 1.7 %first_axial.1 = (f32[12,8,16,128]{3,2,1,0:T(8,128)S(1)}, bf16[2,6,6,8,16,128]{5,4,3,2,1,0:T(8,128)(2,1)S(1)}, f32[4,16,128]{2,1,0:T(8,128)S(1)}) custom-call(f32[12,8,16,128]{3,2,1,0:T(8,128)S(1)} %get-tuple-element.66.error_in_ref, f32[3,16,128]{2,1,0:T(8,128)S(1)} %collective-permute-done.even_ref, ...), custom_call_target="tpu_custom_call", output_to_operand_aliasing={{0}: (0, {})} | custom-call | tf_op jit(solution)/shard_map/first_axial/pallas_call | solution.py:750
  16.6 0.6 %span_rim.1 = (f32[12,12,16,128]{3,2,1,0:T(8,128)S(1)}, f32[12,8,16,128]{3,2,1,0:T(8,128)S(1)}, f32[16,128]{1,0:T(8,128)S(1)}) custom-call(f32[12,12,16,128]{3,2,1,0:T(8,128)S(1)} %get-tuple-element.61.wide_ref.wide_in_ref, f32[12,8,16,128]{3,2,1,0:T(8,128)S(1)} %get-tuple-element.72.error_in_ref, ...), custom_call_target="tpu_custom_call", output_to_operand_aliasing={{0}: (0, {}), {1}: (1, {})} | custom-call | tf_op jit(solution)/shard_map/span_rim/pallas_call | solution.py:777
  17.3 0.2 pitch_terms.1
  17.5 0.6 %collective-permute-start.9 = (f32[2,12,2,16,128]{4,3,2,1,0:T(8,128)S(1)}, f32[2,12,2,16,128]{4,3,2,1,0:T(8,128)S(1)}, u32[]{:S(2)}, u32[]{:S(2)}) collective-permute-start(f32[2,12,2,16,128]{4,3,2,1,0:T(8,128)S(1)} %get-tuple-element.93), channel_id=1, source_target_pairs={{0,16},{16,0},{1,17},{17,1},{2,18},{18,2},{3,19},{19,3},{4,20},{20... | collective-permute-start | bytes 1179656 | tf_op jit(solution)/shard_map/ppermute | solution.py:674
  18.1 0.9 %span_core.1 = (f32[12,12,16,128]{3,2,1,0:T(8,128)S(1)}, f32[12,8,16,128]{3,2,1,0:T(8,128)S(1)}, f32[16,128]{1,0:T(8,128)S(1)}, f32[12,8,2,128]{3,2,1,0:T(2,128)...) custom-call(f32[12,12,16,128]{3,2,1,0:T(8,128)S(1)} %get-tuple-eleme, ...), custom_call_target="tpu_custom_call", output_to_operand_aliasing={{0}: (0, {}), {1}: (1, {})} | custom-call | tf_op jit(solution)/shard_map/span_core/pallas_call | solution.py:787
  19.0 0.1 collective-permute-start.7
  19.0 1.6 %collective-permute-start.8 = (f32[12,8,2,128]{3,2,1,0:T(2,128)S(1)}, f32[12,8,2,128]{3,2,1,0:T(2,128)S(1)}, u32[]{:S(2)}, u32[]{:S(2)}) collective-permute-start(f32[12,8,2,128]{3,2,1,0:T(2,128)S(1)} %get-tuple-element.90), channel_id=1, source_target_pairs={{0,4},{1,5},{2,6},{3,7},{4,0},{5,1},{6,2},{7,3},{8,12},{9,13},{10,... | collective-permute-start | bytes 294920 | tf_op jit(solution)/shard_map/ppermute | solution.py:693
  20.7 1.0 %collective-permute-start.5 = (f32[3,16,128]{2,1,0:T(8,128)S(1)}, f32[3,16,128]{2,1,0:T(8,128)S(1)}, u32[]{:S(2)}, u32[]{:S(2)}) collective-permute-start(f32[3,16,128]{2,1,0:T(8,128)S(1)} %get-tuple-element.85), channel_id=1, source_target_pairs={{0,1},{2,3},{1,0},{3,2},{4,5},{6,7},{5,4},{7,6},{8,9},{10,11},{9,8... | collective-permute-start | bytes 73736 | tf_op jit(solution)/shard_map/ppermute | solution.py:699
  21.7 1.8 %near.1 = (f32[12,8,16,128]{3,2,1,0:T(8,128)S(1)}, f32[12,8,16,128]{3,2,1,0:T(8,128)S(1)}, f32[12,8,16,128]{3,2,1,0:T(8,128)S(1)}, f32[12,8,16,128]{3,2,1,0:T(8,128)S(1)}) custom-call(f32[12,12,16,128]{3,2,1,0:T(8,128)S(1)} %get-tuple-element.83.wide_ref.wide_in_ref, bf16[2,6,6,8,16,128]{5,4,3,2,1,0:T(8,128)(2,1)S(1)} %get-tuple-element.79.neighbour_ref, ...), custom_call_target="tpu_custom_call" | custom-call | tf_op jit(solution)/shard_map/near/pallas_call | solution.py:768
  23.5 0.4 %collective-permute-done.6.refs_1_ = f32[3,16,128]{2,1,0:T(8,128)S(1)} collective-permute-done((f32[3,16,128]{2,1,0:T(8,128)S(1)}, f32[3,16,128]{2,1,0:T(8,128)S(1)}, u32[]{:S(2)}, u32[]{:S(2)}) %collective-permute-start.6) | collective-permute-done | bytes 24608 | tf_op jit(solution)/shard_map/ppermute | solution.py:699
  23.9 1.7 %axial.1.error_in_ref = f32[12,8,16,128]{3,2,1,0:T(8,128)S(1)} custom-call(f32[12,8,16,128]{3,2,1,0:T(8,128)S(1)} %get-tuple-element.84.error_in_ref, f32[3,16,128]{2,1,0:T(8,128)S(1)} %collective-permute-done.5.refs_0_, f32[3,16,128]{2,1,0:T(8,128)S(1)} %collective-permute-done.6.refs_1_, ...), custom_call_target="tpu_custom_call", output_to_operand_aliasing={{}: (0, {})} | custom-call | tf_op jit(solution)/shard_map/axial/pallas_call | solution.py:771
  25.7 1.4 %span.1 = (f32[12,12,16,128]{3,2,1,0:T(8,128)S(1)}, f32[12,8,16,128]{3,2,1,0:T(8,128)S(1)}, f32[16,128]{1,0:T(8,128)S(1)}, f32[12,8,16,128]{3,2,1,0:T(8,128)}) custom-call(f32[12,12,16,128]{3,2,1,0:T(8,128)S(1)} %get-tuple-element.83.wide_ref.wide_in_ref, f32[12,8,16,128]{3,2,1,0:T(8,128)S(1)} %axial.1.error_in_ref, ...), custom_call_target="tpu_custom_call", output_to_operand_aliasing={{0}: (0, {}), {1}: (1, {})} | custom-call | tf_op jit(solution)/shard_map/span/pallas_call | solution.py:796
  27.1 1.5 %collective-permute-done.9.halo_ref = f32[2,12,2,16,128]{4,3,2,1,0:T(8,128)S(1)} collective-permute-done((f32[2,12,2,16,128]{4,3,2,1,0:T(8,128)S(1)}, f32[2,12,2,16,128]{4,3,2,1,0:T(8,128)S(1)}, u32[]{:S(2)}, u32[]{:S(2)}) %collective-permute-start.9) | collective-permute-done | bytes 393248 | tf_op jit(solution)/shard_map/ppermute | solution.py:674
  28.6 0.3 last_pitch_terms.1
  28.9 8.8 %all_to_all.5.share_ref = f32[32,1,128]{2,1,0:T(1,128)S(1)} all-to-all(f32[32,1,128]{2,1,0:T(1,128)S(1)} %get-tuple-element.99), channel_id=1, replica_groups=mesh['pitch'=2,'span'=4,'axial'=4] {'pitch','span','axial'}, dimensions={0} | all-to-all | bytes 32768 | tf_op jit(solution)/shard_map/all_to_all | solution.py:812
  37.7 0.8 %close.1 = (f32[12,8,16,128]{3,2,1,0:T(8,128)}, f32[2]{0:T(128)}) custom-call(f32[12,8,16,128]{3,2,1,0:T(8,128)} %get-tuple-element.91.out_in_ref, f32[12,4,16,128]{3,2,1,0:T(8,128)S(1)} %get-tuple-element.98.rim_ref, f32[32,1,128]{2,1,0:T(1,128)S(1)} %all_to_all.5.share_ref), custom_call_target="tpu_custom_call", output_to_operand_aliasing={{0}: (0, {})} | custom-call | tf_op jit(solution)/shard_map/close/pallas_call | solution.py:814
  (10 shorter events, 0.1 us)
Async XLA Ops:
  3.6 13.6 %collective-permute-start.4 = (f32[2,12,2,16,128]{4,3,2,1,0:T(8,128)S(1)}, f32[2,12,2,16,128]{4,3,2,1,0:T(8,128)S(1)}, u32[]{:S(2)}, u32[]{:S(2)}) collective-permute-start(f32[2,12,2,16,128]{4,3,2,1,0:T(8,128)S(1)} %pitch_faces.1), channel_id=1, source_target_pairs={{0,16},{16,0},{1,17},{17,1},{2,18},{18,2},{3,19},{19,3},{4,20},{20... | collective-permute-start | bytes 1179656 | tf_op jit(solution)/shard_map/ppermute | solution.py:674
  6.7 9.9 %collective-permute-start.2 = (f32[12,8,2,128]{3,2,1,0:T(2,128)S(1)}, f32[12,8,2,128]{3,2,1,0:T(2,128)S(1)}, u32[]{:S(2)}, u32[]{:S(2)}) collective-permute-start(f32[12,8,2,128]{3,2,1,0:T(2,128)S(1)} %get-tuple-element.73), channel_id=1, source_target_pairs={{0,1},{1,0},{2,3},{3,2},{4,8},{5,9},{6,10},{7,11},{8,4},{9,5},{10,... | collective-permute-start | bytes 294920 | tf_op jit(solution)/shard_map/ppermute | solution.py:693
  6.8 9.8 %collective-permute-start.3 = (f32[12,8,2,128]{3,2,1,0:T(2,128)S(1)}, f32[12,8,2,128]{3,2,1,0:T(2,128)S(1)}, u32[]{:S(2)}, u32[]{:S(2)}) collective-permute-start(f32[12,8,2,128]{3,2,1,0:T(2,128)S(1)} %get-tuple-element.74), channel_id=1, source_target_pairs={{0,4},{1,5},{2,6},{3,7},{4,0},{5,1},{6,2},{7,3},{8,12},{9,13},{10,... | collective-permute-start | bytes 294920 | tf_op jit(solution)/shard_map/ppermute | solution.py:693
  9.9 4.9 %collective-permute-start.1 = (f32[3,16,128]{2,1,0:T(8,128)S(1)}, f32[3,16,128]{2,1,0:T(8,128)S(1)}, u32[]{:S(2)}, u32[]{:S(2)}) collective-permute-start(f32[3,16,128]{2,1,0:T(8,128)S(1)} %get-tuple-element.67), channel_id=1, source_target_pairs={{1,2},{0,3},{2,1},{3,0},{5,6},{4,7},{6,5},{7,4},{9,10},{8,11},{10,... | collective-permute-start | bytes 73736 | tf_op jit(solution)/shard_map/ppermute | solution.py:699
  10.0 4.8 %collective-permute-start = (f32[3,16,128]{2,1,0:T(8,128)S(1)}, f32[3,16,128]{2,1,0:T(8,128)S(1)}, u32[]{:S(2)}, u32[]{:S(2)}) collective-permute-start(f32[3,16,128]{2,1,0:T(8,128)S(1)} %get-tuple-element.67), channel_id=1, source_target_pairs={{0,1},{2,3},{1,0},{3,2},{4,5},{6,7},{5,4},{7,6},{8,9},{10,11},{9,8... | collective-permute-start | bytes 73736 | tf_op jit(solution)/shard_map/ppermute | solution.py:699
  17.5 11.1 %collective-permute-start.9 = (f32[2,12,2,16,128]{4,3,2,1,0:T(8,128)S(1)}, f32[2,12,2,16,128]{4,3,2,1,0:T(8,128)S(1)}, u32[]{:S(2)}, u32[]{:S(2)}) collective-permute-start(f32[2,12,2,16,128]{4,3,2,1,0:T(8,128)S(1)} %get-tuple-element.93), channel_id=1, source_target_pairs={{0,16},{16,0},{1,17},{17,1},{2,18},{18,2},{3,19},{19,3},{4,20},{20... | collective-permute-start | bytes 1179656 | tf_op jit(solution)/shard_map/ppermute | solution.py:674
  19.0 6.7 %collective-permute-start.7 = (f32[12,8,2,128]{3,2,1,0:T(2,128)S(1)}, f32[12,8,2,128]{3,2,1,0:T(2,128)S(1)}, u32[]{:S(2)}, u32[]{:S(2)}) collective-permute-start(f32[12,8,2,128]{3,2,1,0:T(2,128)S(1)} %get-tuple-element.89), channel_id=1, source_target_pairs={{0,1},{1,0},{2,3},{3,2},{4,8},{5,9},{6,10},{7,11},{8,4},{9,5},{10,... | collective-permute-start | bytes 294920 | tf_op jit(solution)/shard_map/ppermute | solution.py:693
  19.0 6.6 %collective-permute-start.8 = (f32[12,8,2,128]{3,2,1,0:T(2,128)S(1)}, f32[12,8,2,128]{3,2,1,0:T(2,128)S(1)}, u32[]{:S(2)}, u32[]{:S(2)}) collective-permute-start(f32[12,8,2,128]{3,2,1,0:T(2,128)S(1)} %get-tuple-element.90), channel_id=1, source_target_pairs={{0,4},{1,5},{2,6},{3,7},{4,0},{5,1},{6,2},{7,3},{8,12},{9,13},{10,... | collective-permute-start | bytes 294920 | tf_op jit(solution)/shard_map/ppermute | solution.py:693
  20.7 3.3 %collective-permute-start.6 = (f32[3,16,128]{2,1,0:T(8,128)S(1)}, f32[3,16,128]{2,1,0:T(8,128)S(1)}, u32[]{:S(2)}, u32[]{:S(2)}) collective-permute-start(f32[3,16,128]{2,1,0:T(8,128)S(1)} %get-tuple-element.85), channel_id=1, source_target_pairs={{1,2},{0,3},{2,1},{3,0},{5,6},{4,7},{6,5},{7,4},{9,10},{8,11},{10,... | collective-permute-start | bytes 73736 | tf_op jit(solution)/shard_map/ppermute | solution.py:699
  20.7 3.3 %collective-permute-start.5 = (f32[3,16,128]{2,1,0:T(8,128)S(1)}, f32[3,16,128]{2,1,0:T(8,128)S(1)}, u32[]{:S(2)}, u32[]{:S(2)}) collective-permute-start(f32[3,16,128]{2,1,0:T(8,128)S(1)} %get-tuple-element.85), channel_id=1, source_target_pairs={{0,1},{2,3},{1,0},{3,2},{4,5},{6,7},{5,4},{7,6},{8,9},{10,11},{9,8... | collective-permute-start | bytes 73736 | tf_op jit(solution)/shard_map/ppermute | solution.py:699

commit v9 on v8

--- a/solution.py
+++ b/solution.py
@@ -10,7 +10,7 @@
 ITERS = 2
 WIDTH = 2
 PAD = 8
-GROUPS = 4
+GROUPS = 2
 VMEM = pl.BlockSpec(memory_space=pltpu.VMEM)
 SMEM = pl.BlockSpec(memory_space=pltpu.SMEM)
 ANY = pl.BlockSpec(memory_space=pl.ANY)
@@ -131,7 +131,7 @@
 def staggered_open_kernel(turn, *refs):
     @pl.when(lax.axis_index("axial") % 2 == turn)
     def _():
-        open_kernel(*refs[:6], *refs[-10:])
+        open_kernel(*refs[:7], *refs[-11:])
 
 
 def open_kernel(
@@ -141,6 +141,7 @@
     omega_hbm,
     step_hbm,
     diag_hbm,
+    neighbour_hbm,
     wide_ref,
     even_ref,
     odd_ref,
@@ -150,17 +151,20 @@
     omega_ref,
     step_ref,
     diag_ref,
+    neighbour_ref,
     sems,
 ):
     rows, wide, span, lanes = wide_ref.shape
     planes = wide - 2 * WIDTH
+    half = planes // 2
     pairs = (
         (guess_hbm, wide_ref.at[:, WIDTH : WIDTH + planes]),
         (dissipation_hbm, dissipation_ref),
         (omega_hbm, omega_ref),
         (step_hbm, step_ref),
         (right_hbm, right_ref),
-        (diag_hbm, diag_ref),
+        (diag_hbm.at[:, :, 0:half], diag_ref.at[:, :, 0:half]),
+        (neighbour_hbm.at[0:2, :, :, 0:half], neighbour_ref.at[:, :, :, 0:half]),
     )
     copies = [pltpu.make_async_copy(*pair, sems.at[at]) for at, pair in enumerate(pairs)]
     for copy in copies:
@@ -176,56 +180,55 @@
 
 def near_loading_kernel(
     wide_ref,
+    neighbour_in_ref,
+    diag_in_ref,
     neighbour_hbm,
-    diag_ref,
+    diag_hbm,
     right_ref,
     dissipation_ref,
     omega_ref,
+    neighbour_ref,
+    diag_ref,
     error_ref,
     lower_ref,
     upper_ref,
     spaced_ref,
-    neighbour_ref,
     axial_ref,
     near_sems,
     axial_sem,
 ):
     planes = error_ref.shape[1]
-    groups = near_sems.shape[1]
-    loads = Loads([(neighbour_hbm.at[0:2], neighbour_ref, 3)], near_sems, 0, planes // groups)
+    half = planes // 2
+    loads = Loads(
+        [(diag_hbm, diag_ref, 2), (neighbour_hbm.at[0:2], neighbour_ref, 3)],
+        near_sems,
+        half,
+        (planes - half) // near_sems.shape[1],
+    )
     later = pltpu.make_async_copy(neighbour_hbm.at[4:6], axial_ref, axial_sem)
     loads.start()
     later.start()
-    shifts = (lower_ref, upper_ref)
-
-    def own(p, carry):
-        total = own_terms(wide_ref, right_ref, dissipation_ref, omega_ref, p)
-        add_blocks(total, [(diag_ref, (), WIDTH)], wide_ref, p, shifts[:2], None)
-        for k, value in enumerate(total):
-            error_ref[k, p] = value
-        return carry
-
-    def pitch(p, carry):
-        loads.ready(p)
-        total = [error_ref[k, p] for k in range(error_ref.shape[0])]
-        add_blocks(
-            total,
-            [(neighbour_ref, (0,), WIDTH - 1), (neighbour_ref, (1,), WIDTH + 1)],
-            wide_ref,
-            p,
-            None,
-            spaced_ref,
-        )
-        for k, value in enumerate(total):
-            error_ref[k, p] = value
-        return carry
-
-    lax.fori_loop(0, planes, own, 0)
-    lax.fori_loop(0, planes, pitch, 0)
+    near_sweep(
+        wide_ref,
+        neighbour_ref,
+        diag_ref,
+        right_ref,
+        dissipation_ref,
+        omega_ref,
+        error_ref,
+        lower_ref,
+        upper_ref,
+        spaced_ref,
+        loads,
+    )
     later.wait()
 
 
-def near_kernel(
+def near_kernel(*refs):
+    near_sweep(*refs, None)
+
+
+def near_sweep(
     wide_ref,
     neighbour_ref,
     diag_ref,
@@ -236,8 +239,11 @@
     lower_ref,
     upper_ref,
     spaced_ref,
+    loads,
 ):
     def plane(p, carry):
+        if loads is not None:
+            loads.ready(p)
         total = own_terms(wide_ref, right_ref, dissipation_ref, omega_ref, p)
         add_blocks(
             total,
@@ -664,7 +670,7 @@
         kept((rows, planes, WIDTH, lanes)),
         kept((lane_groups(rows, planes, lanes), span, lanes)),
     )
-    groups = GROUPS if planes % GROUPS == 0 else 1
+    groups = GROUPS if (planes - planes // 2) % GROUPS == 0 else 1
     dma = pltpu.SemaphoreType.DMA
 
     def exchange_pitch(faces):
@@ -709,44 +715,57 @@
     neighbour_blocks = outside(neighbour_blocks)
     sources = (right_side.reshape(block), dissipation, omega_volume, pseudo_step, diag_block)
     guess = outside(guess.reshape(block))
+    pair = kept((2,) + neighbour_blocks.shape[1:], neighbour_blocks.dtype)
     opening = (
-        (kept(wide),) + face_shapes[1:] + tuple(kept(c.shape, c.dtype) for c in sources)
-    )
-    given = (guess, *[outside(c) for c in sources])
+        (kept(wide),)
+        + face_shapes[1:]
+        + tuple(kept(c.shape, c.dtype) for c in sources)
+        + (pair,)
+    )
+    given = (guess, *[outside(c) for c in sources], neighbour_blocks)
     opened = call(
         functools.partial(staggered_open_kernel, 0),
         "open_even",
         opening,
-        [ANY] * 6,
-        [dma((6,))],
+        [ANY] * 7,
+        [dma((7,))],
     )(*given)
     (faces,) = call(faces_kernel, "pitch_faces", face_shapes[:1], [ANY, VMEM], [dma((2,))])(
         guess, opened[3]
     )
-    state, even, odd, axial, right, dissipation, omega, step, diag = call(
+    state, even, odd, axial, right, dissipation, omega, step, diag, near_blocks = call(
         functools.partial(staggered_open_kernel, 1),
         "open_odd",
         opening,
-        [ANY] * 6 + [VMEM] * 9,
-        [dma((6,))],
-        {6 + at: at for at in range(9)},
+        [ANY] * 7 + [VMEM] * 10,
+        [dma((7,))],
+        {7 + at: at for at in range(10)},
     )(*given, *opened)
 
     axial_buf = [pltpu.VMEM(face_shapes[3].shape, jnp.float32)]
     span_buf = [pltpu.VMEM((rows, span + 2 * PAD, lanes), jnp.float32)]
-    pair = kept((2,) + neighbour_blocks.shape[1:], neighbour_blocks.dtype)
     sweep = (kept(wide), kept(block), kept(tile))
     for iteration in range(ITERS):
         halo = resident(exchange_pitch(faces))
         span_even, span_odd, axial_even, axial_odd = exchange_rest(even, odd, axial)
         if iteration == 0:
-            error, *shifts, near_blocks, axial_blocks = call(
+            near_blocks, diag, error, *shifts, axial_blocks = call(
                 near_loading_kernel,
                 "first_near",
-                (kept(block),) * 4 + (pair, pair),
-                [VMEM, ANY] + [VMEM] * 4,
-                [dma((1, groups)), dma],
-            )(state, neighbour_blocks, diag, right, dissipation, omega)
+                (pair, kept(diag.shape, diag.dtype)) + (kept(block),) * 4 + (pair,),
+                [VMEM] * 3 + [ANY] * 2 + [VMEM] * 3,
+                [dma((2, groups)), dma],
+                {1: 0, 2: 1},
+            )(
+                state,
+                near_blocks,
+                diag,
+                neighbour_blocks,
+                outside(diag_block),
+                right,
+                dissipation,
+                omega,
+            )
             error, span_blocks, turn = call(
                 first_axial_kernel,
                 "first_axial",

time: 38.7 us -> 38.8 us (level)
  transfers between devices with their start and end apart: 10 -> 10, of which waited for: 2 -> 2; matrix products, arithmetic and copies ran while one was open for 0% -> 0% of each run, Pallas kernels for 28% -> 27%
where the time goes in v9:
time: 38.8 us; the launch traced here: 38.6 us
  Pallas kernels  15 us (39%)
  starting transfers between devices  11.3 us (29%)
  blocking collectives  9.08 us (23%)
  waiting for transfers between devices  1.81 us (5%)
  between operations  1.45 us (4%)
    all_to_all x1, blocking collectives, body(): shares = lax.all_to_all(share, ('pitch', 'span', 'axial'), 0, 0, tiled=True)  9.08 us
    ppermute x4, starting transfers between devices, span_swap(): return resident(lax.ppermute(values, ('span', 'axial'), pairs))  4.92 us
    ppermute x2, starting transfers between devices, exchange_pitch(): return lax.ppermute(faces, 'pitch', up)  3.6 us
    ppermute x4, starting transfers between devices, axial_swap(): lax.ppermute(values, 'axial', pairs + [(j, i) for i, j in pairs])  2.75 us
    pallas_call x1, Pallas kernels, body(): call(near_loading_kernel, 'first_near', (pair, kept(diag.shape, diag.dtyp...  2.28 us
    pallas_call x1, Pallas kernels, body(): call(functools.partial(staggered_open_kernel, 0), 'open_even', opening, [...  2.12 us
    pallas_call x1, Pallas kernels, body(): call(near_kernel, 'near', (kept(block),) * 4, [VMEM] * 6)  1.83 us
    pallas_call x1, Pallas kernels, body(): call(first_axial_kernel, 'first_axial', (kept(block), pair, kept((4,) + t...  1.73 us
  transfers between devices with their start and end apart: 10, of which 2 were waited for; matrix products, arithmetic and copies ran while one was open for 0% of the time, Pallas kernels for 27%

profile of v9, /device:TPU:0, one launch (start us, length us, event | category | flops | bytes accessed | tf_op | source)
XLA Modules:
  0.0 38.6 jit_solution(6031078529105412838)
XLA Ops:
  0.6 2.1 %open_even.1 = (f32[12,12,16,128]{3,2,1,0:T(8,128)S(1)}, f32[12,8,2,128]{3,2,1,0:T(2,128)S(1)}, f32[12,8,2,128]{3,2,1,0:T(2,128)S(1)}, f32[3,16,128]{2,1,0:T(8,1...) custom-call(f32[12,8,16,128]{3,2,1,0:T(8,128)} %bitcast.3, ...), custom_call_target="tpu_custom_call" | custom-call | tf_op jit(solution)/shard_map/open_even/pallas_call | solution.py:726
  2.8 1.0 %pitch_faces.1 = f32[2,12,2,16,128]{4,3,2,1,0:T(8,128)S(1)} custom-call(f32[12,8,16,128]{3,2,1,0:T(8,128)} %bitcast.4, f32[3,16,128]{2,1,0:T(8,128)S(1)} %get-tuple-element.58.refs_10_.after_ref), custom_call_target="tpu_custom_call" | custom-call | tf_op jit(solution)/shard_map/pitch_faces/pallas_call | solution.py:733
  3.8 3.0 %collective-permute-start.4 = (f32[2,12,2,16,128]{4,3,2,1,0:T(8,128)S(1)}, f32[2,12,2,16,128]{4,3,2,1,0:T(8,128)S(1)}, u32[]{:S(2)}, u32[]{:S(2)}) collective-permute-start(f32[2,12,2,16,128]{4,3,2,1,0:T(8,128)S(1)} %pitch_faces.1), channel_id=1, source_target_pairs={{0,16},{16,0},{1,17},{17,1},{2,18},{18,2},{3,19},{19,3},{4,20},{20... | collective-permute-start | bytes 1179656 | tf_op jit(solution)/shard_map/ppermute | solution.py:680
  6.8 0.1 open_odd.1
  6.9 0.1 collective-permute-start.2
  7.0 3.1 %collective-permute-start.3 = (f32[12,8,2,128]{3,2,1,0:T(2,128)S(1)}, f32[12,8,2,128]{3,2,1,0:T(2,128)S(1)}, u32[]{:S(2)}, u32[]{:S(2)}) collective-permute-start(f32[12,8,2,128]{3,2,1,0:T(2,128)S(1)} %get-tuple-element.79), channel_id=1, source_target_pairs={{0,4},{1,5},{2,6},{3,7},{4,0},{5,1},{6,2},{7,3},{8,12},{9,13},{10,... | collective-permute-start | bytes 294920 | tf_op jit(solution)/shard_map/ppermute | solution.py:699
  10.1 1.6 %collective-permute-start.1 = (f32[3,16,128]{2,1,0:T(8,128)S(1)}, f32[3,16,128]{2,1,0:T(8,128)S(1)}, u32[]{:S(2)}, u32[]{:S(2)}) collective-permute-start(f32[3,16,128]{2,1,0:T(8,128)S(1)} %get-tuple-element.72), channel_id=1, source_target_pairs={{1,2},{0,3},{2,1},{3,0},{5,6},{4,7},{6,5},{7,4},{9,10},{8,11},{10,... | collective-permute-start | bytes 73736 | tf_op jit(solution)/shard_map/ppermute | solution.py:705
  12.4 2.3 %first_near.1 = (bf16[2,6,6,8,16,128]{5,4,3,2,1,0:T(8,128)(2,1)S(1)}, bf16[6,6,8,16,128]{4,3,2,1,0:T(8,128)(2,1)S(1)}, f32[12,8,16,128]{3,2,1,0:T(8,128)S(1)}, f...) custom-call(f32[12,12,16,128]{3,2,1,0:T(8,128)S(1)} %get-tuple-eleme, ...), custom_call_target="tpu_custom_call", output_to_operand_aliasing={{0}: (1, {}), {1}: (2, {})} | custom-call | tf_op jit(solution)/shard_map/first_near/pallas_call | solution.py:752
  14.7 1.7 %first_axial.1 = (f32[12,8,16,128]{3,2,1,0:T(8,128)S(1)}, bf16[2,6,6,8,16,128]{5,4,3,2,1,0:T(8,128)(2,1)S(1)}, f32[4,16,128]{2,1,0:T(8,128)S(1)}) custom-call(f32[12,8,16,128]{3,2,1,0:T(8,128)S(1)} %get-tuple-element.71.error_in_ref, f32[3,16,128]{2,1,0:T(8,128)S(1)} %collective-permute-done.even_ref, ...), custom_call_target="tpu_custom_call", output_to_operand_aliasing={{0}: (0, {})} | custom-call | tf_op jit(solution)/shard_map/first_axial/pallas_call | solution.py:769
  16.5 0.6 %span_rim.1 = (f32[12,12,16,128]{3,2,1,0:T(8,128)S(1)}, f32[12,8,16,128]{3,2,1,0:T(8,128)S(1)}, f32[16,128]{1,0:T(8,128)S(1)}) custom-call(f32[12,12,16,128]{3,2,1,0:T(8,128)S(1)} %get-tuple-element.65.wide_ref.wide_in_ref, f32[12,8,16,128]{3,2,1,0:T(8,128)S(1)} %get-tuple-element.77.error_in_ref, ...), custom_call_target="tpu_custom_call", output_to_operand_aliasing={{0}: (0, {}), {1}: (1, {})} | custom-call | tf_op jit(solution)/shard_map/span_rim/pallas_call | solution.py:796
  17.1 0.2 pitch_terms.1
  17.3 0.6 %collective-permute-start.9 = (f32[2,12,2,16,128]{4,3,2,1,0:T(8,128)S(1)}, f32[2,12,2,16,128]{4,3,2,1,0:T(8,128)S(1)}, u32[]{:S(2)}, u32[]{:S(2)}) collective-permute-start(f32[2,12,2,16,128]{4,3,2,1,0:T(8,128)S(1)} %get-tuple-element.99), channel_id=1, source_target_pairs={{0,16},{16,0},{1,17},{17,1},{2,18},{18,2},{3,19},{19,3},{4,20},{20... | collective-permute-start | bytes 1179656 | tf_op jit(solution)/shard_map/ppermute | solution.py:680
  17.9 0.9 %span_core.1 = (f32[12,12,16,128]{3,2,1,0:T(8,128)S(1)}, f32[12,8,16,128]{3,2,1,0:T(8,128)S(1)}, f32[16,128]{1,0:T(8,128)S(1)}, f32[12,8,2,128]{3,2,1,0:T(2,128)...) custom-call(f32[12,12,16,128]{3,2,1,0:T(8,128)S(1)} %get-tuple-eleme, ...), custom_call_target="tpu_custom_call", output_to_operand_aliasing={{0}: (0, {}), {1}: (1, {})} | custom-call | tf_op jit(solution)/shard_map/span_core/pallas_call | solution.py:806
  18.8 0.1 collective-permute-start.7
  18.9 1.6 %collective-permute-start.8 = (f32[12,8,2,128]{3,2,1,0:T(2,128)S(1)}, f32[12,8,2,128]{3,2,1,0:T(2,128)S(1)}, u32[]{:S(2)}, u32[]{:S(2)}) collective-permute-start(f32[12,8,2,128]{3,2,1,0:T(2,128)S(1)} %get-tuple-element.96), channel_id=1, source_target_pairs={{0,4},{1,5},{2,6},{3,7},{4,0},{5,1},{6,2},{7,3},{8,12},{9,13},{10,... | collective-permute-start | bytes 294920 | tf_op jit(solution)/shard_map/ppermute | solution.py:699
  20.5 1.1 %collective-permute-start.6 = (f32[3,16,128]{2,1,0:T(8,128)S(1)}, f32[3,16,128]{2,1,0:T(8,128)S(1)}, u32[]{:S(2)}, u32[]{:S(2)}) collective-permute-start(f32[3,16,128]{2,1,0:T(8,128)S(1)} %get-tuple-element.91), channel_id=1, source_target_pairs={{1,2},{0,3},{2,1},{3,0},{5,6},{4,7},{6,5},{7,4},{9,10},{8,11},{10,... | collective-permute-start | bytes 73736 | tf_op jit(solution)/shard_map/ppermute | solution.py:705
  21.7 1.8 %near.1 = (f32[12,8,16,128]{3,2,1,0:T(8,128)S(1)}, f32[12,8,16,128]{3,2,1,0:T(8,128)S(1)}, f32[12,8,16,128]{3,2,1,0:T(8,128)S(1)}, f32[12,8,16,128]{3,2,1,0:T(8,128)S(1)}) custom-call(f32[12,12,16,128]{3,2,1,0:T(8,128)S(1)} %get-tuple-element.88.refs_0_.wide_in_ref, bf16[2,6,6,8,16,128]{5,4,3,2,1,0:T(8,128)(2,1)S(1)} %get-tuple-element.84.neighbour_ref.refs_1_, ...), custom_call_target="tpu_custom_call" | custom-call | tf_op jit(solution)/shard_map/near/pallas_call | solution.py:787
  23.5 0.3 collective-permute-done.6.refs_1_
  23.8 1.7 %axial.1.error_in_ref = f32[12,8,16,128]{3,2,1,0:T(8,128)S(1)} custom-call(f32[12,8,16,128]{3,2,1,0:T(8,128)S(1)} %get-tuple-element.90.error_in_ref, f32[3,16,128]{2,1,0:T(8,128)S(1)} %collective-permute-done.5.refs_0_, f32[3,16,128]{2,1,0:T(8,128)S(1)} %collective-permute-done.6.refs_1_, ...), custom_call_target="tpu_custom_call", output_to_operand_aliasing={{}: (0, {})} | custom-call | tf_op jit(solution)/shard_map/axial/pallas_call | solution.py:790
  25.5 1.4 %span.1 = (f32[12,12,16,128]{3,2,1,0:T(8,128)S(1)}, f32[12,8,16,128]{3,2,1,0:T(8,128)S(1)}, f32[16,128]{1,0:T(8,128)S(1)}, f32[12,8,16,128]{3,2,1,0:T(8,128)}) custom-call(f32[12,12,16,128]{3,2,1,0:T(8,128)S(1)} %get-tuple-element.88.refs_0_.wide_in_ref, f32[12,8,16,128]{3,2,1,0:T(8,128)S(1)} %axial.1.error_in_ref, ...), custom_call_target="tpu_custom_call", output_to_operand_aliasing={{0}: (0, {}), {1}: (1, {})} | custom-call | tf_op jit(solution)/shard_map/span/pallas_call | solution.py:815
  26.9 1.5 %collective-permute-done.9.halo_ref = f32[2,12,2,16,128]{4,3,2,1,0:T(8,128)S(1)} collective-permute-done((f32[2,12,2,16,128]{4,3,2,1,0:T(8,128)S(1)}, f32[2,12,2,16,128]{4,3,2,1,0:T(8,128)S(1)}, u32[]{:S(2)}, u32[]{:S(2)}) %collective-permute-start.9) | collective-permute-done | bytes 393248 | tf_op jit(solution)/shard_map/ppermute | solution.py:680
  28.4 0.3 last_pitch_terms.1
  28.7 9.1 %all_to_all.5.share_ref = f32[32,1,128]{2,1,0:T(1,128)S(1)} all-to-all(f32[32,1,128]{2,1,0:T(1,128)S(1)} %get-tuple-element.105), channel_id=1, replica_groups=mesh['pitch'=2,'span'=4,'axial'=4] {'pitch','span','axial'}, dimensions={0} | all-to-all | bytes 32768 | tf_op jit(solution)/shard_map/all_to_all | solution.py:831
  37.8 0.8 %close.1 = (f32[12,8,16,128]{3,2,1,0:T(8,128)}, f32[2]{0:T(128)}) custom-call(f32[12,8,16,128]{3,2,1,0:T(8,128)} %get-tuple-element.97.out_in_ref, f32[12,4,16,128]{3,2,1,0:T(8,128)S(1)} %get-tuple-element.104.rim_ref, f32[32,1,128]{2,1,0:T(1,128)S(1)} %all_to_all.5.share_ref), custom_call_target="tpu_custom_call", output_to_operand_aliasing={{0}: (0, {})} | custom-call | tf_op jit(solution)/shard_map/close/pallas_call | solution.py:833
  (10 shorter events, 0.0 us)
Async XLA Ops:
  3.8 13.3 %collective-permute-start.4 = (f32[2,12,2,16,128]{4,3,2,1,0:T(8,128)S(1)}, f32[2,12,2,16,128]{4,3,2,1,0:T(8,128)S(1)}, u32[]{:S(2)}, u32[]{:S(2)}) collective-permute-start(f32[2,12,2,16,128]{4,3,2,1,0:T(8,128)S(1)} %pitch_faces.1), channel_id=1, source_target_pairs={{0,16},{16,0},{1,17},{17,1},{2,18},{18,2},{3,19},{19,3},{4,20},{20... | collective-permute-start | bytes 1179656 | tf_op jit(solution)/shard_map/ppermute | solution.py:680
  6.9 9.5 %collective-permute-start.2 = (f32[12,8,2,128]{3,2,1,0:T(2,128)S(1)}, f32[12,8,2,128]{3,2,1,0:T(2,128)S(1)}, u32[]{:S(2)}, u32[]{:S(2)}) collective-permute-start(f32[12,8,2,128]{3,2,1,0:T(2,128)S(1)} %get-tuple-element.78), channel_id=1, source_target_pairs={{0,1},{1,0},{2,3},{3,2},{4,8},{5,9},{6,10},{7,11},{8,4},{9,5},{10,... | collective-permute-start | bytes 294920 | tf_op jit(solution)/shard_map/ppermute | solution.py:699
  7.0 9.5 %collective-permute-start.3 = (f32[12,8,2,128]{3,2,1,0:T(2,128)S(1)}, f32[12,8,2,128]{3,2,1,0:T(2,128)S(1)}, u32[]{:S(2)}, u32[]{:S(2)}) collective-permute-start(f32[12,8,2,128]{3,2,1,0:T(2,128)S(1)} %get-tuple-element.79), channel_id=1, source_target_pairs={{0,4},{1,5},{2,6},{3,7},{4,0},{5,1},{6,2},{7,3},{8,12},{9,13},{10,... | collective-permute-start | bytes 294920 | tf_op jit(solution)/shard_map/ppermute | solution.py:699
  10.1 4.6 %collective-permute-start = (f32[3,16,128]{2,1,0:T(8,128)S(1)}, f32[3,16,128]{2,1,0:T(8,128)S(1)}, u32[]{:S(2)}, u32[]{:S(2)}) collective-permute-start(f32[3,16,128]{2,1,0:T(8,128)S(1)} %get-tuple-element.72), channel_id=1, source_target_pairs={{0,1},{2,3},{1,0},{3,2},{4,5},{6,7},{5,4},{7,6},{8,9},{10,11},{9,8... | collective-permute-start | bytes 73736 | tf_op jit(solution)/shard_map/ppermute | solution.py:705
  10.1 4.6 %collective-permute-start.1 = (f32[3,16,128]{2,1,0:T(8,128)S(1)}, f32[3,16,128]{2,1,0:T(8,128)S(1)}, u32[]{:S(2)}, u32[]{:S(2)}) collective-permute-start(f32[3,16,128]{2,1,0:T(8,128)S(1)} %get-tuple-element.72), channel_id=1, source_target_pairs={{1,2},{0,3},{2,1},{3,0},{5,6},{4,7},{6,5},{7,4},{9,10},{8,11},{10,... | collective-permute-start | bytes 73736 | tf_op jit(solution)/shard_map/ppermute | solution.py:705
  17.3 11.1 %collective-permute-start.9 = (f32[2,12,2,16,128]{4,3,2,1,0:T(8,128)S(1)}, f32[2,12,2,16,128]{4,3,2,1,0:T(8,128)S(1)}, u32[]{:S(2)}, u32[]{:S(2)}) collective-permute-start(f32[2,12,2,16,128]{4,3,2,1,0:T(8,128)S(1)} %get-tuple-element.99), channel_id=1, source_target_pairs={{0,16},{16,0},{1,17},{17,1},{2,18},{18,2},{3,19},{19,3},{4,20},{20... | collective-permute-start | bytes 1179656 | tf_op jit(solution)/shard_map/ppermute | solution.py:680
  18.8 6.7 %collective-permute-start.7 = (f32[12,8,2,128]{3,2,1,0:T(2,128)S(1)}, f32[12,8,2,128]{3,2,1,0:T(2,128)S(1)}, u32[]{:S(2)}, u32[]{:S(2)}) collective-permute-start(f32[12,8,2,128]{3,2,1,0:T(2,128)S(1)} %get-tuple-element.95), channel_id=1, source_target_pairs={{0,1},{1,0},{2,3},{3,2},{4,8},{5,9},{6,10},{7,11},{8,4},{9,5},{10,... | collective-permute-start | bytes 294920 | tf_op jit(solution)/shard_map/ppermute | solution.py:699
  18.9 6.6 %collective-permute-start.8 = (f32[12,8,2,128]{3,2,1,0:T(2,128)S(1)}, f32[12,8,2,128]{3,2,1,0:T(2,128)S(1)}, u32[]{:S(2)}, u32[]{:S(2)}) collective-permute-start(f32[12,8,2,128]{3,2,1,0:T(2,128)S(1)} %get-tuple-element.96), channel_id=1, source_target_pairs={{0,4},{1,5},{2,6},{3,7},{4,0},{5,1},{6,2},{7,3},{8,12},{9,13},{10,... | collective-permute-start | bytes 294920 | tf_op jit(solution)/shard_map/ppermute | solution.py:699
  20.5 3.0 %collective-permute-start.5 = (f32[3,16,128]{2,1,0:T(8,128)S(1)}, f32[3,16,128]{2,1,0:T(8,128)S(1)}, u32[]{:S(2)}, u32[]{:S(2)}) collective-permute-start(f32[3,16,128]{2,1,0:T(8,128)S(1)} %get-tuple-element.91), channel_id=1, source_target_pairs={{0,1},{2,3},{1,0},{3,2},{4,5},{6,7},{5,4},{7,6},{8,9},{10,11},{9,8... | collective-permute-start | bytes 73736 | tf_op jit(solution)/shard_map/ppermute | solution.py:705
  20.5 3.3 %collective-permute-start.6 = (f32[3,16,128]{2,1,0:T(8,128)S(1)}, f32[3,16,128]{2,1,0:T(8,128)S(1)}, u32[]{:S(2)}, u32[]{:S(2)}) collective-permute-start(f32[3,16,128]{2,1,0:T(8,128)S(1)} %get-tuple-element.91), channel_id=1, source_target_pairs={{1,2},{0,3},{2,1},{3,0},{5,6},{4,7},{6,5},{7,4},{9,10},{8,11},{10,... | collective-permute-start | bytes 73736 | tf_op jit(solution)/shard_map/ppermute | solution.py:705
